TPU v7x, 512 devices: a whole 4x4x16 slice. The times are simulated.
512 devices in a mesh: dp: 32 (over y, x, core), fsdp: 16 (over z).
Axes of the slice: x: 4, y: 4, z: 16, core: 2. Of those that a mesh axis runs over, the one named last changes fastest.
Arguments:
- activations: bfloat16 [24576, 8192], P('dp', 'fsdp'), may hold values from -6 to 6
- cotangent: bfloat16 [24576, 14336], P('dp', 'fsdp'), may hold values from -0.059814453 to 0.059814453
- basis: bfloat16 [8192, 1024], P('fsdp'), may hold values from -0.0625 to 0.0625
- first_moment: float32 [1024, 14336], P('dp', 'fsdp'), may hold values from -6 to 6
- second_moment: float32 [1024, 14336], P('dp', 'fsdp'), may hold values from 0.5 to 4
Outputs:
- moment_next: float32 [1024, 14336], P('dp', 'fsdp')
- square_next: float32 [1024, 14336], P('dp', 'fsdp')
- expanded: bfloat16 [8192, 14336], P('dp', 'fsdp')
All inputs are finite; a program needn't handle non-finite values.
Results may differ from a plain program's by a relative error of at most 0.0035.
The roundings to bfloat16 on the way count: a program that leaves them out, or rounds other values in their place, can miss the bound.
Values may be sent and summed in bfloat16 or wider, within the bound.
No kernel may reach another device: no remote copies, remote signals or barrier semaphores. Data moves between devices by JAX's collectives and lax.ppermute only.
A program may use at most 64 MiB of HBM per device.

v0:
```python
import jax
import jax.numpy as jnp
from jax import lax
from jax.sharding import PartitionSpec as P

decay_first = 0.9
decay_second = 0.999
epsilon = 1e-08


def broadcast(value, axis, root):
    mine = lax.axis_index(axis) == root
    return lax.psum(jnp.where(mine, value, jnp.zeros_like(value)), axis)


def body(activations, cotangent, basis, first_moment, second_moment):
    replicas = lax.axis_size("dp")
    shards = lax.axis_size("fsdp")
    partial_proj = jnp.dot(activations, basis, preferred_element_type=jnp.float32)
    summed = lax.psum(partial_proj, "fsdp")
    blocks = [summed.astype(jnp.bfloat16)]
    cot_blocks = [cotangent]
    own_rows = basis.shape[1] // replicas
    total = jnp.zeros((own_rows * lax.axis_size("dp"), cotangent.shape[1]), jnp.float32)
    for proj_block, cot_block in zip(blocks, cot_blocks):
        total = lax.dot_general(
            proj_block, cot_block, (((0,), (0,)), ((), ())), preferred_element_type=jnp.float32
        )
    gradient = lax.psum_scatter(total, "dp", scatter_dimension=0, tiled=True)
    moment_next = decay_first * first_moment + (1.0 - decay_first) * gradient
    square_next = decay_second * second_moment + (1.0 - decay_second) * gradient * gradient
    direction = (moment_next / (jnp.sqrt(square_next) + epsilon)).astype(jnp.bfloat16)
    groups_per = replicas // shards
    block_rows = basis.shape[0] // groups_per
    replica_index = lax.axis_index("dp")
    offset_rows = replica_index % groups_per * block_rows
    mine = lax.dynamic_slice_in_dim(basis, offset_rows, block_rows, 0)
    basis_block = broadcast(mine, "fsdp", replica_index // groups_per)
    expanded = jnp.dot(
        basis_block,
        lax.all_gather(direction, "dp", axis=0, tiled=True),
        preferred_element_type=jnp.float32,
    ).astype(jnp.bfloat16)
    return (moment_next, square_next, expanded)


def solution(mesh):
    in_specs = (P("dp", "fsdp"), P("dp", "fsdp"), P("fsdp", None), P("dp", "fsdp"), P("dp", "fsdp"))
    out_specs = (P("dp", "fsdp"), P("dp", "fsdp"), P("dp", "fsdp"))
    return jax.shard_map(body, mesh=mesh, in_specs=in_specs, out_specs=out_specs, check_vma=False)
```

profile of v0, /device:TPU:1, one launch (start us, length us, event | category | flops | bytes accessed | tf_op | source)
XLA Modules:
  0.0 278.0 jit_solution(12227861917685791047)
XLA Ops:
  8.0 0.0 copy-start
  8.0 0.0 reduce-scatter.2.cloned.1.call-start
  8.1 4.2 %fusion.4 = f32[768,1024]{1,0:T(8,128)} fusion(bf16[768,512]{1,0:T(8,128)(2,1)} %param.5, bf16[512,1024]{1,0:T(8,128)(2,1)} %param.7), kind=kOutput, calls=%fused_computation.8 | convolution fusion | flops 805306368 | bytes 4980736 | tf_op jit(solution)/shard_map/dot_general | solution.py:19
  12.3 79.5 %all-reduce.4 = bf16[768,1024]{1,0:T(8,128)(2,1)S(1)} all-reduce(f32[768,1024]{1,0:T(8,128)} %fusion.4), channel_id=1, replica_groups=mesh['dp'=32,'fsdp'=16] {'fsdp'}, use_global_device_ids=true, to_apply=%region_0.0 | all-reduce | flops 786432 | bytes 4718592 | tf_op jit(solution)/shard_map/psum | solution.py:20
  91.8 0.0 copy-done
  91.8 3.6 %fusion.5 = f32[1024,896]{1,0:T(8,128)} fusion(bf16[768,1024]{1,0:T(8,128)(2,1)S(1)} %all-reduce.4, bf16[768,896]{1,0:T(8,128)(2,1)S(1)} %copy-done), kind=kOutput, calls=%fused_computation.9 | convolution fusion | flops 1409286144 | bytes 6619136 | tf_op jit(solution)/shard_map/dot_general | solution.py:26
  95.4 0.0 copy-start.1
  95.4 0.0 copy-start.2
  95.4 0.0 copy-start.3
  95.4 0.0 reduce-scatter.2.cloned.1.call-update
  95.5 0.0 all-reduce.3.cloned.1.call-start
  95.5 1.1 copy-done.1
  96.7 0.9 dynamic-slice_select_fusion
  97.6 0.0 all-reduce.3.cloned.1.call-update
  97.6 0.0 all-gather.2.cloned.1.call-start
  97.7 105.9 %reduce-scatter.2.cloned.1.call-done = f32[32,896]{1,0:T(8,128)} async-done(((f32[1024,896]{1,0:T(8,128)}), f32[32,896]{1,0:T(8,128)}) %reduce-scatter.2.cloned.1.call-update) | async-done | bytes 114704 | tf_op jit(solution)/shard_map/reduce_scatter | solution.py:29
  203.6 0.0 copy-done.2
  203.6 0.0 copy-done.3
  203.6 1.6 divide_convert_fusion
  205.2 0.0 all-gather.2.cloned.1.call-update
  205.2 25.8 %all-reduce.3.cloned.1.call-done = bf16[256,1024]{1,0:T(8,128)(2,1)} async-done(((bf16[256,1024]{1,0:T(8,128)(2,1)}), bf16[256,1024]{1,0:T(8,128)(2,1)}) %all-reduce.3.cloned.1.call-update) | async-done | bytes 524304 | tf_op jit(solution)/shard_map/psum | solution.py:13
  231.0 36.5 %all-gather.2.cloned.1.call-done = bf16[1024,896]{1,0:T(8,128)(2,1)} async-done(((bf16[32,896]{1,0:T(8,128)(2,1)}), bf16[1024,896]{1,0:T(8,128)(2,1)}) %all-gather.2.cloned.1.call-update) | async-done | bytes 1835024 | tf_op jit(solution)/shard_map/all_gather | solution.py:41
  267.5 3.2 %convolution_convert_fusion = bf16[256,896]{1,0:T(8,128)(2,1)} fusion(bf16[256,1024]{1,0:T(8,128)(2,1)} %all-reduce.3.cloned.1.call-done, bf16[1024,896]{1,0:T(8,128)(2,1)} %all-gather.2.cloned.1.call-done), kind=kOutput, calls=%fused_computation.2 | convolution fusion | flops 469991424 | bytes 2818048 | tf_op jit(solution)/shard_map/dot_general | solution.py:39
Async XLA Ops:
  8.0 83.8 %copy-start = (bf16[768,896]{1,0:T(8,128)(2,1)S(1)}, bf16[768,896]{1,0:T(8,128)(2,1)}, u32[]{:S(2)}) copy-start(bf16[768,896]{1,0:T(8,128)(2,1)} %param.6) | copy-start | bytes 4128772
  8.0 195.6 %reduce-scatter.2.cloned.1.call-start = ((), (), s32[]{:S(2)}) async-start(), calls=%async_computation.1 | async-start | bytes 3784704 | tf_op jit(solution)/shard_map/reduce_scatter | solution.py:29
  95.4 1.2 copy-start.1
  95.4 108.1 %copy-start.2 = (f32[32,896]{1,0:T(8,128)S(1)}, f32[32,896]{1,0:T(8,128)}, u32[]{:S(2)}) copy-start(f32[32,896]{1,0:T(8,128)} %param.9) | copy-start | bytes 344068
  95.4 108.1 %copy-start.3 = (f32[32,896]{1,0:T(8,128)S(1)}, f32[32,896]{1,0:T(8,128)}, u32[]{:S(2)}) copy-start(f32[32,896]{1,0:T(8,128)} %param.8) | copy-start | bytes 344068
  95.5 135.5 %all-reduce.3.cloned.1.call-start = ((), (), s32[]{:S(2)}) async-start(), calls=%async_computation.2 | async-start | bytes 1048576 | tf_op jit(solution)/shard_map/psum | solution.py:13
  97.6 169.9 %all-gather.2.cloned.1.call-start = ((), (), s32[]{:S(2)}) async-start(), calls=%async_computation.3 | async-start | bytes 1892352 | tf_op jit(solution)/shard_map/all_gather | solution.py:41
Sparse Core Ops, SparseCore 0:
  95.6 107.9 reduce-scatter.1
  207.3 60.1 all-gather.1
Sparse Core Ops, SparseCore 1:
  98.4 132.6 all-reduce.2
where the time goes:
time: 278 us
  waiting for transfers between devices  168 us (60%)
  blocking collectives  79.5 us (29%)
  between operations  15.5 us (6%)
  matrix products  11 us (4%)
    reduce_scatter x1, waiting for transfers between devices, body(): gradient = lax.psum_scatter(total, 'dp', scatter_dimension=0, tiled=True)  106 us
    psum x1, blocking collectives, body(): summed = lax.psum(partial_proj, 'fsdp')  79.5 us
    all_gather x1, waiting for transfers between devices, body(): lax.all_gather(direction, 'dp', axis=0, tiled=True)  36.5 us
    psum x1, waiting for transfers between devices, broadcast(): return lax.psum(jnp.where(mine, value, jnp.zeros_like(value)), axis)  25.8 us
  transfers between devices with their start and end apart: 3, of which 3 were waited for; matrix products, arithmetic and copies ran while one was open for 1% of the time, Pallas kernels for 0%

commit v1 on v0

v1 whole, which is shorter than its diff:
```python
import numpy as np
import jax
import jax.numpy as jnp
from jax import lax
from jax.experimental import pallas as pl
from jax.experimental.pallas import tpu as pltpu
from jax.sharding import Mesh, PartitionSpec as P

decay_first = 0.9
decay_second = 0.999
epsilon = 1e-08

SWAP = [(0, 1), (1, 0)]
VMEM_LIMIT = 40 * 1024 * 1024
LAST = (((1,), (1,)), ((), ()))
IN_VMEM = pl.BlockSpec(memory_space=pltpu.VMEM)
IN_HBM = pl.BlockSpec(memory_space=pl.ANY)
IN_SMEM = pl.BlockSpec(memory_space=pltpu.SMEM)


def params():
    return pltpu.CompilerParams(vmem_limit_bytes=VMEM_LIMIT)


def cost(flops, moved):
    return pl.CostEstimate(flops=flops, bytes_accessed=moved, transcendentals=0)


def project_own(own_rows, core_ref, basis_ref, act_ref, out_ref, picked_ref):
    rank = basis_ref.shape[1]
    at = lax.broadcasted_iota(jnp.int32, (rank // 2, rank), 0)
    wanted = at // own_rows * (2 * own_rows) + core_ref[0] * own_rows + at % own_rows
    pick = (lax.broadcasted_iota(jnp.int32, (rank // 2, rank), 1) == wanted).astype(jnp.bfloat16)
    picked = lax.dot_general(pick, basis_ref[...], LAST, preferred_element_type=jnp.float32).astype(jnp.bfloat16)
    picked_ref[...] = picked
    out_ref[...] = lax.dot_general(picked, act_ref[...], LAST, preferred_element_type=jnp.float32)[None]


def project_other(picked_ref, act_ref, _, out_ref):
    out_ref[...] = lax.dot_general(picked_ref[...], act_ref[...], LAST, preferred_element_type=jnp.float32)[None]


def grad_terms(proj_ref, own_ref, other_ref, _, out_ref):
    total = jnp.dot(proj_ref[0], own_ref[...], preferred_element_type=jnp.float32)
    total += jnp.dot(proj_ref[1], other_ref[...], preferred_element_type=jnp.float32)
    out_ref[...] = total.astype(jnp.bfloat16)


def adam(terms_ref, first_ref, second_ref, moment_ref, square_ref, copies_ref):
    gradient = terms_ref[0].astype(jnp.float32)
    for i in range(1, terms_ref.shape[0]):
        gradient += terms_ref[i].astype(jnp.float32)
    moment_next = decay_first * first_ref[...] + (1.0 - decay_first) * gradient
    square_next = decay_second * second_ref[...] + (1.0 - decay_second) * gradient * gradient
    moment_ref[...] = moment_next
    square_ref[...] = square_next
    direction = (moment_next / (jnp.sqrt(square_next) + epsilon)).astype(jnp.bfloat16)
    for i in range(copies_ref.shape[0]):
        copies_ref[i] = direction


def expand(core_ref, shard_ref, mine_ref, other_ref, out_ref, all_ref):
    block_rows = out_ref.shape[0]
    core = core_ref[0]
    all_ref[:, pl.ds(core, 1)] = mine_ref[...][:, None]
    all_ref[:, pl.ds(1 - core, 1)] = other_ref[...][:, None]
    rows = pl.ds(pl.multiple_of(core * block_rows, block_rows), block_rows)
    direction = all_ref[...].reshape(shard_ref.shape[1], out_ref.shape[1])
    out_ref[...] = jnp.dot(shard_ref[rows, :], direction, preferred_element_type=jnp.float32).astype(jnp.bfloat16)


def body(activations, cotangent, basis, first_moment, second_moment):
    chips = lax.axis_size("chip")
    shards = lax.axis_size("fsdp")
    features, rank = basis.shape
    tokens = activations.shape[0]
    own_rows, columns = first_moment.shape
    chip, core, shard = lax.axis_index("chip"), lax.axis_index("core"), lax.axis_index("fsdp")
    core_at = core.astype(jnp.int32).reshape(1)
    f32, bf16 = jnp.float32, jnp.bfloat16

    piece_rows = features // shards
    piece = lax.dynamic_slice_in_dim(basis, (chip + shards - shard) % shards * piece_rows, piece_rows, 0)
    hand_on = [
        ((p * 2 + c) * shards + k, (k * 2 + c) * shards + (p - k) % shards)
        for p in range(chips) for c in range(2) for k in range(shards)
    ]
    piece = lax.ppermute(piece, ("chip", "core", "fsdp"), hand_on)
    chip_basis = lax.all_gather(piece, "fsdp", axis=0, tiled=True)

    other_act = lax.ppermute(activations, "core", SWAP)
    other_cot = lax.ppermute(cotangent, "core", SWAP)
    flops = rank * tokens * features
    partial, picked = pl.pallas_call(
        lambda *refs: project_own(own_rows, *refs),
        grid=(1,),
        out_shape=(
            jax.ShapeDtypeStruct((2, rank // 2, tokens), f32),
            jax.ShapeDtypeStruct((rank // 2, features), bf16),
        ),
        in_specs=[IN_SMEM, pl.BlockSpec((features, rank), lambda i: (0, 0)), pl.BlockSpec((tokens, features), lambda i: (0, 0))],
        out_specs=(
            pl.BlockSpec((1, rank // 2, tokens), lambda i: (0, 0, 0)),
            pl.BlockSpec((rank // 2, features), lambda i: (0, 0)),
        ),
        compiler_params=params(),
        cost_estimate=cost(flops * 2, 5 << 20),
    )(core_at, basis, activations)
    partial = pl.pallas_call(
        project_other,
        grid=(1,),
        out_shape=jax.ShapeDtypeStruct((2, rank // 2, tokens), f32),
        in_specs=[
            pl.BlockSpec((rank // 2, features), lambda i: (0, 0)),
            pl.BlockSpec((tokens, features), lambda i: (0, 0)),
            IN_HBM,
        ],
        out_specs=pl.BlockSpec((1, rank // 2, tokens), lambda i: (1, 0, 0)),
        input_output_aliases={2: 0},
        compiler_params=params(),
        cost_estimate=cost(flops, 3 << 20),
    )(picked, other_act, partial)
    projected = lax.psum(partial, "fsdp").astype(bf16)

    terms = pl.pallas_call(
        grad_terms,
        out_shape=jax.ShapeDtypeStruct((rank // 2, columns), bf16),
        in_specs=[IN_VMEM, IN_VMEM, IN_VMEM, IN_HBM],
        out_specs=IN_VMEM,
        compiler_params=params(),
        cost_estimate=cost(2 * rank * tokens * columns, 5 << 20),
    )(projected, cotangent, other_cot, chip_basis)
    terms = lax.all_to_all(terms.reshape(chips, own_rows, columns), "chip", 0, 0, tiled=True)

    moment_next, square_next, copies = pl.pallas_call(
        adam,
        out_shape=(
            jax.ShapeDtypeStruct((own_rows, columns), f32),
            jax.ShapeDtypeStruct((own_rows, columns), f32),
            jax.ShapeDtypeStruct((chips, own_rows, columns), bf16),
        ),
        in_specs=[IN_VMEM] * 3,
        out_specs=(IN_VMEM,) * 3,
        compiler_params=params(),
        cost_estimate=cost(1 << 20, 2 << 20),
    )(terms, first_moment, second_moment)
    mine = lax.all_to_all(copies, "chip", 0, 0, tiled=True)
    other = lax.ppermute(mine, "core", SWAP)
    expanded = pl.pallas_call(
        expand,
        out_shape=jax.ShapeDtypeStruct((features // 2, columns), bf16),
        in_specs=[IN_SMEM] + [IN_VMEM] * 3,
        out_specs=IN_VMEM,
        scratch_shapes=[pltpu.VMEM((chips, 2, own_rows, columns), bf16)],
        compiler_params=params(),
        cost_estimate=cost(features * rank * columns, 4 << 20),
    )(core_at, chip_basis, mine, other)
    return (moment_next, square_next, expanded)


def solution(mesh):
    devices = np.asarray(mesh.devices)
    inner = Mesh(devices.reshape(devices.shape[0] // 2, 2, devices.shape[1]), ("chip", "core", "fsdp"))
    split = P(("chip", "core"), "fsdp")
    in_specs = (split, split, P("fsdp", None), split, split)
    return jax.shard_map(body, mesh=inner, in_specs=in_specs, out_specs=(split, split, split), check_vma=False)
```

time: 278 us -> 183 us (0.66)
  waiting for transfers between devices: 168 us -> 2.1 us
  blocking collectives: 79.5 us -> 124 us
  starting transfers between devices: 0.12 us -> 23.2 us
  matrix products: 11 us -> 0 us
  Pallas kernels: 0 us -> 8.66 us
  local copies, waits for them, and re-layouts: 1.14 us -> 9.66 us
    reduce_scatter x1 -> x0, waiting for transfers between devices: 106 us -> none  [body(): gradient = lax.psum_scatter(total, 'dp', scatter_dimension=0, tiled=True)]
    all_gather x1, waiting for transfers between devices: 36.5 us -> 0.01 us  [body(): chip_basis = lax.all_gather(piece, 'fsdp', axis=0, tiled=True)]
    all_to_all x0 -> x2, blocking collectives: none -> 30.7 us  [the longest x1 17 us: body(): lax.all_to_all(terms.reshape(chips, own_rows, columns), 'chip', 0, 0, til...]
    psum x1 -> x0, waiting for transfers between devices: 25.8 us -> none  [broadcast(): return lax.psum(jnp.where(mine, value, jnp.zeros_like(value)), axis)]
    ppermute x0 -> x4, starting transfers between devices: none -> 23.2 us  [the longest x1 11.8 us: body(): other = lax.ppermute(mine, 'core', SWAP)]
    psum x1, blocking collectives: 79.5 us -> 93.7 us  [body(): projected = lax.psum(partial, 'fsdp').astype(bf16)]
    dot_general x3 -> x0, matrix products: 11 us -> none  [the longest x1 4.2 us: body(): jnp.dot(activations, basis, preferred_element_type=jnp.float32)]
    pallas_call x0 -> x5, Pallas kernels: none -> 8.66 us  [the longest x1 3.12 us: body(): pl.pallas_call(grad_terms, out_shape=jax.ShapeDtypeStruct((rank // 2, col...]
  transfers between devices with their start and end apart: 3 -> 5, of which waited for: 3 -> 1; matrix products, arithmetic and copies ran while one was open for 1% -> 0% of each run, Pallas kernels for 0% -> 2%
where the time goes in v1:
time: 183 us; the launch traced here: 182 us
  blocking collectives  124 us (68%)
  starting transfers between devices  23.2 us (13%)
  between operations  14.2 us (8%)
  local copies, waits for them, and re-layouts  9.66 us (5%)
  Pallas kernels  8.66 us (5%)
  waiting for transfers between devices  2.1 us (1%)
    psum x1, blocking collectives, body(): projected = lax.psum(partial, 'fsdp').astype(bf16)  93.7 us
    all_to_all x1, blocking collectives, body(): lax.all_to_all(terms.reshape(chips, own_rows, columns), 'chip', 0, 0, til...  17 us
    all_to_all x1, blocking collectives, body(): mine = lax.all_to_all(copies, 'chip', 0, 0, tiled=True)  13.7 us
    ppermute x1, starting transfers between devices, body(): other = lax.ppermute(mine, 'core', SWAP)  11.8 us
    unnamed x20, local copies, waits for them, and re-layouts  8.81 us
    ppermute x1, starting transfers between devices, body(): other_act = lax.ppermute(activations, 'core', SWAP)  8.79 us
  transfers between devices with their start and end apart: 5, of which 1 were waited for; matrix products, arithmetic and copies ran while one was open for 0% of the time, Pallas kernels for 2%

profile of v1, /device:TPU:1, one launch (start us, length us, event | category | flops | bytes accessed | tf_op | source)
XLA Modules:
  0.0 182.2 jit_solution(11098435083743638541)
XLA Ops:
  7.2 0.0 all-gather.2.cloned.1.call-start
  7.2 8.8 %collective-permute-start = (bf16[768,512]{1,0:T(8,128)(2,1)}, bf16[768,512]{1,0:T(8,128)(2,1)}, u32[]{:S(2)}, u32[]{:S(2)}) collective-permute-start(bf16[768,512]{1,0:T(8,128)(2,1)} %refs_2_.1), channel_id=1, source_target_pairs={{0,16},{16,0},{1,17},{17,1},{2,18},{18,2},{3,19},{19,3},{4,20},{20... | collective-permute-start | bytes 2359304 | tf_op jit(solution)/shard_map/ppermute | solution.py:91
  16.0 1.9 %collective-permute-start.1 = (bf16[768,896]{1,0:T(8,128)(2,1)}, bf16[768,896]{1,0:T(8,128)(2,1)}, u32[]{:S(2)}, u32[]{:S(2)}) collective-permute-start(bf16[768,896]{1,0:T(8,128)(2,1)} %own_ref.1), channel_id=1, source_target_pairs={{0,16},{16,0},{1,17},{17,1},{2,18},{18,2},{3,19},{19,3},{4,20},{20... | collective-permute-start | bytes 4128776 | tf_op jit(solution)/shard_map/ppermute | solution.py:92
  18.0 0.8 constant_dynamic-slice_fusion
  18.8 0.7 collective-permute-start.2
  19.5 0.0 copy-start.7
  19.5 1.2 copy-done.7
  20.7 0.0 copy-start.8
  20.7 1.1 copy-done.8
  21.8 1.3 shard_map.76
  23.2 0.0 copy-start.3
  23.2 0.8 copy-done.3
  24.0 0.0 collective-permute-done.2
  24.0 0.0 copy-start.9
  24.0 0.6 copy-done.9
  24.6 0.0 all-gather.2.cloned.1.call-update
  24.6 0.0 collective-permute-done.act_ref
  24.6 0.0 copy-start.4
  24.7 1.0 copy-done.4
  25.7 1.7 shard_map.77
  27.4 93.7 %all-reduce.1.proj_ref = bf16[2,512,768]{2,1,0:T(8,128)(2,1)} all-reduce(f32[2,512,768]{2,1,0:T(8,128)S(1)} %shard_map.77), channel_id=1, replica_groups=mesh['chip'=16,'core'=2,'fsdp'=16] {'fsdp'}, use_global_device_ids=true, to_apply=%region_0.1 | all-reduce | flops 786432 | bytes 4718592 | tf_op jit(solution)/shard_map/psum | solution.py:123
  121.1 0.0 collective-permute-done.1.other_ref
  121.1 0.0 all-gather.2.cloned.1.call-done._.shard_ref
  121.1 0.0 copy-start
  121.1 1.4 copy-done
  122.5 0.0 copy-start.1
  122.5 1.2 copy-done.1
  123.8 0.0 copy-start.2
  123.8 1.3 copy-done.2
  125.1 3.1 %shard_map.78 = bf16[512,896]{1,0:T(8,128)(2,1)S(1)} custom-call(bf16[2,512,768]{2,1,0:T(8,128)(2,1)S(1)} %copy-done, bf16[768,896]{1,0:T(8,128)(2,1)S(1)} %copy-done.2, bf16[768,896]{1,0:T(8,128)(2,1)} %collective-permute-done.1.other_ref, bf16[512,1024]{1,0:T(8,128)(2,1)S(1)} %copy-done.1), custom_call_target="tpu_custom_call" | custom-call | flops 1409286144 | bytes 5242880 | tf_op jit(solution)/shard_map/pallas_call | solution.py:125
  128.2 0.0 copy-start.5
  128.2 0.0 copy-start.6
  128.3 17.0 %all_to_all.10.terms_ref = bf16[16,32,896]{2,1,0:T(8,128)(2,1)S(1)} all-to-all(bf16[16,32,896]{2,1,0:T(8,128)(2,1)S(1)} %bitcast.2), channel_id=1, replica_groups=mesh['chip'=16,'core'=2,'fsdp'=16] {'chip'}, dimensions={0} | all-to-all | bytes 1835008 | tf_op jit(solution)/shard_map/all_to_all | solution.py:133
  145.2 0.0 copy-done.5
  145.2 0.0 copy-done.6
  145.2 0.9 shard_map.79
  146.1 13.7 %all_to_all.11.mine_ref = bf16[16,32,896]{2,1,0:T(8,128)(2,1)S(1)} all-to-all(bf16[16,32,896]{2,1,0:T(8,128)(2,1)S(1)} %get-tuple-element.12), channel_id=1, replica_groups=mesh['chip'=16,'core'=2,'fsdp'=16] {'chip'}, dimensions={0} | all-to-all | bytes 1835008 | tf_op jit(solution)/shard_map/all_to_all | solution.py:147
  159.8 11.8 %collective-permute-start.3 = (bf16[16,32,896]{2,1,0:T(8,128)(2,1)S(1)}, bf16[16,32,896]{2,1,0:T(8,128)(2,1)S(1)}, u32[]{:S(2)}, u32[]{:S(2)}) collective-permute-start(bf16[16,32,896]{2,1,0:T(8,128)(2,1)S(1)} %all_to_all.11.mine_ref), channel_id=1, source_target_pairs={{0,16},{16,0},{1,17},{17,1},{2,18},{18,2},{3,19},{19,3},{4,20},{20... | collective-permute-start | bytes 2752520 | tf_op jit(solution)/shard_map/ppermute | solution.py:148
  171.7 2.1 %collective-permute-done.3.other_ref = bf16[16,32,896]{2,1,0:T(8,128)(2,1)S(1)} collective-permute-done((bf16[16,32,896]{2,1,0:T(8,128)(2,1)S(1)}, bf16[16,32,896]{2,1,0:T(8,128)(2,1)S(1)}, u32[]{:S(2)}, u32[]{:S(2)}) %collective-permute-start.3) | collective-permute-done | bytes 917536 | tf_op jit(solution)/shard_map/ppermute | solution.py:148
  173.8 1.6 shard_map.80
Async XLA Ops:
  7.2 114.0 %all-gather.2.cloned.1.call-start = ((), (), s32[]{:S(2)}) async-start(), calls=%async_computation.2 | async-start | bytes 1114112 | tf_op jit(solution)/shard_map/all_gather | solution.py:89
  7.2 17.4 %collective-permute-start = (bf16[768,512]{1,0:T(8,128)(2,1)}, bf16[768,512]{1,0:T(8,128)(2,1)}, u32[]{:S(2)}, u32[]{:S(2)}) collective-permute-start(bf16[768,512]{1,0:T(8,128)(2,1)} %refs_2_.1), channel_id=1, source_target_pairs={{0,16},{16,0},{1,17},{17,1},{2,18},{18,2},{3,19},{19,3},{4,20},{20... | collective-permute-start | bytes 2359304 | tf_op jit(solution)/shard_map/ppermute | solution.py:91
  16.0 105.1 %collective-permute-start.1 = (bf16[768,896]{1,0:T(8,128)(2,1)}, bf16[768,896]{1,0:T(8,128)(2,1)}, u32[]{:S(2)}, u32[]{:S(2)}) collective-permute-start(bf16[768,896]{1,0:T(8,128)(2,1)} %own_ref.1), channel_id=1, source_target_pairs={{0,16},{16,0},{1,17},{17,1},{2,18},{18,2},{3,19},{19,3},{4,20},{20... | collective-permute-start | bytes 4128776 | tf_op jit(solution)/shard_map/ppermute | solution.py:92
  18.8 5.2 %collective-permute-start.2 = (bf16[32,1024]{1,0:T(8,128)(2,1)S(1)}, bf16[32,1024]{1,0:T(8,128)(2,1)S(1)}, u32[]{:S(2)}, u32[]{:S(2)}) collective-permute-start(bf16[32,1024]{1,0:T(8,128)(2,1)S(1)} %constant_dynamic-slice_fusion), channel_id=1, source_target_pairs={{0,0},{1,47},{2,78},{3,109},{4,140},{5,171},{6,202},{7,233},{8,264... | collective-permute-start | bytes 196616 | tf_op jit(solution)/shard_map/ppermute | solution.py:88
  19.5 1.2 copy-start.7
  20.7 1.1 copy-start.8
  23.2 0.8 copy-start.3
  24.0 0.6 copy-start.9
  24.6 1.0 copy-start.4
  121.1 1.4 copy-start
  122.5 1.2 copy-start.1
  123.8 1.3 copy-start.2
  128.2 17.0 %copy-start.5 = (f32[32,896]{1,0:T(8,128)S(1)}, f32[32,896]{1,0:T(8,128)}, u32[]{:S(2)}) copy-start(f32[32,896]{1,0:T(8,128)} %first_ref.1) | copy-start | bytes 344068
  128.2 17.0 %copy-start.6 = (f32[32,896]{1,0:T(8,128)S(1)}, f32[32,896]{1,0:T(8,128)}, u32[]{:S(2)}) copy-start(f32[32,896]{1,0:T(8,128)} %second_ref.1) | copy-start | bytes 344068
  159.8 13.9 %collective-permute-start.3 = (bf16[16,32,896]{2,1,0:T(8,128)(2,1)S(1)}, bf16[16,32,896]{2,1,0:T(8,128)(2,1)S(1)}, u32[]{:S(2)}, u32[]{:S(2)}) collective-permute-start(bf16[16,32,896]{2,1,0:T(8,128)(2,1)S(1)} %all_to_all.11.mine_ref), channel_id=1, source_target_pairs={{0,16},{16,0},{1,17},{17,1},{2,18},{18,2},{3,19},{19,3},{4,20},{20... | collective-permute-start | bytes 2752520 | tf_op jit(solution)/shard_map/ppermute | solution.py:148
Sparse Core Ops, SparseCore 0:
  24.8 75.1 all-gather.1

commit v2 on v1

v2 whole, which is shorter than its diff:
```python
import numpy as np
import jax
import jax.numpy as jnp
from jax import lax
from jax.experimental import pallas as pl
from jax.experimental.pallas import tpu as pltpu
from jax.sharding import Mesh, PartitionSpec as P

decay_first = 0.9
decay_second = 0.999
epsilon = 1e-08

SWAP = [(0, 1), (1, 0)]
VMEM_LIMIT = 40 * 1024 * 1024
LAST = (((1,), (1,)), ((), ()))
IN_VMEM = pl.BlockSpec(memory_space=pltpu.VMEM)
IN_HBM = pl.BlockSpec(memory_space=pltpu.HBM)
IN_SMEM = pl.BlockSpec(memory_space=pltpu.SMEM)


def params(limit=VMEM_LIMIT):
    return pltpu.CompilerParams(vmem_limit_bytes=limit)


def cost(flops, moved):
    return pl.CostEstimate(flops=flops, bytes_accessed=moved, transcendentals=0)


def project_own(own_rows, place_ref, basis_hbm, act_hbm, out_hbm, picked_ref, basis_ref, act_ref, own_ref, block_ref, sems):
    features, rank = basis_ref.shape
    tokens = act_ref.shape[0]
    half = rank // 2
    rows = features // 2
    core, holds = place_ref[0], place_ref[1]
    load_basis = pltpu.make_async_copy(basis_hbm, basis_ref, sems.at[0])
    load_act = pltpu.make_async_copy(act_hbm, act_ref, sems.at[1])
    load_basis.start()
    load_act.start()
    at = lax.broadcasted_iota(jnp.int32, (half, rank), 0)
    wanted = at // own_rows * (2 * own_rows) + core * own_rows + at % own_rows
    pick = (lax.broadcasted_iota(jnp.int32, (half, rank), 1) == wanted).astype(jnp.bfloat16)
    load_basis.wait()
    mine = basis_ref[pl.ds(pl.multiple_of(core * rows, rows), rows), :].astype(jnp.float32)
    mine = jnp.where(holds == 1, mine, 0.0)
    block_ref[:rows, :] = mine[:, :half]
    block_ref[rows:, :] = mine[:, half:]
    save_block = pltpu.make_async_copy(block_ref, out_hbm.at[:, pl.ds(2 * tokens, half)], sems.at[2])
    save_block.start()
    picked = lax.dot_general(pick, basis_ref[...], LAST, preferred_element_type=jnp.float32).astype(jnp.bfloat16)
    picked_ref[...] = picked
    load_act.wait()
    own_ref[...] = lax.dot_general(picked, act_ref[...], LAST, preferred_element_type=jnp.float32)
    save_own = pltpu.make_async_copy(own_ref, out_hbm.at[:, pl.ds(0, tokens)], sems.at[3])
    save_own.start()
    save_block.wait()
    save_own.wait()


def project_other(picked_ref, act_ref, _, out_hbm, other_ref, sems):
    tokens = act_ref.shape[0]
    half = other_ref.shape[0] // 2
    copies = []
    for i in range(2):
        rows = pl.ds(i * half, half)
        other_ref[rows, :] = lax.dot_general(picked_ref[rows, :], act_ref[...], LAST, preferred_element_type=jnp.float32)
        copies.append(pltpu.make_async_copy(other_ref.at[rows, :], out_hbm.at[rows, pl.ds(tokens, tokens)], sems.at[i]))
        copies[i].start()
    for copy in copies:
        copy.wait()


def grad_terms(proj_ref, own_ref, other_hbm, out_ref, other_ref, sems):
    tokens = own_ref.shape[0]
    part = tokens // 4
    copies = []
    for i in range(4):
        rows = pl.ds(i * part, part)
        copies.append(pltpu.make_async_copy(other_hbm.at[rows, :], other_ref.at[rows, :], sems.at[i]))
        copies[i].start()
    total = jnp.dot(proj_ref[:, :tokens], own_ref[...], preferred_element_type=jnp.float32)
    for copy in copies:
        copy.wait()
    total += jnp.dot(proj_ref[:, tokens : 2 * tokens], other_ref[...], preferred_element_type=jnp.float32)
    out_ref[...] = total.astype(jnp.bfloat16)


def adam(terms_ref, first_ref, second_ref, moment_ref, square_ref, copies_ref):
    gradient = terms_ref[0].astype(jnp.float32)
    for i in range(1, terms_ref.shape[0]):
        gradient += terms_ref[i].astype(jnp.float32)
    moment_next = decay_first * first_ref[...] + (1.0 - decay_first) * gradient
    square_next = decay_second * second_ref[...] + (1.0 - decay_second) * gradient * gradient
    moment_ref[...] = moment_next
    square_ref[...] = square_next
    direction = (moment_next / (jnp.sqrt(square_next) + epsilon)).astype(jnp.bfloat16)
    for i in range(copies_ref.shape[0]):
        copies_ref[i] = direction


def expand(place_ref, summed_hbm, mine_ref, other_ref, out_ref, block_ref, all_ref, sem):
    half = block_ref.shape[0]
    columns = out_ref.shape[1]
    rows = out_ref.shape[0]
    core = place_ref[0]
    copy = pltpu.make_async_copy(summed_hbm.at[:, pl.ds(summed_hbm.shape[1] - half, half)], block_ref, sem)
    copy.start()
    all_ref[:, pl.ds(core, 1)] = mine_ref[...][:, None]
    all_ref[:, pl.ds(1 - core, 1)] = other_ref[...][:, None]
    direction = all_ref[...].reshape(2 * half, columns)
    copy.wait()
    total = jnp.dot(block_ref[:rows, :], direction[:half], preferred_element_type=jnp.float32)
    total += jnp.dot(block_ref[rows:, :], direction[half:], preferred_element_type=jnp.float32)
    out_ref[...] = total.astype(jnp.bfloat16)


def body(activations, cotangent, basis, first_moment, second_moment):
    chips = lax.axis_size("chip")
    features, rank = basis.shape
    tokens = activations.shape[0]
    half = rank // 2
    own_rows, columns = first_moment.shape
    core = lax.axis_index("core")
    holds = lax.axis_index("chip") == lax.axis_index("fsdp")
    place = jnp.stack([core, holds]).astype(jnp.int32)
    f32, bf16 = jnp.float32, jnp.bfloat16

    other_act = lax.ppermute(activations, "core", SWAP)
    other_cot = lax.ppermute(cotangent, "core", SWAP)
    partial, picked = pl.pallas_call(
        lambda *refs: project_own(own_rows, *refs),
        out_shape=(pltpu.HBM((half, 2 * tokens + half), f32), pltpu.VMEM((half, features), bf16)),
        in_specs=[IN_SMEM, IN_HBM, IN_HBM],
        out_specs=(IN_HBM, IN_VMEM),
        scratch_shapes=[
            pltpu.VMEM((features, rank), bf16),
            pltpu.VMEM((tokens, features), bf16),
            pltpu.VMEM((half, tokens), f32),
            pltpu.VMEM((half, half), f32),
            pltpu.SemaphoreType.DMA((4,)),
        ],
        compiler_params=params(60 * 1024 * 1024),
        cost_estimate=cost(2 * rank * tokens * features, 5 << 20),
    )(place, basis, activations)
    partial = pl.pallas_call(
        project_other,
        out_shape=pltpu.HBM((half, 2 * tokens + half), f32),
        in_specs=[IN_VMEM, IN_VMEM, IN_HBM],
        out_specs=IN_HBM,
        scratch_shapes=[pltpu.VMEM((half, tokens), f32), pltpu.SemaphoreType.DMA((2,))],
        input_output_aliases={2: 0},
        compiler_params=params(),
        cost_estimate=cost(rank * tokens * features, 3 << 20),
    )(picked, other_act, partial)
    summed = lax.psum(partial, "fsdp").astype(bf16)

    terms = pl.pallas_call(
        grad_terms,
        out_shape=jax.ShapeDtypeStruct((half, columns), bf16),
        in_specs=[IN_VMEM, IN_VMEM, IN_HBM],
        out_specs=IN_VMEM,
        scratch_shapes=[pltpu.VMEM((tokens, columns), bf16), pltpu.SemaphoreType.DMA((4,))],
        compiler_params=params(),
        cost_estimate=cost(2 * rank * tokens * columns, 5 << 20),
    )(summed, cotangent, other_cot)
    terms = lax.all_to_all(terms.reshape(chips, own_rows, columns), "chip", 0, 0, tiled=True)

    moment_next, square_next, copies = pl.pallas_call(
        adam,
        out_shape=(
            jax.ShapeDtypeStruct((own_rows, columns), f32),
            jax.ShapeDtypeStruct((own_rows, columns), f32),
            jax.ShapeDtypeStruct((chips, own_rows, columns), bf16),
        ),
        in_specs=[IN_VMEM] * 3,
        out_specs=(IN_VMEM,) * 3,
        compiler_params=params(),
        cost_estimate=cost(1 << 20, 2 << 20),
    )(terms, first_moment, second_moment)
    mine = lax.all_to_all(copies, "chip", 0, 0, tiled=True)
    other = lax.ppermute(mine, "core", SWAP)
    expanded = pl.pallas_call(
        expand,
        out_shape=jax.ShapeDtypeStruct((features // 2, columns), bf16),
        in_specs=[IN_SMEM, IN_HBM, IN_VMEM, IN_VMEM],
        out_specs=IN_VMEM,
        scratch_shapes=[
            pltpu.VMEM((half, half), bf16),
            pltpu.VMEM((chips, 2, own_rows, columns), bf16),
            pltpu.SemaphoreType.DMA,
        ],
        compiler_params=params(),
        cost_estimate=cost(features * rank * columns, 4 << 20),
    )(place, summed, mine, other)
    return (moment_next, square_next, expanded)


def solution(mesh):
    devices = np.asarray(mesh.devices)
    inner = Mesh(devices.reshape(devices.shape[0] // 2, 2, devices.shape[1]), ("chip", "core", "fsdp"))
    split = P(("chip", "core"), "fsdp")
    in_specs = (split, split, P("fsdp", None), split, split)
    return jax.shard_map(body, mesh=inner, in_specs=in_specs, out_specs=(split, split, split), check_vma=False)
```

time: 183 us -> 164 us (0.90)
  between operations: 14.2 us -> 0.75 us
  local copies, waits for them, and re-layouts: 9.66 us -> 0.03 us
  blocking collectives: 124 us -> 129 us
  Pallas kernels: 8.66 us -> 12.9 us
  starting transfers between devices: 23.2 us -> 19.1 us
    unnamed x20 -> x8, local copies, waits for them, and re-layouts: 8.81 us -> 0.03 us
    pallas_call x3, Pallas kernels: 6.17 us -> 9.69 us  [the longest x1 4.81 us: body(): pl.pallas_call(lambda *refs: project_own(own_rows, *refs), out_shape=(plt...]
    ppermute x1, starting transfers between devices: 11.8 us -> 8.34 us  [body(): other = lax.ppermute(mine, 'core', SWAP)]
    psum x1, blocking collectives: 93.7 us -> 96.7 us  [body(): summed = lax.psum(partial, 'fsdp').astype(bf16)]
  transfers between devices with their start and end apart: 5 -> 3, of which waited for: 1 -> 1; matrix products, arithmetic and copies ran while one was open for 0% -> 0% of each run, Pallas kernels for 2% -> 4%
where the time goes in v2:
time: 164 us
  blocking collectives  129 us (79%)
  starting transfers between devices  19.1 us (12%)
  Pallas kernels  12.9 us (8%)
  waiting for transfers between devices  2.08 us (1%)
    psum x1, blocking collectives, body(): summed = lax.psum(partial, 'fsdp').astype(bf16)  96.7 us
    all_to_all x1, blocking collectives, body(): lax.all_to_all(terms.reshape(chips, own_rows, columns), 'chip', 0, 0, til...  18.1 us
    all_to_all x1, blocking collectives, body(): mine = lax.all_to_all(copies, 'chip', 0, 0, tiled=True)  13.8 us
    ppermute x1, starting transfers between devices, body(): other_act = lax.ppermute(activations, 'core', SWAP)  8.79 us
    ppermute x1, starting transfers between devices, body(): other = lax.ppermute(mine, 'core', SWAP)  8.34 us
    pallas_call x1, Pallas kernels, body(): pl.pallas_call(lambda *refs: project_own(own_rows, *refs), out_shape=(plt...  4.81 us
  transfers between devices with their start and end apart: 3, of which 1 were waited for; matrix products, arithmetic and copies ran while one was open for 0% of the time, Pallas kernels for 4%

profile of v2, /device:TPU:1, one launch (start us, length us, event | category | flops | bytes accessed | tf_op | source)
XLA Modules:
  0.0 164.1 jit_solution(1120369951286710847)
XLA Ops:
  0.6 8.8 %collective-permute-start = (bf16[768,512]{1,0:T(8,128)(2,1)}, bf16[768,512]{1,0:T(8,128)(2,1)S(1)}, u32[]{:S(2)}, u32[]{:S(2)}) collective-permute-start(bf16[768,512]{1,0:T(8,128)(2,1)} %refs_2_.1), channel_id=1, source_target_pairs={{0,16},{16,0},{1,17},{17,1},{2,18},{18,2},{3,19},{19,3},{4,20},{20... | collective-permute-start | bytes 2359304 | tf_op jit(solution)/shard_map/ppermute | solution.py:127
  9.4 1.9 %collective-permute-start.1 = (bf16[768,896]{1,0:T(8,128)(2,1)}, bf16[768,896]{1,0:T(8,128)(2,1)}, u32[]{:S(2)}, u32[]{:S(2)}) collective-permute-start(bf16[768,896]{1,0:T(8,128)(2,1)} %own_ref.1), channel_id=1, source_target_pairs={{0,16},{16,0},{1,17},{17,1},{2,18},{18,2},{3,19},{19,3},{4,20},{20... | collective-permute-start | bytes 4128776 | tf_op jit(solution)/shard_map/ppermute | solution.py:128
  11.4 0.6 pad_add_fusion.refs_0_.place_ref
  12.0 4.8 %shard_map.76 = (f32[512,2048]{1,0:T(8,128)}, bf16[512,512]{1,0:T(8,128)(2,1)S(1)}) custom-call(s32[2]{0:T(128)} %pad_add_fusion.refs_0_.place_ref, bf16[512,1024]{1,0:T(8,128)(2,1)} %refs_1_.1, bf16[768,512]{1,0:T(8,128)(2,1)} %refs_2_.1), custom_call_target="tpu_custom_call" | custom-call | flops 805306368 | bytes 5242880 | tf_op jit(solution)/shard_map/pallas_call | solution.py:129
  16.8 0.0 collective-permute-done.act_ref
  16.8 1.7 %shard_map.77 = f32[512,2048]{1,0:T(8,128)} custom-call(bf16[512,512]{1,0:T(8,128)(2,1)S(1)} %get-tuple-element.8.picked_ref, bf16[768,512]{1,0:T(8,128)(2,1)S(1)} %collective-permute-done.act_ref, f32[512,2048]{1,0:T(8,128)} %get-tuple-element.9._), custom_call_target="tpu_custom_call", output_to_operand_aliasing={{}: (2, {})} | custom-call | flops 402653184 | bytes 3145728 | tf_op jit(solution)/shard_map/pallas_call | solution.py:144
  18.5 0.0 copy-start
  18.5 96.7 %all-reduce.1.proj_ref.summed_hbm = bf16[512,2048]{1,0:T(8,128)(2,1)S(1)} all-reduce(f32[512,2048]{1,0:T(8,128)} %shard_map.77), channel_id=1, replica_groups=mesh['chip'=16,'core'=2,'fsdp'=16] {'fsdp'}, use_global_device_ids=true, to_apply=%region_0.0 | all-reduce | flops 1048576 | bytes 6291456 | tf_op jit(solution)/shard_map/psum | solution.py:154
  115.2 0.0 copy-start.1
  115.2 0.0 copy-start.2
  115.2 0.0 collective-permute-done.1.other_hbm
  115.2 0.0 copy-done
  115.3 3.2 %shard_map.78 = bf16[512,896]{1,0:T(8,128)(2,1)S(1)} custom-call(bf16[512,2048]{1,0:T(8,128)(2,1)S(1)} %all-reduce.1.proj_ref.summed_hbm, bf16[768,896]{1,0:T(8,128)(2,1)S(1)} %copy-done, bf16[768,896]{1,0:T(8,128)(2,1)} %collective-permute-done.1.other_hbm), custom_call_target="tpu_custom_call" | custom-call | flops 1409286144 | bytes 5242880 | tf_op jit(solution)/shard_map/pallas_call | solution.py:156
  118.4 0.0 copy-start.3
  118.4 18.1 %all_to_all.10.terms_ref = bf16[16,32,896]{2,1,0:T(8,128)(2,1)S(1)} all-to-all(bf16[16,32,896]{2,1,0:T(8,128)(2,1)S(1)} %bitcast.3), channel_id=1, replica_groups=mesh['chip'=16,'core'=2,'fsdp'=16] {'chip'}, dimensions={0} | all-to-all | bytes 1835008 | tf_op jit(solution)/shard_map/all_to_all | solution.py:165
  136.6 0.0 copy-done.1
  136.6 0.0 copy-done.2
  136.6 0.9 shard_map.79
  137.5 13.8 %all_to_all.11.mine_ref = bf16[16,32,896]{2,1,0:T(8,128)(2,1)S(1)} all-to-all(bf16[16,32,896]{2,1,0:T(8,128)(2,1)S(1)} %get-tuple-element.12), channel_id=1, replica_groups=mesh['chip'=16,'core'=2,'fsdp'=16] {'chip'}, dimensions={0} | all-to-all | bytes 1835008 | tf_op jit(solution)/shard_map/all_to_all | solution.py:179
  151.3 8.3 %collective-permute-start.2 = (bf16[16,32,896]{2,1,0:T(8,128)(2,1)S(1)}, bf16[16,32,896]{2,1,0:T(8,128)(2,1)S(1)}, u32[]{:S(2)}, u32[]{:S(2)}) collective-permute-start(bf16[16,32,896]{2,1,0:T(8,128)(2,1)S(1)} %all_to_all.11.mine_ref), channel_id=1, source_target_pairs={{0,16},{16,0},{1,17},{17,1},{2,18},{18,2},{3,19},{19,3},{4,20},{20... | collective-permute-start | bytes 2752520 | tf_op jit(solution)/shard_map/ppermute | solution.py:180
  159.7 2.1 %collective-permute-done.2.other_ref = bf16[16,32,896]{2,1,0:T(8,128)(2,1)S(1)} collective-permute-done((bf16[16,32,896]{2,1,0:T(8,128)(2,1)S(1)}, bf16[16,32,896]{2,1,0:T(8,128)(2,1)S(1)}, u32[]{:S(2)}, u32[]{:S(2)}) %collective-permute-start.2) | collective-permute-done | bytes 917536 | tf_op jit(solution)/shard_map/ppermute | solution.py:180
  161.7 0.0 copy-done.3
  161.8 2.4 %shard_map.80 = bf16[256,896]{1,0:T(8,128)(2,1)} custom-call(s32[2]{0:T(128)S(1)} %copy-done.3, bf16[512,2048]{1,0:T(8,128)(2,1)S(1)} %all-reduce.1.proj_ref.summed_hbm, bf16[16,32,896]{2,1,0:T(8,128)(2,1)S(1)} %all_to_all.11.mine_ref, bf16[16,32,896]{2,1,0:T(8,128)(2,1)S(1)} %collective-permute-done.2.other_ref), custom_call_target="tpu_custom_call" | custom-call | flops 469762048 | bytes 4194304 | tf_op jit(solution)/shard_map/pallas_call | solution.py:181
Async XLA Ops:
  0.6 16.1 %collective-permute-start = (bf16[768,512]{1,0:T(8,128)(2,1)}, bf16[768,512]{1,0:T(8,128)(2,1)S(1)}, u32[]{:S(2)}, u32[]{:S(2)}) collective-permute-start(bf16[768,512]{1,0:T(8,128)(2,1)} %refs_2_.1), channel_id=1, source_target_pairs={{0,16},{16,0},{1,17},{17,1},{2,18},{18,2},{3,19},{19,3},{4,20},{20... | collective-permute-start | bytes 2359304 | tf_op jit(solution)/shard_map/ppermute | solution.py:127
  9.4 105.8 %collective-permute-start.1 = (bf16[768,896]{1,0:T(8,128)(2,1)}, bf16[768,896]{1,0:T(8,128)(2,1)}, u32[]{:S(2)}, u32[]{:S(2)}) collective-permute-start(bf16[768,896]{1,0:T(8,128)(2,1)} %own_ref.1), channel_id=1, source_target_pairs={{0,16},{16,0},{1,17},{17,1},{2,18},{18,2},{3,19},{19,3},{4,20},{20... | collective-permute-start | bytes 4128776 | tf_op jit(solution)/shard_map/ppermute | solution.py:128
  18.5 96.7 %copy-start = (bf16[768,896]{1,0:T(8,128)(2,1)S(1)}, bf16[768,896]{1,0:T(8,128)(2,1)}, u32[]{:S(2)}) copy-start(bf16[768,896]{1,0:T(8,128)(2,1)} %own_ref.1) | copy-start | bytes 4128772
  115.2 21.4 %copy-start.1 = (f32[32,896]{1,0:T(8,128)S(1)}, f32[32,896]{1,0:T(8,128)}, u32[]{:S(2)}) copy-start(f32[32,896]{1,0:T(8,128)} %first_ref.1) | copy-start | bytes 344068
  115.2 21.4 %copy-start.2 = (f32[32,896]{1,0:T(8,128)S(1)}, f32[32,896]{1,0:T(8,128)}, u32[]{:S(2)}) copy-start(f32[32,896]{1,0:T(8,128)} %second_ref.1) | copy-start | bytes 344068
  118.4 43.3 %copy-start.3 = (s32[2]{0:T(128)S(1)}, s32[2]{0:T(128)}, u32[]{:S(2)}) copy-start(s32[2]{0:T(128)} %pad_add_fusion.refs_0_.place_ref) | copy-start | bytes 28
  151.3 10.4 %collective-permute-start.2 = (bf16[16,32,896]{2,1,0:T(8,128)(2,1)S(1)}, bf16[16,32,896]{2,1,0:T(8,128)(2,1)S(1)}, u32[]{:S(2)}, u32[]{:S(2)}) collective-permute-start(bf16[16,32,896]{2,1,0:T(8,128)(2,1)S(1)} %all_to_all.11.mine_ref), channel_id=1, source_target_pairs={{0,16},{16,0},{1,17},{17,1},{2,18},{18,2},{3,19},{19,3},{4,20},{20... | collective-permute-start | bytes 2752520 | tf_op jit(solution)/shard_map/ppermute | solution.py:180

commit v3 on v2

v3 whole, which is shorter than its diff:
```python
import numpy as np
import jax
import jax.numpy as jnp
from jax import lax
from jax.experimental import pallas as pl
from jax.experimental.pallas import tpu as pltpu
from jax.sharding import Mesh, PartitionSpec as P

decay_first = 0.9
decay_second = 0.999
epsilon = 1e-08

SWAP = [(0, 1), (1, 0)]
VMEM_LIMIT = 40 * 1024 * 1024
LAST = (((1,), (1,)), ((), ()))
IN_VMEM = pl.BlockSpec(memory_space=pltpu.VMEM)
IN_HBM = pl.BlockSpec(memory_space=pltpu.HBM)
IN_SMEM = pl.BlockSpec(memory_space=pltpu.SMEM)


def params(limit=VMEM_LIMIT):
    return pltpu.CompilerParams(vmem_limit_bytes=limit)


def cost(flops, moved):
    return pl.CostEstimate(flops=flops, bytes_accessed=moved, transcendentals=0)


def project_rows(picked_ref, act_ref, out_ref, out_hbm, sems):
    part = out_ref.shape[0] // 4
    copies = []
    for i in range(4):
        rows = pl.ds(i * part, part)
        out_ref[rows, :] = lax.dot_general(picked_ref[rows, :], act_ref[...], LAST, preferred_element_type=jnp.float32)
        copies.append(pltpu.make_async_copy(out_ref.at[rows, :], out_hbm.at[rows, :], sems.at[i]))
        copies[i].start()
    for copy in copies:
        copy.wait()


def project_own(own_rows, place_ref, basis_hbm, act_hbm, out_hbm, picked_ref, basis_ref, act_ref, out_ref, sems):
    features, rank = basis_ref.shape
    half = rank // 2
    copies = []
    for hbm, ref in ((basis_hbm, basis_ref), (act_hbm, act_ref)):
        part = ref.shape[0] // 4
        for i in range(4):
            rows = pl.ds(i * part, part)
            copies.append(pltpu.make_async_copy(hbm.at[rows, :], ref.at[rows, :], sems.at[len(copies)]))
            copies[-1].start()
    at = lax.broadcasted_iota(jnp.int32, (half, rank), 0)
    wanted = at // own_rows * (2 * own_rows) + place_ref[0] * own_rows + at % own_rows
    pick = (lax.broadcasted_iota(jnp.int32, (half, rank), 1) == wanted).astype(jnp.bfloat16)
    for copy in copies[:4]:
        copy.wait()
    picked = lax.dot_general(pick, basis_ref[...], LAST, preferred_element_type=jnp.float32).astype(jnp.bfloat16)
    picked_ref[...] = picked
    for copy in copies[4:]:
        copy.wait()
    project_rows(picked_ref, act_ref, out_ref, out_hbm.at[0], sems)


def project_other(picked_ref, act_ref, _, out_hbm, out_ref, sems):
    project_rows(picked_ref, act_ref, out_ref, out_hbm.at[1], sems)


def grad_terms(proj_ref, own_ref, other_hbm, _, out_ref, other_ref, sems):
    tokens = own_ref.shape[0]
    part = tokens // 4
    copies = []
    for i in range(4):
        rows = pl.ds(i * part, part)
        copies.append(pltpu.make_async_copy(other_hbm.at[rows, :], other_ref.at[rows, :], sems.at[i]))
        copies[i].start()
    total = jnp.dot(proj_ref[0], own_ref[...], preferred_element_type=jnp.float32)
    for copy in copies:
        copy.wait()
    total += jnp.dot(proj_ref[1], other_ref[...], preferred_element_type=jnp.float32)
    out_ref[...] = total.astype(jnp.bfloat16)


def adam(terms_ref, first_ref, second_ref, moment_ref, square_ref, copies_ref):
    gradient = terms_ref[0].astype(jnp.float32)
    for i in range(1, terms_ref.shape[0]):
        gradient += terms_ref[i].astype(jnp.float32)
    moment_next = decay_first * first_ref[...] + (1.0 - decay_first) * gradient
    square_next = decay_second * second_ref[...] + (1.0 - decay_second) * gradient * gradient
    moment_ref[...] = moment_next
    square_ref[...] = square_next
    direction = (moment_next / (jnp.sqrt(square_next) + epsilon)).astype(jnp.bfloat16)
    for i in range(copies_ref.shape[0]):
        copies_ref[i] = direction


def expand(place_ref, block_hbm, mine_ref, other_ref, out_ref, block_ref, all_ref, sem):
    core = place_ref[0]
    copy = pltpu.make_async_copy(block_hbm, block_ref, sem)
    copy.start()
    all_ref[:, pl.ds(core, 1)] = mine_ref[...][:, None]
    all_ref[:, pl.ds(1 - core, 1)] = other_ref[...][:, None]
    direction = all_ref[...].reshape(block_ref.shape[1], out_ref.shape[1])
    copy.wait()
    out_ref[...] = jnp.dot(block_ref[...], direction, preferred_element_type=jnp.float32).astype(jnp.bfloat16)


def block_pairs(chips):
    pairs = []
    for p in range(chips):
        for k in range(chips):
            z = (k + p // 4 + 4 * ((p + k) % 4)) % chips
            pairs += [((p * 2 + c) * chips + k, (k * 2 + c) * chips + z) for c in range(2)]
    return pairs


def body(activations, cotangent, basis, first_moment, second_moment):
    chips = lax.axis_size("chip")
    features, rank = basis.shape
    tokens = activations.shape[0]
    half = rank // 2
    own_rows, columns = first_moment.shape
    core = lax.axis_index("core")
    place = core.astype(jnp.int32).reshape(1)
    f32, bf16 = jnp.float32, jnp.bfloat16

    rows = features // 2
    block = lax.dynamic_slice_in_dim(basis, core * rows, rows, 0)
    block = lax.ppermute(block, ("chip", "core", "fsdp"), block_pairs(chips))

    other_act = lax.ppermute(activations, "core", SWAP)
    other_cot = lax.ppermute(cotangent, "core", SWAP)
    partial, picked = pl.pallas_call(
        lambda *refs: project_own(own_rows, *refs),
        out_shape=(pltpu.HBM((2, half, tokens), f32), pltpu.VMEM((half, features), bf16)),
        in_specs=[IN_SMEM, IN_HBM, IN_HBM],
        out_specs=(IN_HBM, IN_VMEM),
        scratch_shapes=[
            pltpu.VMEM((features, rank), bf16),
            pltpu.VMEM((tokens, features), bf16),
            pltpu.VMEM((half, tokens), f32),
            pltpu.SemaphoreType.DMA((8,)),
        ],
        compiler_params=params(55 * 1024 * 1024),
        cost_estimate=cost(2 * rank * tokens * features, 5 << 20),
    )(place, basis, activations)
    partial = pl.pallas_call(
        project_other,
        out_shape=pltpu.HBM((2, half, tokens), f32),
        in_specs=[IN_VMEM, IN_VMEM, IN_HBM],
        out_specs=IN_HBM,
        scratch_shapes=[pltpu.VMEM((half, tokens), f32), pltpu.SemaphoreType.DMA((4,))],
        input_output_aliases={2: 0},
        compiler_params=params(),
        cost_estimate=cost(rank * tokens * features, 3 << 20),
    )(picked, other_act, partial)
    projected = lax.psum(partial, "fsdp").astype(bf16)

    terms = pl.pallas_call(
        grad_terms,
        out_shape=jax.ShapeDtypeStruct((half, columns), bf16),
        in_specs=[IN_VMEM, IN_VMEM, IN_HBM, IN_HBM],
        out_specs=IN_VMEM,
        scratch_shapes=[pltpu.VMEM((tokens, columns), bf16), pltpu.SemaphoreType.DMA((4,))],
        compiler_params=params(),
        cost_estimate=cost(2 * rank * tokens * columns, 5 << 20),
    )(projected, cotangent, other_cot, block)
    terms = lax.all_to_all(terms.reshape(chips, own_rows, columns), "chip", 0, 0, tiled=True)

    moment_next, square_next, copies = pl.pallas_call(
        adam,
        out_shape=(
            jax.ShapeDtypeStruct((own_rows, columns), f32),
            jax.ShapeDtypeStruct((own_rows, columns), f32),
            jax.ShapeDtypeStruct((chips, own_rows, columns), bf16),
        ),
        in_specs=[IN_VMEM] * 3,
        out_specs=(IN_VMEM,) * 3,
        compiler_params=params(),
        cost_estimate=cost(1 << 20, 2 << 20),
    )(terms, first_moment, second_moment)
    mine = lax.all_to_all(copies, "chip", 0, 0, tiled=True)
    other = lax.ppermute(mine, "core", SWAP)
    expanded = pl.pallas_call(
        expand,
        out_shape=jax.ShapeDtypeStruct((features // 2, columns), bf16),
        in_specs=[IN_SMEM, IN_HBM, IN_VMEM, IN_VMEM],
        out_specs=IN_VMEM,
        scratch_shapes=[
            pltpu.VMEM((rows, rank), bf16),
            pltpu.VMEM((chips, 2, own_rows, columns), bf16),
            pltpu.SemaphoreType.DMA,
        ],
        compiler_params=params(),
        cost_estimate=cost(features * rank * columns, 4 << 20),
    )(place, block, mine, other)
    return (moment_next, square_next, expanded)


def solution(mesh):
    devices = np.asarray(mesh.devices)
    inner = Mesh(devices.reshape(devices.shape[0] // 2, 2, devices.shape[1]), ("chip", "core", "fsdp"))
    split = P(("chip", "core"), "fsdp")
    in_specs = (split, split, P("fsdp", None), split, split)
    return jax.shard_map(body, mesh=inner, in_specs=in_specs, out_specs=(split, split, split), check_vma=False)
```

time: 164 us -> 179 us (1.091)
  blocking collectives: 129 us -> 142 us
  local copies, waits for them, and re-layouts: 0.03 us -> 1.9 us
    psum x1, blocking collectives: 96.7 us -> 104 us  [body(): projected = lax.psum(partial, 'fsdp').astype(bf16)]
    all_to_all x1, blocking collectives: 18.1 us -> 23.8 us  [body(): lax.all_to_all(terms.reshape(chips, own_rows, columns), 'chip', 0, 0, til...]
    dynamic_slice x0 -> x1, local copies, waits for them, and re-layouts: none -> 1.88 us  [body(): block = lax.dynamic_slice_in_dim(basis, core * rows, rows, 0)]
  transfers between devices with their start and end apart: 3 -> 4, of which waited for: 1 -> 1; matrix products, arithmetic and copies ran while one was open for 0% -> 1% of each run, Pallas kernels for 4% -> 3%
where the time goes in v3:
time: 179 us
  blocking collectives  142 us (79%)
  starting transfers between devices  20.5 us (11%)
  Pallas kernels  11.7 us (7%)
  waiting for transfers between devices  2.09 us (1%)
  local copies, waits for them, and re-layouts  1.9 us (1%)
    psum x1, blocking collectives, body(): projected = lax.psum(partial, 'fsdp').astype(bf16)  104 us
    all_to_all x1, blocking collectives, body(): lax.all_to_all(terms.reshape(chips, own_rows, columns), 'chip', 0, 0, til...  23.8 us
    all_to_all x1, blocking collectives, body(): mine = lax.all_to_all(copies, 'chip', 0, 0, tiled=True)  13.8 us
    ppermute x1, starting transfers between devices, body(): other_act = lax.ppermute(activations, 'core', SWAP)  8.79 us
    ppermute x1, starting transfers between devices, body(): other = lax.ppermute(mine, 'core', SWAP)  8.11 us
    pallas_call x1, Pallas kernels, body(): pl.pallas_call(lambda *refs: project_own(own_rows, *refs), out_shape=(plt...  3.91 us
  transfers between devices with their start and end apart: 4, of which 1 were waited for; matrix products, arithmetic and copies ran while one was open for 1% of the time, Pallas kernels for 3%

profile of v3, /device:TPU:1, one launch (start us, length us, event | category | flops | bytes accessed | tf_op | source)
XLA Modules:
  0.0 178.7 jit_solution(17549598079353244468)
XLA Ops:
  0.6 8.8 %collective-permute-start = (bf16[768,512]{1,0:T(8,128)(2,1)}, bf16[768,512]{1,0:T(8,128)(2,1)S(1)}, u32[]{:S(2)}, u32[]{:S(2)}) collective-permute-start(bf16[768,512]{1,0:T(8,128)(2,1)} %refs_2_.1), channel_id=1, source_target_pairs={{0,16},{16,0},{1,17},{17,1},{2,18},{18,2},{3,19},{19,3},{4,20},{20... | collective-permute-start | bytes 2359304 | tf_op jit(solution)/shard_map/ppermute | solution.py:129
  9.4 1.9 %collective-permute-start.1 = (bf16[768,896]{1,0:T(8,128)(2,1)}, bf16[768,896]{1,0:T(8,128)(2,1)}, u32[]{:S(2)}, u32[]{:S(2)}) collective-permute-start(bf16[768,896]{1,0:T(8,128)(2,1)} %own_ref.1), channel_id=1, source_target_pairs={{0,16},{16,0},{1,17},{17,1},{2,18},{18,2},{3,19},{19,3},{4,20},{20... | collective-permute-start | bytes 4128776 | tf_op jit(solution)/shard_map/ppermute | solution.py:130
  11.4 1.9 %constant_dynamic-slice_fusion = bf16[256,1024]{1,0:T(8,128)(2,1)} fusion(bf16[512,1024]{1,0:T(8,128)(2,1)} %refs_1_.1, s32[]{:T(128)S(6)} %select_n.3), kind=kLoop, calls=%fused_computation | loop fusion | bytes 1048580 | tf_op jit(solution)/shard_map/dynamic_slice | solution.py:126
  13.2 1.7 collective-permute-start.2
  14.9 3.9 %shard_map.76 = (f32[2,512,768]{2,1,0:T(8,128)}, bf16[512,512]{1,0:T(8,128)(2,1)S(1)}) custom-call(s32[1]{0:T(128)} %bitcast.refs_0_.place_ref, bf16[512,1024]{1,0:T(8,128)(2,1)} %refs_1_.1, bf16[768,512]{1,0:T(8,128)(2,1)} %refs_2_.1), custom_call_target="tpu_custom_call" | custom-call | flops 805306368 | bytes 5242880 | tf_op jit(solution)/shard_map/pallas_call | solution.py:131
  18.9 0.0 collective-permute-done.act_ref
  18.9 2.0 %shard_map.77 = f32[2,512,768]{2,1,0:T(8,128)} custom-call(bf16[512,512]{1,0:T(8,128)(2,1)S(1)} %get-tuple-element.8.picked_ref, bf16[768,512]{1,0:T(8,128)(2,1)S(1)} %collective-permute-done.act_ref, f32[2,512,768]{2,1,0:T(8,128)} %get-tuple-element.9._), custom_call_target="tpu_custom_call", output_to_operand_aliasing={{}: (2, {})} | custom-call | flops 402653184 | bytes 3145728 | tf_op jit(solution)/shard_map/pallas_call | solution.py:145
  20.8 0.0 copy-start
  20.8 104.1 %all-reduce.1.proj_ref = bf16[2,512,768]{2,1,0:T(8,128)(2,1)S(1)} all-reduce(f32[2,512,768]{2,1,0:T(8,128)} %shard_map.77), channel_id=1, replica_groups=mesh['chip'=16,'core'=2,'fsdp'=16] {'fsdp'}, use_global_device_ids=true, to_apply=%region_0.0 | all-reduce | flops 786432 | bytes 4718592 | tf_op jit(solution)/shard_map/psum | solution.py:155
  125.0 0.0 collective-permute-done.2._.block_hbm
  125.0 0.0 collective-permute-done.1.other_hbm
  125.0 0.0 copy-done
  125.0 3.1 %shard_map.78 = bf16[512,896]{1,0:T(8,128)(2,1)S(1)} custom-call(bf16[2,512,768]{2,1,0:T(8,128)(2,1)S(1)} %all-reduce.1.proj_ref, bf16[768,896]{1,0:T(8,128)(2,1)S(1)} %copy-done, bf16[768,896]{1,0:T(8,128)(2,1)} %collective-permute-done.1.other_hbm, bf16[256,1024]{1,0:T(8,128)(2,1)S(1)} %collective-permute-done.2._.block_hbm), custom_call_target="tpu_custom_call" | custom-call | flops 1409286144 | bytes 5242880 | tf_op jit(solution)/shard_map/pallas_call | solution.py:157
  128.1 0.0 copy-start.1
  128.1 0.0 copy-start.2
  128.1 23.8 %all_to_all.10.terms_ref = bf16[16,32,896]{2,1,0:T(8,128)(2,1)S(1)} all-to-all(bf16[16,32,896]{2,1,0:T(8,128)(2,1)S(1)} %bitcast.2), channel_id=1, replica_groups=mesh['chip'=16,'core'=2,'fsdp'=16] {'chip'}, dimensions={0} | all-to-all | bytes 1835008 | tf_op jit(solution)/shard_map/all_to_all | solution.py:166
  152.0 0.0 copy-done.1
  152.0 0.0 copy-done.2
  152.0 0.9 shard_map.79
  152.9 13.8 %all_to_all.11.mine_ref = bf16[16,32,896]{2,1,0:T(8,128)(2,1)S(1)} all-to-all(bf16[16,32,896]{2,1,0:T(8,128)(2,1)S(1)} %get-tuple-element.12), channel_id=1, replica_groups=mesh['chip'=16,'core'=2,'fsdp'=16] {'chip'}, dimensions={0} | all-to-all | bytes 1835008 | tf_op jit(solution)/shard_map/all_to_all | solution.py:180
  166.7 8.1 %collective-permute-start.3 = (bf16[16,32,896]{2,1,0:T(8,128)(2,1)S(1)}, bf16[16,32,896]{2,1,0:T(8,128)(2,1)S(1)}, u32[]{:S(2)}, u32[]{:S(2)}) collective-permute-start(bf16[16,32,896]{2,1,0:T(8,128)(2,1)S(1)} %all_to_all.11.mine_ref), channel_id=1, source_target_pairs={{0,16},{16,0},{1,17},{17,1},{2,18},{18,2},{3,19},{19,3},{4,20},{20... | collective-permute-start | bytes 2752520 | tf_op jit(solution)/shard_map/ppermute | solution.py:181
  174.8 2.1 %collective-permute-done.3.other_ref = bf16[16,32,896]{2,1,0:T(8,128)(2,1)S(1)} collective-permute-done((bf16[16,32,896]{2,1,0:T(8,128)(2,1)S(1)}, bf16[16,32,896]{2,1,0:T(8,128)(2,1)S(1)}, u32[]{:S(2)}, u32[]{:S(2)}) %collective-permute-start.3) | collective-permute-done | bytes 917536 | tf_op jit(solution)/shard_map/ppermute | solution.py:181
  176.9 1.8 %shard_map.80 = bf16[256,896]{1,0:T(8,128)(2,1)} custom-call(s32[1]{0:T(128)} %bitcast.refs_0_.place_ref, bf16[256,1024]{1,0:T(8,128)(2,1)S(1)} %collective-permute-done.2._.block_hbm, bf16[16,32,896]{2,1,0:T(8,128)(2,1)S(1)} %all_to_all.11.mine_ref, bf16[16,32,896]{2,1,0:T(8,128)(2,1)S(1)} %collective-permute-done.3.other_ref), custom_call_target="tpu_custom_call" | custom-call | flops 469762048 | bytes 4194304 | tf_op jit(solution)/shard_map/pallas_call | solution.py:182
Async XLA Ops:
  0.6 18.2 %collective-permute-start = (bf16[768,512]{1,0:T(8,128)(2,1)}, bf16[768,512]{1,0:T(8,128)(2,1)S(1)}, u32[]{:S(2)}, u32[]{:S(2)}) collective-permute-start(bf16[768,512]{1,0:T(8,128)(2,1)} %refs_2_.1), channel_id=1, source_target_pairs={{0,16},{16,0},{1,17},{17,1},{2,18},{18,2},{3,19},{19,3},{4,20},{20... | collective-permute-start | bytes 2359304 | tf_op jit(solution)/shard_map/ppermute | solution.py:129
  9.4 115.5 %collective-permute-start.1 = (bf16[768,896]{1,0:T(8,128)(2,1)}, bf16[768,896]{1,0:T(8,128)(2,1)}, u32[]{:S(2)}, u32[]{:S(2)}) collective-permute-start(bf16[768,896]{1,0:T(8,128)(2,1)} %own_ref.1), channel_id=1, source_target_pairs={{0,16},{16,0},{1,17},{17,1},{2,18},{18,2},{3,19},{19,3},{4,20},{20... | collective-permute-start | bytes 4128776 | tf_op jit(solution)/shard_map/ppermute | solution.py:130
  13.2 111.7 %collective-permute-start.2 = (bf16[256,1024]{1,0:T(8,128)(2,1)}, bf16[256,1024]{1,0:T(8,128)(2,1)S(1)}, u32[]{:S(2)}, u32[]{:S(2)}) collective-permute-start(bf16[256,1024]{1,0:T(8,128)(2,1)} %constant_dynamic-slice_fusion), channel_id=1, source_target_pairs={{0,0},{16,16},{1,37},{17,53},{2,74},{18,90},{3,111},{19,127},{4,13... | collective-permute-start | bytes 1572872 | tf_op jit(solution)/shard_map/ppermute | solution.py:127
  20.8 104.1 %copy-start = (bf16[768,896]{1,0:T(8,128)(2,1)S(1)}, bf16[768,896]{1,0:T(8,128)(2,1)}, u32[]{:S(2)}) copy-start(bf16[768,896]{1,0:T(8,128)(2,1)} %own_ref.1) | copy-start | bytes 4128772
  128.1 23.9 %copy-start.1 = (f32[32,896]{1,0:T(8,128)S(1)}, f32[32,896]{1,0:T(8,128)}, u32[]{:S(2)}) copy-start(f32[32,896]{1,0:T(8,128)} %first_ref.1) | copy-start | bytes 344068
  128.1 23.9 %copy-start.2 = (f32[32,896]{1,0:T(8,128)S(1)}, f32[32,896]{1,0:T(8,128)}, u32[]{:S(2)}) copy-start(f32[32,896]{1,0:T(8,128)} %second_ref.1) | copy-start | bytes 344068
  166.7 10.2 %collective-permute-start.3 = (bf16[16,32,896]{2,1,0:T(8,128)(2,1)S(1)}, bf16[16,32,896]{2,1,0:T(8,128)(2,1)S(1)}, u32[]{:S(2)}, u32[]{:S(2)}) collective-permute-start(bf16[16,32,896]{2,1,0:T(8,128)(2,1)S(1)} %all_to_all.11.mine_ref), channel_id=1, source_target_pairs={{0,16},{16,0},{1,17},{17,1},{2,18},{18,2},{3,19},{19,3},{4,20},{20... | collective-permute-start | bytes 2752520 | tf_op jit(solution)/shard_map/ppermute | solution.py:181

commit v4 on v2

v4 whole, which is shorter than its diff:
```python
import numpy as np
import jax
import jax.numpy as jnp
from jax import lax
from jax.experimental import pallas as pl
from jax.experimental.pallas import tpu as pltpu
from jax.sharding import Mesh, PartitionSpec as P

decay_first = 0.9
decay_second = 0.999
epsilon = 1e-08

SWAP = [(0, 1), (1, 0)]
VMEM_LIMIT = 40 * 1024 * 1024
LAST = (((1,), (1,)), ((), ()))
IN_VMEM = pl.BlockSpec(memory_space=pltpu.VMEM)
IN_HBM = pl.BlockSpec(memory_space=pltpu.HBM)
IN_SMEM = pl.BlockSpec(memory_space=pltpu.SMEM)


def params(limit=VMEM_LIMIT):
    return pltpu.CompilerParams(vmem_limit_bytes=limit)


def cost(flops, moved):
    return pl.CostEstimate(flops=flops, bytes_accessed=moved, transcendentals=0)


def project(own_rows, core_ref, holds_ref, basis_hbm, own_hbm, other_hbm, out_hbm, basis_ref, own_ref, other_ref, out_ref, sems):
    features, rank = basis_ref.shape
    tokens = own_ref.shape[0]
    half = rank // 2
    rows = features // 2
    load_basis = pltpu.make_async_copy(basis_hbm, basis_ref, sems.at[0])
    load_own = pltpu.make_async_copy(own_hbm, own_ref, sems.at[1])
    load_basis.start()
    load_own.start()
    load_other = pltpu.make_async_copy(other_hbm, other_ref, sems.at[2])
    load_other.start()
    at = lax.broadcasted_iota(jnp.int32, (half, rank), 0)
    wanted = at // own_rows * (2 * own_rows) + core_ref[0] * own_rows + at % own_rows
    pick = (lax.broadcasted_iota(jnp.int32, (half, rank), 1) == wanted).astype(jnp.bfloat16)
    load_basis.wait()
    picked = lax.dot_general(pick, basis_ref[...], LAST, preferred_element_type=jnp.float32).astype(jnp.bfloat16)
    saves = []

    def save(start, size):
        here = pl.ds(start, size)
        saves.append(pltpu.make_async_copy(out_ref.at[:, here], out_hbm.at[:, here], sems.at[3 + len(saves)]))
        saves[-1].start()

    load_own.wait()
    out_ref[:, :tokens] = lax.dot_general(picked, own_ref[...], LAST, preferred_element_type=jnp.float32)
    save(0, tokens)
    load_other.wait()
    out_ref[:, tokens : 2 * tokens] = lax.dot_general(picked, other_ref[...], LAST, preferred_element_type=jnp.float32)
    save(tokens, tokens)
    mine = basis_ref[pl.ds(pl.multiple_of(core_ref[0] * rows, rows), rows), :].astype(jnp.float32)
    mine = jnp.where(holds_ref[0] == 1, mine, 0.0)
    out_ref[:rows, 2 * tokens :] = mine[:, :half]
    out_ref[rows:, 2 * tokens :] = mine[:, half:]
    save(2 * tokens, half)
    for copy in saves:
        copy.wait()


def grad_terms(summed_ref, own_ref, other_hbm, out_ref, other_ref, sems):
    tokens = own_ref.shape[0]
    first = tokens // 3 * 2
    copies = []
    for i, (start, size) in enumerate(((0, first), (first, tokens - first))):
        rows = pl.ds(start, size)
        copies.append(pltpu.make_async_copy(other_hbm.at[rows, :], other_ref.at[rows, :], sems.at[i]))
        copies[i].start()
    total = jnp.dot(summed_ref[:, :tokens], own_ref[...], preferred_element_type=jnp.float32)
    copies[0].wait()
    total += jnp.dot(summed_ref[:, tokens : tokens + first], other_ref[:first, :], preferred_element_type=jnp.float32)
    copies[1].wait()
    total += jnp.dot(summed_ref[:, tokens + first : 2 * tokens], other_ref[first:, :], preferred_element_type=jnp.float32)
    out_ref[...] = total.astype(jnp.bfloat16)


def adam(terms_ref, first_ref, second_ref, moment_ref, square_ref, copies_ref):
    gradient = terms_ref[0].astype(jnp.float32)
    for i in range(1, terms_ref.shape[0]):
        gradient += terms_ref[i].astype(jnp.float32)
    moment_next = decay_first * first_ref[...] + (1.0 - decay_first) * gradient
    square_next = decay_second * second_ref[...] + (1.0 - decay_second) * gradient * gradient
    moment_ref[...] = moment_next
    square_ref[...] = square_next
    direction = (moment_next / (jnp.sqrt(square_next) + epsilon)).astype(jnp.bfloat16)
    for i in range(copies_ref.shape[0]):
        copies_ref[i] = direction


def expand(core_ref, summed_ref, mine_ref, other_ref, out_ref, all_ref):
    rows, columns = out_ref.shape
    half = summed_ref.shape[0]
    start = summed_ref.shape[1] - half
    core = core_ref[0]
    all_ref[:, pl.ds(core, 1)] = mine_ref[...][:, None]
    all_ref[:, pl.ds(1 - core, 1)] = other_ref[...][:, None]
    direction = all_ref[...].reshape(2 * half, columns)
    total = jnp.dot(summed_ref[:rows, start:], direction[:half], preferred_element_type=jnp.float32)
    total += jnp.dot(summed_ref[rows:, start:], direction[half:], preferred_element_type=jnp.float32)
    out_ref[...] = total.astype(jnp.bfloat16)


def body(activations, cotangent, basis, first_moment, second_moment):
    chips = lax.axis_size("chip")
    features, rank = basis.shape
    tokens = activations.shape[0]
    half = rank // 2
    own_rows, columns = first_moment.shape
    core = lax.axis_index("core").astype(jnp.int32).reshape(1)
    holds = (lax.axis_index("chip") == lax.axis_index("fsdp")).astype(jnp.int32).reshape(1)
    f32, bf16 = jnp.float32, jnp.bfloat16

    other_act = lax.ppermute(activations, "core", SWAP)
    other_cot = lax.ppermute(cotangent, "core", SWAP)
    partial = pl.pallas_call(
        lambda *refs: project(own_rows, *refs),
        out_shape=pltpu.HBM((half, 2 * tokens + half), f32),
        in_specs=[IN_SMEM, IN_SMEM, IN_HBM, IN_HBM, IN_HBM],
        out_specs=IN_HBM,
        scratch_shapes=[
            pltpu.VMEM((features, rank), bf16),
            pltpu.VMEM((tokens, features), bf16),
            pltpu.VMEM((tokens, features), bf16),
            pltpu.VMEM((half, 2 * tokens + half), f32),
            pltpu.SemaphoreType.DMA((6,)),
        ],
        compiler_params=params(55 * 1024 * 1024),
        cost_estimate=cost(3 * rank * tokens * features, 7 << 20),
    )(core, holds, basis, activations, other_act)
    summed = lax.psum(partial, "fsdp").astype(bf16)

    terms = pl.pallas_call(
        grad_terms,
        out_shape=jax.ShapeDtypeStruct((half, columns), bf16),
        in_specs=[IN_VMEM, IN_VMEM, IN_HBM],
        out_specs=IN_VMEM,
        scratch_shapes=[pltpu.VMEM((tokens, columns), bf16), pltpu.SemaphoreType.DMA((2,))],
        compiler_params=params(),
        cost_estimate=cost(2 * rank * tokens * columns, 5 << 20),
    )(summed, cotangent, other_cot)
    terms = lax.all_to_all(terms.reshape(chips, own_rows, columns), "chip", 0, 0, tiled=True)

    moment_next, square_next, copies = pl.pallas_call(
        adam,
        out_shape=(
            jax.ShapeDtypeStruct((own_rows, columns), f32),
            jax.ShapeDtypeStruct((own_rows, columns), f32),
            jax.ShapeDtypeStruct((chips, own_rows, columns), bf16),
        ),
        in_specs=[IN_VMEM] * 3,
        out_specs=(IN_VMEM,) * 3,
        compiler_params=params(),
        cost_estimate=cost(1 << 20, 2 << 20),
    )(terms, first_moment, second_moment)
    mine = lax.all_to_all(copies, "chip", 0, 0, tiled=True)
    other = lax.ppermute(mine, "core", SWAP)
    expanded = pl.pallas_call(
        expand,
        out_shape=jax.ShapeDtypeStruct((features // 2, columns), bf16),
        in_specs=[IN_SMEM, IN_VMEM, IN_VMEM, IN_VMEM],
        out_specs=IN_VMEM,
        scratch_shapes=[pltpu.VMEM((chips, 2, own_rows, columns), bf16)],
        compiler_params=params(),
        cost_estimate=cost(features * rank * columns, 4 << 20),
    )(core, summed, mine, other)
    return (moment_next, square_next, expanded)


def solution(mesh):
    devices = np.asarray(mesh.devices)
    inner = Mesh(devices.reshape(devices.shape[0] // 2, 2, devices.shape[1]), ("chip", "core", "fsdp"))
    split = P(("chip", "core"), "fsdp")
    in_specs = (split, split, P("fsdp", None), split, split)
    return jax.shard_map(body, mesh=inner, in_specs=in_specs, out_specs=(split, split, split), check_vma=False)
```

time: 164 us -> 163 us (level)
  Pallas kernels: 12.9 us -> 10.7 us
    pallas_call x2 -> x1, Pallas kernels: 6.52 us -> 5.07 us  [body(): pl.pallas_call(lambda *refs: project(own_rows, *refs), out_shape=pltpu.HB...]
  transfers between devices with their start and end apart: 3 -> 3, of which waited for: 1 -> 2; matrix products, arithmetic and copies ran while one was open for 0% -> 0% of each run, Pallas kernels for 4% -> 3%
where the time goes in v4:
time: 163 us
  blocking collectives  129 us (79%)
  starting transfers between devices  18.9 us (12%)
  Pallas kernels  10.7 us (7%)
  waiting for transfers between devices  2.24 us (1%)
    psum x1, blocking collectives, body(): summed = lax.psum(partial, 'fsdp').astype(bf16)  97 us
    all_to_all x1, blocking collectives, body(): lax.all_to_all(terms.reshape(chips, own_rows, columns), 'chip', 0, 0, til...  18.3 us
    all_to_all x1, blocking collectives, body(): mine = lax.all_to_all(copies, 'chip', 0, 0, tiled=True)  13.8 us
    ppermute x1, starting transfers between devices, body(): other_act = lax.ppermute(activations, 'core', SWAP)  8.79 us
    ppermute x1, starting transfers between devices, body(): other = lax.ppermute(mine, 'core', SWAP)  8.15 us
    pallas_call x1, Pallas kernels, body(): pl.pallas_call(lambda *refs: project(own_rows, *refs), out_shape=pltpu.HB...  5.07 us
  transfers between devices with their start and end apart: 3, of which 2 were waited for; matrix products, arithmetic and copies ran while one was open for 0% of the time, Pallas kernels for 3%

profile of v4, /device:TPU:1, one launch (start us, length us, event | category | flops | bytes accessed | tf_op | source)
XLA Modules:
  0.0 162.5 jit_solution(18393092659981569074)
XLA Ops:
  0.6 8.8 %collective-permute-start = (bf16[768,512]{1,0:T(8,128)(2,1)}, bf16[768,512]{1,0:T(8,128)(2,1)S(1)}, u32[]{:S(2)}, u32[]{:S(2)}) collective-permute-start(bf16[768,512]{1,0:T(8,128)(2,1)} %refs_3_.1), channel_id=1, source_target_pairs={{0,16},{16,0},{1,17},{17,1},{2,18},{18,2},{3,19},{19,3},{4,20},{20... | collective-permute-start | bytes 2359304 | tf_op jit(solution)/shard_map/ppermute | solution.py:119
  9.4 1.9 %collective-permute-start.1 = (bf16[768,896]{1,0:T(8,128)(2,1)}, bf16[768,896]{1,0:T(8,128)(2,1)}, u32[]{:S(2)}, u32[]{:S(2)}) collective-permute-start(bf16[768,896]{1,0:T(8,128)(2,1)} %own_ref.1), channel_id=1, source_target_pairs={{0,16},{16,0},{1,17},{17,1},{2,18},{18,2},{3,19},{19,3},{4,20},{20... | collective-permute-start | bytes 4128776 | tf_op jit(solution)/shard_map/ppermute | solution.py:120
  11.4 0.2 collective-permute-done.refs_4_
  11.5 0.0 copy-start.3
  11.5 0.9 copy-done.3
  12.4 5.1 %shard_map.76 = f32[512,2048]{1,0:T(8,128)} custom-call(s32[1]{0:T(128)} %bitcast.refs_0_.core_ref, s32[1]{0:T(128)} %bitcast.1.refs_1_, bf16[512,1024]{1,0:T(8,128)(2,1)} %refs_2_.1, bf16[768,512]{1,0:T(8,128)(2,1)} %refs_3_.1, bf16[768,512]{1,0:T(8,128)(2,1)} %copy-done.3), custom_call_target="tpu_custom_call" | custom-call | flops 1207959552 | bytes 7340032 | tf_op jit(solution)/shard_map/pallas_call | solution.py:121
  17.5 0.0 copy-start
  17.5 97.0 %all-reduce.1.summed_ref = bf16[512,2048]{1,0:T(8,128)(2,1)S(1)} all-reduce(f32[512,2048]{1,0:T(8,128)} %shard_map.76), channel_id=1, replica_groups=mesh['chip'=16,'core'=2,'fsdp'=16] {'fsdp'}, use_global_device_ids=true, to_apply=%region_0.0 | all-reduce | flops 1048576 | bytes 6291456 | tf_op jit(solution)/shard_map/psum | solution.py:136
  114.5 0.0 copy-start.1
  114.5 0.0 copy-start.2
  114.5 0.0 collective-permute-done.1.other_hbm
  114.5 0.0 copy-done
  114.5 3.1 %shard_map.77 = bf16[512,896]{1,0:T(8,128)(2,1)S(1)} custom-call(bf16[512,2048]{1,0:T(8,128)(2,1)S(1)} %all-reduce.1.summed_ref, bf16[768,896]{1,0:T(8,128)(2,1)S(1)} %copy-done, bf16[768,896]{1,0:T(8,128)(2,1)} %collective-permute-done.1.other_hbm), custom_call_target="tpu_custom_call" | custom-call | flops 1409286144 | bytes 5242880 | tf_op jit(solution)/shard_map/pallas_call | solution.py:138
  117.7 18.3 %all_to_all.10.terms_ref = bf16[16,32,896]{2,1,0:T(8,128)(2,1)S(1)} all-to-all(bf16[16,32,896]{2,1,0:T(8,128)(2,1)S(1)} %bitcast.3), channel_id=1, replica_groups=mesh['chip'=16,'core'=2,'fsdp'=16] {'chip'}, dimensions={0} | all-to-all | bytes 1835008 | tf_op jit(solution)/shard_map/all_to_all | solution.py:147
  136.0 0.0 copy-done.1
  136.0 0.0 copy-done.2
  136.0 0.9 shard_map.78
  136.9 13.8 %all_to_all.11.mine_ref = bf16[16,32,896]{2,1,0:T(8,128)(2,1)S(1)} all-to-all(bf16[16,32,896]{2,1,0:T(8,128)(2,1)S(1)} %get-tuple-element.8), channel_id=1, replica_groups=mesh['chip'=16,'core'=2,'fsdp'=16] {'chip'}, dimensions={0} | all-to-all | bytes 1835008 | tf_op jit(solution)/shard_map/all_to_all | solution.py:161
  150.7 8.2 %collective-permute-start.2 = (bf16[16,32,896]{2,1,0:T(8,128)(2,1)S(1)}, bf16[16,32,896]{2,1,0:T(8,128)(2,1)S(1)}, u32[]{:S(2)}, u32[]{:S(2)}) collective-permute-start(bf16[16,32,896]{2,1,0:T(8,128)(2,1)S(1)} %all_to_all.11.mine_ref), channel_id=1, source_target_pairs={{0,16},{16,0},{1,17},{17,1},{2,18},{18,2},{3,19},{19,3},{4,20},{20... | collective-permute-start | bytes 2752520 | tf_op jit(solution)/shard_map/ppermute | solution.py:162
  158.8 2.1 %collective-permute-done.2.other_ref = bf16[16,32,896]{2,1,0:T(8,128)(2,1)S(1)} collective-permute-done((bf16[16,32,896]{2,1,0:T(8,128)(2,1)S(1)}, bf16[16,32,896]{2,1,0:T(8,128)(2,1)S(1)}, u32[]{:S(2)}, u32[]{:S(2)}) %collective-permute-start.2) | collective-permute-done | bytes 917536 | tf_op jit(solution)/shard_map/ppermute | solution.py:162
  160.9 1.6 shard_map.79
Async XLA Ops:
  0.6 10.9 %collective-permute-start = (bf16[768,512]{1,0:T(8,128)(2,1)}, bf16[768,512]{1,0:T(8,128)(2,1)S(1)}, u32[]{:S(2)}, u32[]{:S(2)}) collective-permute-start(bf16[768,512]{1,0:T(8,128)(2,1)} %refs_3_.1), channel_id=1, source_target_pairs={{0,16},{16,0},{1,17},{17,1},{2,18},{18,2},{3,19},{19,3},{4,20},{20... | collective-permute-start | bytes 2359304 | tf_op jit(solution)/shard_map/ppermute | solution.py:119
  9.4 105.1 %collective-permute-start.1 = (bf16[768,896]{1,0:T(8,128)(2,1)}, bf16[768,896]{1,0:T(8,128)(2,1)}, u32[]{:S(2)}, u32[]{:S(2)}) collective-permute-start(bf16[768,896]{1,0:T(8,128)(2,1)} %own_ref.1), channel_id=1, source_target_pairs={{0,16},{16,0},{1,17},{17,1},{2,18},{18,2},{3,19},{19,3},{4,20},{20... | collective-permute-start | bytes 4128776 | tf_op jit(solution)/shard_map/ppermute | solution.py:120
  11.5 0.9 copy-start.3
  17.5 97.1 %copy-start = (bf16[768,896]{1,0:T(8,128)(2,1)S(1)}, bf16[768,896]{1,0:T(8,128)(2,1)}, u32[]{:S(2)}) copy-start(bf16[768,896]{1,0:T(8,128)(2,1)} %own_ref.1) | copy-start | bytes 4128772
  114.5 21.5 %copy-start.1 = (f32[32,896]{1,0:T(8,128)S(1)}, f32[32,896]{1,0:T(8,128)}, u32[]{:S(2)}) copy-start(f32[32,896]{1,0:T(8,128)} %first_ref.1) | copy-start | bytes 344068
  114.5 21.5 %copy-start.2 = (f32[32,896]{1,0:T(8,128)S(1)}, f32[32,896]{1,0:T(8,128)}, u32[]{:S(2)}) copy-start(f32[32,896]{1,0:T(8,128)} %second_ref.1) | copy-start | bytes 344068
  150.7 10.2 %collective-permute-start.2 = (bf16[16,32,896]{2,1,0:T(8,128)(2,1)S(1)}, bf16[16,32,896]{2,1,0:T(8,128)(2,1)S(1)}, u32[]{:S(2)}, u32[]{:S(2)}) collective-permute-start(bf16[16,32,896]{2,1,0:T(8,128)(2,1)S(1)} %all_to_all.11.mine_ref), channel_id=1, source_target_pairs={{0,16},{16,0},{1,17},{17,1},{2,18},{18,2},{3,19},{19,3},{4,20},{20... | collective-permute-start | bytes 2752520 | tf_op jit(solution)/shard_map/ppermute | solution.py:162

commit v5 on v4

v5 whole, which is shorter than its diff:
```python
import numpy as np
import jax
import jax.numpy as jnp
from jax import lax
from jax.experimental import pallas as pl
from jax.experimental.pallas import tpu as pltpu
from jax.sharding import Mesh, PartitionSpec as P

decay_first = 0.9
decay_second = 0.999
epsilon = 1e-08

SWAP = [(0, 1), (1, 0)]
VMEM_LIMIT = 40 * 1024 * 1024
LAST = (((1,), (1,)), ((), ()))
IN_VMEM = pl.BlockSpec(memory_space=pltpu.VMEM)
IN_HBM = pl.BlockSpec(memory_space=pltpu.HBM)
IN_SMEM = pl.BlockSpec(memory_space=pltpu.SMEM)


def params(limit=VMEM_LIMIT):
    return pltpu.CompilerParams(vmem_limit_bytes=limit)


def cost(flops, moved):
    return pl.CostEstimate(flops=flops, bytes_accessed=moved, transcendentals=0)


def project(own_rows, core_ref, holds_ref, basis_hbm, own_hbm, other_hbm, out_hbm, rest_hbm, basis_ref, own_ref, other_ref, out_ref, sems):
    features, rank = basis_ref.shape
    tokens = own_ref.shape[0]
    half = rank // 2
    rows = features // 4
    parts = half // rows
    wide = rank // parts
    load_basis = pltpu.make_async_copy(basis_hbm, basis_ref, sems.at[0])
    load_own = pltpu.make_async_copy(own_hbm, own_ref, sems.at[1])
    load_basis.start()
    load_own.start()
    load_other = pltpu.make_async_copy(other_hbm, other_ref, sems.at[2])
    load_other.start()
    at = lax.broadcasted_iota(jnp.int32, (half, rank), 0)
    wanted = at // own_rows * (2 * own_rows) + core_ref[0] * own_rows + at % own_rows
    pick = (lax.broadcasted_iota(jnp.int32, (half, rank), 1) == wanted).astype(jnp.bfloat16)
    load_basis.wait()
    picked = lax.dot_general(pick, basis_ref[...], LAST, preferred_element_type=jnp.float32).astype(jnp.bfloat16)
    saves = []

    def save(start, size):
        here = pl.ds(start, size)
        saves.append(pltpu.make_async_copy(out_ref.at[:, here], out_hbm.at[:, here], sems.at[3 + len(saves)]))
        saves[-1].start()

    load_own.wait()
    out_ref[:, :tokens] = lax.dot_general(picked, own_ref[...], LAST, preferred_element_type=jnp.float32)
    save(0, tokens)
    load_other.wait()
    out_ref[:, tokens : 2 * tokens] = lax.dot_general(picked, other_ref[...], LAST, preferred_element_type=jnp.float32)
    save(tokens, tokens)
    mine = basis_ref[pl.ds(pl.multiple_of(core_ref[0] * (2 * rows), rows), rows), :].astype(jnp.float32)
    mine = jnp.where(holds_ref[0] == 1, mine, 0.0)
    for i in range(parts):
        out_ref[i * rows : (i + 1) * rows, 2 * tokens :] = mine[:, i * wide : (i + 1) * wide]
    save(2 * tokens, wide)
    rest = pl.ds(pl.multiple_of((2 * core_ref[0] + 1) * rows, rows), rows)
    saves.append(pltpu.make_async_copy(basis_ref.at[rest, :], rest_hbm, sems.at[6]))
    saves[-1].start()
    for copy in saves:
        copy.wait()


def grad_terms(summed_ref, own_ref, other_hbm, _, out_hbm, rest_hbm, other_ref, total_ref, out_ref, sems):
    tokens = own_ref.shape[0]
    first = tokens // 3 * 2
    loads = []
    for i, (start, size) in enumerate(((0, first), (first, tokens - first))):
        rows = pl.ds(start, size)
        loads.append(pltpu.make_async_copy(other_hbm.at[rows, :], other_ref.at[rows, :], sems.at[i]))
        loads[i].start()
    total_ref[...] = jnp.dot(summed_ref[:, :tokens], own_ref[...], preferred_element_type=jnp.float32)
    for load in loads:
        load.wait()
    part = out_ref.shape[0] // 2
    saves = []
    for i in range(2):
        rows = pl.ds(i * part, part)
        more = jnp.dot(summed_ref[rows, tokens : 2 * tokens], other_ref[...], preferred_element_type=jnp.float32)
        out_ref[rows, :] = (total_ref[rows, :] + more).astype(jnp.bfloat16)
        saves.append(pltpu.make_async_copy(out_ref.at[rows, :], out_hbm.at[rows, :], sems.at[2 + i]))
        saves[i].start()
    for save in saves:
        save.wait()


def adam(terms_ref, first_ref, second_ref, _, moment_ref, square_ref, copies_ref):
    gradient = terms_ref[0].astype(jnp.float32)
    for i in range(1, terms_ref.shape[0]):
        gradient += terms_ref[i].astype(jnp.float32)
    moment_next = decay_first * first_ref[...] + (1.0 - decay_first) * gradient
    square_next = decay_second * second_ref[...] + (1.0 - decay_second) * gradient * gradient
    moment_ref[...] = moment_next
    square_ref[...] = square_next
    direction = (moment_next / (jnp.sqrt(square_next) + epsilon)).astype(jnp.bfloat16)
    for i in range(copies_ref.shape[0]):
        copies_ref[i] = direction


def expand(core_ref, summed_ref, rest_ref, mine_ref, other_ref, out_ref, block_ref, all_ref):
    rows = rest_ref.shape[0]
    rank = block_ref.shape[1]
    parts = summed_ref.shape[0] // rows
    wide = rank // parts
    start = summed_ref.shape[1] - wide
    core = core_ref[0]
    for i in range(parts):
        block_ref[:rows, i * wide : (i + 1) * wide] = summed_ref[i * rows : (i + 1) * rows, start:]
    block_ref[rows:, :] = rest_ref[...]
    all_ref[:, pl.ds(core, 1)] = mine_ref[...][:, None]
    all_ref[:, pl.ds(1 - core, 1)] = other_ref[...][:, None]
    direction = all_ref[...].reshape(rank, out_ref.shape[1])
    out_ref[...] = jnp.dot(block_ref[...], direction, preferred_element_type=jnp.float32).astype(jnp.bfloat16)


def block_pairs(chips):
    pairs = []
    for p in range(chips):
        for k in range(chips):
            z = (k + p // 4 + 4 * ((p + k) % 4)) % chips
            pairs += [((p * 2 + c) * chips + k, (k * 2 + c) * chips + z) for c in range(2)]
    return pairs


def body(activations, cotangent, basis, first_moment, second_moment):
    chips = lax.axis_size("chip")
    features, rank = basis.shape
    tokens = activations.shape[0]
    half = rank // 2
    rows = features // 4
    width = 2 * tokens + rank * rows // half
    own_rows, columns = first_moment.shape
    core = lax.axis_index("core").astype(jnp.int32).reshape(1)
    holds = (lax.axis_index("chip") == lax.axis_index("fsdp")).astype(jnp.int32).reshape(1)
    f32, bf16 = jnp.float32, jnp.bfloat16

    other_act = lax.ppermute(activations, "core", SWAP)
    other_cot = lax.ppermute(cotangent, "core", SWAP)
    partial, rest = pl.pallas_call(
        lambda *refs: project(own_rows, *refs),
        out_shape=(pltpu.HBM((half, width), f32), pltpu.HBM((rows, rank), bf16)),
        in_specs=[IN_SMEM, IN_SMEM, IN_HBM, IN_HBM, IN_HBM],
        out_specs=(IN_HBM, IN_HBM),
        scratch_shapes=[
            pltpu.VMEM((features, rank), bf16),
            pltpu.VMEM((tokens, features), bf16),
            pltpu.VMEM((tokens, features), bf16),
            pltpu.VMEM((half, width), f32),
            pltpu.SemaphoreType.DMA((7,)),
        ],
        compiler_params=params(55 * 1024 * 1024),
        cost_estimate=cost(3 * rank * tokens * features, 7 << 20),
    )(core, holds, basis, activations, other_act)
    summed = lax.psum(partial, "fsdp").astype(bf16)

    terms, rest = pl.pallas_call(
        grad_terms,
        out_shape=(pltpu.HBM((half, columns), bf16), pltpu.HBM((rows, rank), bf16)),
        in_specs=[IN_VMEM, IN_VMEM, IN_HBM, IN_HBM],
        out_specs=(IN_HBM, IN_HBM),
        input_output_aliases={3: 1},
        scratch_shapes=[
            pltpu.VMEM((tokens, columns), bf16),
            pltpu.VMEM((half, columns), f32),
            pltpu.VMEM((half, columns), bf16),
            pltpu.SemaphoreType.DMA((4,)),
        ],
        compiler_params=params(),
        cost_estimate=cost(2 * rank * tokens * columns, 5 << 20),
    )(summed, cotangent, other_cot, rest)
    rest = lax.ppermute(rest, ("chip", "core", "fsdp"), block_pairs(chips))
    terms = lax.all_to_all(terms.reshape(chips, own_rows, columns), "chip", 0, 0, tiled=True)

    moment_next, square_next, copies = pl.pallas_call(
        adam,
        out_shape=(
            jax.ShapeDtypeStruct((own_rows, columns), f32),
            jax.ShapeDtypeStruct((own_rows, columns), f32),
            jax.ShapeDtypeStruct((chips, own_rows, columns), bf16),
        ),
        in_specs=[IN_VMEM] * 3 + [IN_HBM],
        out_specs=(IN_VMEM,) * 3,
        compiler_params=params(),
        cost_estimate=cost(1 << 20, 2 << 20),
    )(terms, first_moment, second_moment, rest)
    mine = lax.all_to_all(copies, "chip", 0, 0, tiled=True)
    other = lax.ppermute(mine, "core", SWAP)
    expanded = pl.pallas_call(
        expand,
        out_shape=jax.ShapeDtypeStruct((features // 2, columns), bf16),
        in_specs=[IN_SMEM] + [IN_VMEM] * 4,
        out_specs=IN_VMEM,
        scratch_shapes=[pltpu.VMEM((2 * rows, rank), bf16), pltpu.VMEM((chips, 2, own_rows, columns), bf16)],
        compiler_params=params(),
        cost_estimate=cost(features * rank * columns, 4 << 20),
    )(core, summed, rest, mine, other)
    return (moment_next, square_next, expanded)


def solution(mesh):
    devices = np.asarray(mesh.devices)
    inner = Mesh(devices.reshape(devices.shape[0] // 2, 2, devices.shape[1]), ("chip", "core", "fsdp"))
    split = P(("chip", "core"), "fsdp")
    in_specs = (split, split, P("fsdp", None), split, split)
    return jax.shard_map(body, mesh=inner, in_specs=in_specs, out_specs=(split, split, split), check_vma=False)
```

time: 163 us -> 173 us (1.061)
  waiting for transfers between devices: 2.24 us -> 13.3 us
  blocking collectives: 129 us -> 123 us
  starting transfers between devices: 18.9 us -> 24.1 us
    all_to_all x1, blocking collectives: 13.8 us -> 37.5 us  [body(): mine = lax.all_to_all(copies, 'chip', 0, 0, tiled=True)]
    all_to_all x1 -> x0, blocking collectives: 18.3 us -> none  [body(): lax.all_to_all(terms.reshape(chips, own_rows, columns), 'chip', 0, 0, til...]
    psum x1, blocking collectives: 97 us -> 85.4 us  [body(): summed = lax.psum(partial, 'fsdp').astype(bf16)]
    all_to_all x0 -> x1, waiting for transfers between devices: none -> 11.1 us  [body(): lax.all_to_all(terms.reshape(chips, own_rows, columns), 'chip', 0, 0, til...]
    all_to_all x0 -> x1, starting transfers between devices: none -> 6.9 us  [body(): lax.all_to_all(terms.reshape(chips, own_rows, columns), 'chip', 0, 0, til...]
    ppermute x1, starting transfers between devices: 8.15 us -> 5.8 us  [body(): other = lax.ppermute(mine, 'core', SWAP)]
  transfers between devices with their start and end apart: 3 -> 5, of which waited for: 2 -> 3; matrix products, arithmetic and copies ran while one was open for 0% -> 0% of each run, Pallas kernels for 3% -> 3%
where the time goes in v5:
time: 173 us
  blocking collectives  123 us (71%)
  starting transfers between devices  24.1 us (14%)
  waiting for transfers between devices  13.3 us (8%)
  Pallas kernels  10.5 us (6%)
    psum x1, blocking collectives, body(): summed = lax.psum(partial, 'fsdp').astype(bf16)  85.4 us
    all_to_all x1, blocking collectives, body(): mine = lax.all_to_all(copies, 'chip', 0, 0, tiled=True)  37.5 us
    all_to_all x1, waiting for transfers between devices, body(): lax.all_to_all(terms.reshape(chips, own_rows, columns), 'chip', 0, 0, til...  11.1 us
    ppermute x1, starting transfers between devices, body(): other_act = lax.ppermute(activations, 'core', SWAP)  8.79 us
    all_to_all x1, starting transfers between devices, body(): lax.all_to_all(terms.reshape(chips, own_rows, columns), 'chip', 0, 0, til...  6.9 us
    ppermute x1, starting transfers between devices, body(): other = lax.ppermute(mine, 'core', SWAP)  5.8 us
    pallas_call x1, Pallas kernels, body(): pl.pallas_call(lambda *refs: project(own_rows, *refs), out_shape=(pltpu.H...  4.89 us
  transfers between devices with their start and end apart: 5, of which 3 were waited for; matrix products, arithmetic and copies ran while one was open for 0% of the time, Pallas kernels for 3%

profile of v5, /device:TPU:1, one launch (start us, length us, event | category | flops | bytes accessed | tf_op | source)
XLA Modules:
  0.0 172.5 jit_solution(11567398392983119835)
XLA Ops:
  0.6 8.8 %collective-permute-start = (bf16[768,512]{1,0:T(8,128)(2,1)}, bf16[768,512]{1,0:T(8,128)(2,1)S(1)}, u32[]{:S(2)}, u32[]{:S(2)}) collective-permute-start(bf16[768,512]{1,0:T(8,128)(2,1)} %refs_3_.1), channel_id=1, source_target_pairs={{0,16},{16,0},{1,17},{17,1},{2,18},{18,2},{3,19},{19,3},{4,20},{20... | collective-permute-start | bytes 2359304 | tf_op jit(solution)/shard_map/ppermute | solution.py:145
  9.4 1.9 %collective-permute-start.1 = (bf16[768,896]{1,0:T(8,128)(2,1)}, bf16[768,896]{1,0:T(8,128)(2,1)}, u32[]{:S(2)}, u32[]{:S(2)}) collective-permute-start(bf16[768,896]{1,0:T(8,128)(2,1)} %own_ref.1), channel_id=1, source_target_pairs={{0,16},{16,0},{1,17},{17,1},{2,18},{18,2},{3,19},{19,3},{4,20},{20... | collective-permute-start | bytes 4128776 | tf_op jit(solution)/shard_map/ppermute | solution.py:146
  11.4 0.2 collective-permute-done.refs_4_
  11.5 0.0 copy-start.3
  11.5 0.9 copy-done.3
  12.4 4.9 %shard_map.76 = (f32[512,1792]{1,0:T(8,128)}, bf16[128,1024]{1,0:T(8,128)(2,1)}) custom-call(s32[1]{0:T(128)} %bitcast.refs_0_.core_ref, s32[1]{0:T(128)} %bitcast.1.refs_1_, bf16[512,1024]{1,0:T(8,128)(2,1)} %refs_2_.1, bf16[768,512]{1,0:T(8,128)(2,1)} %refs_3_.1, bf16[768,512]{1,0:T(8,128)(2,1)} %copy-done.3), custom_call_target="tpu_custom_call" | custom-call | flops 1207959552 | bytes 7340032 | tf_op jit(solution)/shard_map/pallas_call | solution.py:147
  17.3 0.0 copy-start.2
  17.3 85.4 %all-reduce.1.summed_ref = bf16[512,1792]{1,0:T(8,128)(2,1)S(1)} all-reduce(f32[512,1792]{1,0:T(8,128)} %get-tuple-element.10), channel_id=1, replica_groups=mesh['chip'=16,'core'=2,'fsdp'=16] {'fsdp'}, use_global_device_ids=true, to_apply=%region_0.0 | all-reduce | flops 917504 | bytes 5505024 | tf_op jit(solution)/shard_map/psum | solution.py:162
  102.8 0.0 collective-permute-done.1.other_hbm
  102.8 0.0 copy-done.2
  102.8 3.1 %shard_map.77 = (bf16[512,896]{1,0:T(8,128)(2,1)}, bf16[128,1024]{1,0:T(8,128)(2,1)}) custom-call(bf16[512,1792]{1,0:T(8,128)(2,1)S(1)} %all-reduce.1.summed_ref, bf16[768,896]{1,0:T(8,128)(2,1)S(1)} %copy-done.2, bf16[768,896]{1,0:T(8,128)(2,1)} %collective-permute-done.1.other_hbm, ...), custom_call_target="tpu_custom_call", output_to_operand_aliasing={{1}: (3, {})} | custom-call | flops 1409286144 | bytes 5242880 | tf_op jit(solution)/shard_map/pallas_call | solution.py:164
  105.9 0.0 copy-start.4
  105.9 0.0 copy-start
  105.9 0.0 copy-start.1
  106.0 6.9 %all-to-all-start = ((bf16[16,32,896]{2,1,0:T(8,128)(2,1)}), bf16[16,32,896]{2,1,0:T(8,128)(2,1)S(1)}, u32[]{:S(2)}, u32[]{:S(2)}) async-start(bf16[16,32,896]{2,1,0:T(8,128)(2,1)} %bitcast.3), calls=%async_computation | async-start | bytes 1835008 | tf_op jit(solution)/shard_map/all_to_all | solution.py:180
  112.9 0.0 copy-done.4
  112.9 0.7 collective-permute-start.2
  113.6 0.0 collective-permute-done.2._.rest_ref
  113.6 11.1 %all-to-all-done.terms_ref = bf16[16,32,896]{2,1,0:T(8,128)(2,1)S(1)} async-done(((bf16[16,32,896]{2,1,0:T(8,128)(2,1)}), bf16[16,32,896]{2,1,0:T(8,128)(2,1)S(1)}, u32[]{:S(2)}, u32[]{:S(2)}) %all-to-all-start) | async-done | bytes 917536 | tf_op jit(solution)/shard_map/all_to_all | solution.py:180
  124.6 0.0 copy-done
  124.6 0.0 copy-done.1
  124.6 0.9 shard_map.78
  125.5 37.5 %all_to_all.10.mine_ref = bf16[16,32,896]{2,1,0:T(8,128)(2,1)S(1)} all-to-all(bf16[16,32,896]{2,1,0:T(8,128)(2,1)S(1)} %get-tuple-element.16), channel_id=1, replica_groups=mesh['chip'=16,'core'=2,'fsdp'=16] {'chip'}, dimensions={0} | all-to-all | bytes 1835008 | tf_op jit(solution)/shard_map/all_to_all | solution.py:194
  163.0 5.8 %collective-permute-start.3 = (bf16[16,32,896]{2,1,0:T(8,128)(2,1)S(1)}, bf16[16,32,896]{2,1,0:T(8,128)(2,1)S(1)}, u32[]{:S(2)}, u32[]{:S(2)}) collective-permute-start(bf16[16,32,896]{2,1,0:T(8,128)(2,1)S(1)} %all_to_all.10.mine_ref), channel_id=1, source_target_pairs={{0,16},{16,0},{1,17},{17,1},{2,18},{18,2},{3,19},{19,3},{4,20},{20... | collective-permute-start | bytes 2752520 | tf_op jit(solution)/shard_map/ppermute | solution.py:195
  168.8 2.1 %collective-permute-done.3.other_ref = bf16[16,32,896]{2,1,0:T(8,128)(2,1)S(1)} collective-permute-done((bf16[16,32,896]{2,1,0:T(8,128)(2,1)S(1)}, bf16[16,32,896]{2,1,0:T(8,128)(2,1)S(1)}, u32[]{:S(2)}, u32[]{:S(2)}) %collective-permute-start.3) | collective-permute-done | bytes 917536 | tf_op jit(solution)/shard_map/ppermute | solution.py:195
  170.9 1.6 shard_map.79
Async XLA Ops:
  0.6 10.9 %collective-permute-start = (bf16[768,512]{1,0:T(8,128)(2,1)}, bf16[768,512]{1,0:T(8,128)(2,1)S(1)}, u32[]{:S(2)}, u32[]{:S(2)}) collective-permute-start(bf16[768,512]{1,0:T(8,128)(2,1)} %refs_3_.1), channel_id=1, source_target_pairs={{0,16},{16,0},{1,17},{17,1},{2,18},{18,2},{3,19},{19,3},{4,20},{20... | collective-permute-start | bytes 2359304 | tf_op jit(solution)/shard_map/ppermute | solution.py:145
  9.4 93.4 %collective-permute-start.1 = (bf16[768,896]{1,0:T(8,128)(2,1)}, bf16[768,896]{1,0:T(8,128)(2,1)}, u32[]{:S(2)}, u32[]{:S(2)}) collective-permute-start(bf16[768,896]{1,0:T(8,128)(2,1)} %own_ref.1), channel_id=1, source_target_pairs={{0,16},{16,0},{1,17},{17,1},{2,18},{18,2},{3,19},{19,3},{4,20},{20... | collective-permute-start | bytes 4128776 | tf_op jit(solution)/shard_map/ppermute | solution.py:146
  11.5 0.9 copy-start.3
  17.3 85.5 %copy-start.2 = (bf16[768,896]{1,0:T(8,128)(2,1)S(1)}, bf16[768,896]{1,0:T(8,128)(2,1)}, u32[]{:S(2)}) copy-start(bf16[768,896]{1,0:T(8,128)(2,1)} %own_ref.1) | copy-start | bytes 4128772
  105.9 6.9 %copy-start.4 = (bf16[128,1024]{1,0:T(8,128)(2,1)S(1)}, bf16[128,1024]{1,0:T(8,128)(2,1)}, u32[]{:S(2)}) copy-start(bf16[128,1024]{1,0:T(8,128)(2,1)} %get-tuple-element.13) | copy-start | bytes 786436
  105.9 18.7 %copy-start = (f32[32,896]{1,0:T(8,128)S(1)}, f32[32,896]{1,0:T(8,128)}, u32[]{:S(2)}) copy-start(f32[32,896]{1,0:T(8,128)} %first_ref.1) | copy-start | bytes 344068
  105.9 18.7 %copy-start.1 = (f32[32,896]{1,0:T(8,128)S(1)}, f32[32,896]{1,0:T(8,128)}, u32[]{:S(2)}) copy-start(f32[32,896]{1,0:T(8,128)} %second_ref.1) | copy-start | bytes 344068
  106.0 18.7 %all-to-all-start = ((bf16[16,32,896]{2,1,0:T(8,128)(2,1)}), bf16[16,32,896]{2,1,0:T(8,128)(2,1)S(1)}, u32[]{:S(2)}, u32[]{:S(2)}) async-start(bf16[16,32,896]{2,1,0:T(8,128)(2,1)} %bitcast.3), calls=%async_computation | async-start | bytes 1835008 | tf_op jit(solution)/shard_map/all_to_all | solution.py:180
  112.9 0.7 collective-permute-start.2
  163.0 7.9 %collective-permute-start.3 = (bf16[16,32,896]{2,1,0:T(8,128)(2,1)S(1)}, bf16[16,32,896]{2,1,0:T(8,128)(2,1)S(1)}, u32[]{:S(2)}, u32[]{:S(2)}) collective-permute-start(bf16[16,32,896]{2,1,0:T(8,128)(2,1)S(1)} %all_to_all.10.mine_ref), channel_id=1, source_target_pairs={{0,16},{16,0},{1,17},{17,1},{2,18},{18,2},{3,19},{19,3},{4,20},{20... | collective-permute-start | bytes 2752520 | tf_op jit(solution)/shard_map/ppermute | solution.py:195

commit v6 on v4

v6 whole, which is shorter than its diff:
```python
import numpy as np
import jax
import jax.numpy as jnp
from jax import lax
from jax.experimental import pallas as pl
from jax.experimental.pallas import tpu as pltpu
from jax.sharding import Mesh, PartitionSpec as P

decay_first = 0.9
decay_second = 0.999
epsilon = 1e-08

SWAP = [(0, 1), (1, 0)]
VMEM_LIMIT = 40 * 1024 * 1024
LAST = (((1,), (1,)), ((), ()))
IN_VMEM = pl.BlockSpec(memory_space=pltpu.VMEM)
IN_HBM = pl.BlockSpec(memory_space=pltpu.HBM)
IN_SMEM = pl.BlockSpec(memory_space=pltpu.SMEM)


def params(limit=VMEM_LIMIT):
    return pltpu.CompilerParams(vmem_limit_bytes=limit)


def cost(flops, moved):
    return pl.CostEstimate(flops=flops, bytes_accessed=moved, transcendentals=0)


def project(core_ref, holds_ref, basis_hbm, act_hbm, out_hbm, basis_ref, act_ref, out_ref, sems):
    features, rank = basis_ref.shape
    tokens = act_ref.shape[0]
    rows = features // 2
    parts = rank // rows
    wide = rank // parts
    load_basis = pltpu.make_async_copy(basis_hbm, basis_ref, sems.at[0])
    load_act = pltpu.make_async_copy(act_hbm, act_ref, sems.at[1])
    load_basis.start()
    load_act.start()
    load_basis.wait()
    mine = basis_ref[pl.ds(pl.multiple_of(core_ref[0] * rows, rows), rows), :].astype(jnp.float32)
    mine = jnp.where(holds_ref[0] == 1, mine, 0.0)
    for i in range(parts):
        out_ref[i * rows : (i + 1) * rows, tokens:] = mine[:, i * wide : (i + 1) * wide]
    load_act.wait()
    saves = []
    for i in range(parts):
        here = pl.ds(i * rows, rows)
        some = basis_ref[:, i * rows : (i + 1) * rows].T
        out_ref[here, :tokens] = lax.dot_general(some, act_ref[...], LAST, preferred_element_type=jnp.float32)
        saves.append(pltpu.make_async_copy(out_ref.at[here, :], out_hbm.at[here, :], sems.at[2 + i]))
        saves[i].start()
    for copy in saves:
        copy.wait()


def half_terms(sibling, core_ref, summed_ref, cot_ref, out_ref):
    tokens = cot_ref.shape[0]
    side = 1 - core_ref[0] if sibling else core_ref[0]
    projected = summed_ref[:, pl.ds(side, 1), :, :tokens].reshape(out_ref.shape[0], tokens)
    out_ref[...] = jnp.dot(projected, cot_ref[...], preferred_element_type=jnp.float32).astype(out_ref.dtype)


def add_terms(kept_ref, got_ref, out_ref):
    out_ref[...] = (kept_ref[...] + got_ref[...].astype(jnp.float32)).astype(jnp.bfloat16)


def adam(terms_ref, first_ref, second_ref, moment_ref, square_ref, copies_ref):
    gradient = terms_ref[0].astype(jnp.float32)
    for i in range(1, terms_ref.shape[0]):
        gradient += terms_ref[i].astype(jnp.float32)
    moment_next = decay_first * first_ref[...] + (1.0 - decay_first) * gradient
    square_next = decay_second * second_ref[...] + (1.0 - decay_second) * gradient * gradient
    moment_ref[...] = moment_next
    square_ref[...] = square_next
    direction = (moment_next / (jnp.sqrt(square_next) + epsilon)).astype(jnp.bfloat16)
    for i in range(copies_ref.shape[0]):
        copies_ref[i] = direction


def expand(core_ref, summed_ref, mine_ref, other_ref, out_ref, block_ref, all_ref):
    rows, columns = out_ref.shape
    rank = block_ref.shape[1]
    parts = summed_ref.shape[0] // rows
    wide = rank // parts
    start = summed_ref.shape[1] - wide
    core = core_ref[0]
    for i in range(parts):
        block_ref[:, i * wide : (i + 1) * wide] = summed_ref[i * rows : (i + 1) * rows, start:]
    all_ref[:, pl.ds(core, 1)] = mine_ref[...][:, None]
    all_ref[:, pl.ds(1 - core, 1)] = other_ref[...][:, None]
    direction = all_ref[...].reshape(rank, columns)
    out_ref[...] = jnp.dot(block_ref[...], direction, preferred_element_type=jnp.float32).astype(jnp.bfloat16)


def body(activations, cotangent, basis, first_moment, second_moment):
    chips = lax.axis_size("chip")
    features, rank = basis.shape
    tokens = activations.shape[0]
    half = rank // 2
    own_rows, columns = first_moment.shape
    core = lax.axis_index("core").astype(jnp.int32).reshape(1)
    holds = (lax.axis_index("chip") == lax.axis_index("fsdp")).astype(jnp.int32).reshape(1)
    f32, bf16 = jnp.float32, jnp.bfloat16

    rows = features // 2
    width = tokens + rows
    partial = pl.pallas_call(
        project,
        out_shape=pltpu.HBM((rank, width), f32),
        in_specs=[IN_SMEM, IN_SMEM, IN_HBM, IN_HBM],
        out_specs=IN_HBM,
        scratch_shapes=[
            pltpu.VMEM((features, rank), bf16),
            pltpu.VMEM((tokens, features), bf16),
            pltpu.VMEM((rank, width), f32),
            pltpu.SemaphoreType.DMA((2 + rank // rows,)),
        ],
        compiler_params=params(55 * 1024 * 1024),
        cost_estimate=cost(2 * rank * tokens * features, 6 << 20),
    )(core, holds, basis, activations)
    summed = lax.psum(partial, "fsdp").astype(bf16)

    def half_of(sibling, dtype):
        return pl.pallas_call(
            lambda *refs: half_terms(sibling, *refs),
            out_shape=jax.ShapeDtypeStruct((half, columns), dtype),
            in_specs=[IN_SMEM, IN_VMEM, IN_VMEM],
            out_specs=IN_VMEM,
            compiler_params=params(),
            cost_estimate=cost(rank * tokens * columns, 4 << 20),
        )(core, summed.reshape(chips, 2, own_rows, width), cotangent)

    got = lax.ppermute(half_of(True, bf16), "core", SWAP)
    terms = pl.pallas_call(
        add_terms,
        out_shape=jax.ShapeDtypeStruct((half, columns), bf16),
        in_specs=[IN_VMEM] * 2,
        out_specs=IN_VMEM,
        compiler_params=params(),
        cost_estimate=cost(half * columns, 4 << 20),
    )(half_of(False, f32), got)
    terms = lax.all_to_all(terms.reshape(chips, own_rows, columns), "chip", 0, 0, tiled=True)

    moment_next, square_next, copies = pl.pallas_call(
        adam,
        out_shape=(
            jax.ShapeDtypeStruct((own_rows, columns), f32),
            jax.ShapeDtypeStruct((own_rows, columns), f32),
            jax.ShapeDtypeStruct((chips, own_rows, columns), bf16),
        ),
        in_specs=[IN_VMEM] * 3,
        out_specs=(IN_VMEM,) * 3,
        compiler_params=params(),
        cost_estimate=cost(1 << 20, 2 << 20),
    )(terms, first_moment, second_moment)
    mine = lax.all_to_all(copies, "chip", 0, 0, tiled=True)
    other = lax.ppermute(mine, "core", SWAP)
    expanded = pl.pallas_call(
        expand,
        out_shape=jax.ShapeDtypeStruct((features // 2, columns), bf16),
        in_specs=[IN_SMEM, IN_VMEM, IN_VMEM, IN_VMEM],
        out_specs=IN_VMEM,
        scratch_shapes=[pltpu.VMEM((rows, rank), bf16), pltpu.VMEM((chips, 2, own_rows, columns), bf16)],
        compiler_params=params(),
        cost_estimate=cost(features * rank * columns, 4 << 20),
    )(core, summed, mine, other)
    return (moment_next, square_next, expanded)


def solution(mesh):
    devices = np.asarray(mesh.devices)
    inner = Mesh(devices.reshape(devices.shape[0] // 2, 2, devices.shape[1]), ("chip", "core", "fsdp"))
    split = P(("chip", "core"), "fsdp")
    in_specs = (split, split, P("fsdp", None), split, split)
    return jax.shard_map(body, mesh=inner, in_specs=in_specs, out_specs=(split, split, split), check_vma=False)
```

time: 163 us -> 165 us (1.012)
  blocking collectives: 129 us -> 142 us
  starting transfers between devices: 18.9 us -> 9.88 us
  Pallas kernels: 10.7 us -> 8.52 us
    psum x1, blocking collectives: 97 us -> 103 us  [body(): summed = lax.psum(partial, 'fsdp').astype(bf16)]
    ppermute x2 -> x1, starting transfers between devices: 10.7 us -> 5.84 us  [body(): got = lax.ppermute(half_of(True, bf16), 'core', SWAP)]
    ppermute x1, starting transfers between devices: 8.15 us -> 4.04 us  [body(): other = lax.ppermute(mine, 'core', SWAP)]
    all_to_all x1, blocking collectives: 13.8 us -> 17.7 us  [body(): mine = lax.all_to_all(copies, 'chip', 0, 0, tiled=True)]
    all_to_all x1, blocking collectives: 18.3 us -> 21.7 us  [body(): lax.all_to_all(terms.reshape(chips, own_rows, columns), 'chip', 0, 0, til...]
    pallas_call x2 -> x4, Pallas kernels: 8.17 us -> 6.03 us  [the longest x1 3.91 us: body(): pl.pallas_call(project, out_shape=pltpu.HBM((rank, width), f32), in_specs...]
  transfers between devices with their start and end apart: 3 -> 2, of which waited for: 2 -> 2; matrix products, arithmetic and copies ran while one was open for 0% -> 0% of each run, Pallas kernels for 3% -> 1%
where the time goes in v6:
time: 165 us
  blocking collectives  142 us (86%)
  starting transfers between devices  9.88 us (6%)
  Pallas kernels  8.52 us (5%)
  waiting for transfers between devices  3.15 us (2%)
    psum x1, blocking collectives, body(): summed = lax.psum(partial, 'fsdp').astype(bf16)  103 us
    all_to_all x1, blocking collectives, body(): lax.all_to_all(terms.reshape(chips, own_rows, columns), 'chip', 0, 0, til...  21.7 us
    all_to_all x1, blocking collectives, body(): mine = lax.all_to_all(copies, 'chip', 0, 0, tiled=True)  17.7 us
    ppermute x1, starting transfers between devices, body(): got = lax.ppermute(half_of(True, bf16), 'core', SWAP)  5.84 us
    ppermute x1, starting transfers between devices, body(): other = lax.ppermute(mine, 'core', SWAP)  4.04 us
    pallas_call x1, Pallas kernels, body(): pl.pallas_call(project, out_shape=pltpu.HBM((rank, width), f32), in_specs...  3.91 us
  transfers between devices with their start and end apart: 2, of which 2 were waited for; matrix products, arithmetic and copies ran while one was open for 0% of the time, Pallas kernels for 1%

profile of v6, /device:TPU:1, one launch (start us, length us, event | category | flops | bytes accessed | tf_op | source)
XLA Modules:
  0.0 164.8 jit_solution(14931174459289056169)
XLA Ops:
  0.6 3.9 %shard_map.76 = f32[1024,1024]{1,0:T(8,128)} custom-call(s32[1]{0:T(128)} %bitcast.core_ref.refs_0_, s32[1]{0:T(128)} %bitcast.1.holds_ref, bf16[512,1024]{1,0:T(8,128)(2,1)} %basis_hbm.1, bf16[768,512]{1,0:T(8,128)(2,1)} %act_hbm.1), custom_call_target="tpu_custom_call" | custom-call | flops 805306368 | bytes 6291456 | tf_op jit(solution)/shard_map/pallas_call | solution.py:107
  4.6 0.0 copy-start
  4.6 103.0 %all-reduce.1.summed_ref = bf16[1024,1024]{1,0:T(8,128)(2,1)S(1)} all-reduce(f32[1024,1024]{1,0:T(8,128)} %shard_map.76), channel_id=1, replica_groups=mesh['chip'=16,'core'=2,'fsdp'=16] {'fsdp'}, use_global_device_ids=true, to_apply=%region_0.0 | all-reduce | flops 1048576 | bytes 6291456 | tf_op jit(solution)/shard_map/psum | solution.py:121
  107.6 0.0 copy-done
  107.6 1.0 shard_map.78
  108.6 5.8 %collective-permute-start = (bf16[512,896]{1,0:T(8,128)(2,1)S(1)}, bf16[512,896]{1,0:T(8,128)(2,1)S(1)}, u32[]{:S(2)}, u32[]{:S(2)}) collective-permute-start(bf16[512,896]{1,0:T(8,128)(2,1)S(1)} %shard_map.78), channel_id=1, source_target_pairs={{0,16},{16,0},{1,17},{17,1},{2,18},{18,2},{3,19},{19,3},{4,20},{20... | collective-permute-start | bytes 2752520 | tf_op jit(solution)/shard_map/ppermute | solution.py:133
  114.5 1.0 shard_map.77.kept_ref
  115.4 0.0 copy-start.1
  115.5 0.0 copy-start.2
  115.5 1.1 collective-permute-done.got_ref
  116.5 0.2 shard_map.79
  116.7 21.7 %all_to_all.10.terms_ref = bf16[16,32,896]{2,1,0:T(8,128)(2,1)S(1)} all-to-all(bf16[16,32,896]{2,1,0:T(8,128)(2,1)S(1)} %bitcast.6), channel_id=1, replica_groups=mesh['chip'=16,'core'=2,'fsdp'=16] {'chip'}, dimensions={0} | all-to-all | bytes 1835008 | tf_op jit(solution)/shard_map/all_to_all | solution.py:142
  138.4 0.0 copy-done.1
  138.4 0.0 copy-done.2
  138.4 0.9 shard_map.80
  139.3 17.7 %all_to_all.11.mine_ref = bf16[16,32,896]{2,1,0:T(8,128)(2,1)S(1)} all-to-all(bf16[16,32,896]{2,1,0:T(8,128)(2,1)S(1)} %get-tuple-element.8), channel_id=1, replica_groups=mesh['chip'=16,'core'=2,'fsdp'=16] {'chip'}, dimensions={0} | all-to-all | bytes 1835008 | tf_op jit(solution)/shard_map/all_to_all | solution.py:156
  157.0 4.0 %collective-permute-start.1 = (bf16[16,32,896]{2,1,0:T(8,128)(2,1)S(1)}, bf16[16,32,896]{2,1,0:T(8,128)(2,1)S(1)}, u32[]{:S(2)}, u32[]{:S(2)}) collective-permute-start(bf16[16,32,896]{2,1,0:T(8,128)(2,1)S(1)} %all_to_all.11.mine_ref), channel_id=1, source_target_pairs={{0,16},{16,0},{1,17},{17,1},{2,18},{18,2},{3,19},{19,3},{4,20},{20... | collective-permute-start | bytes 2752520 | tf_op jit(solution)/shard_map/ppermute | solution.py:157
  161.1 2.1 %collective-permute-done.1.other_ref = bf16[16,32,896]{2,1,0:T(8,128)(2,1)S(1)} collective-permute-done((bf16[16,32,896]{2,1,0:T(8,128)(2,1)S(1)}, bf16[16,32,896]{2,1,0:T(8,128)(2,1)S(1)}, u32[]{:S(2)}, u32[]{:S(2)}) %collective-permute-start.1) | collective-permute-done | bytes 917536 | tf_op jit(solution)/shard_map/ppermute | solution.py:157
  163.1 1.6 shard_map.81
Async XLA Ops:
  4.6 103.1 %copy-start = (bf16[768,896]{1,0:T(8,128)(2,1)S(1)}, bf16[768,896]{1,0:T(8,128)(2,1)}, u32[]{:S(2)}) copy-start(bf16[768,896]{1,0:T(8,128)(2,1)} %refs_2_.3) | copy-start | bytes 4128772
  108.6 7.9 %collective-permute-start = (bf16[512,896]{1,0:T(8,128)(2,1)S(1)}, bf16[512,896]{1,0:T(8,128)(2,1)S(1)}, u32[]{:S(2)}, u32[]{:S(2)}) collective-permute-start(bf16[512,896]{1,0:T(8,128)(2,1)S(1)} %shard_map.78), channel_id=1, source_target_pairs={{0,16},{16,0},{1,17},{17,1},{2,18},{18,2},{3,19},{19,3},{4,20},{20... | collective-permute-start | bytes 2752520 | tf_op jit(solution)/shard_map/ppermute | solution.py:133
  115.4 23.0 %copy-start.1 = (f32[32,896]{1,0:T(8,128)S(1)}, f32[32,896]{1,0:T(8,128)}, u32[]{:S(2)}) copy-start(f32[32,896]{1,0:T(8,128)} %first_ref.1) | copy-start | bytes 344068
  115.5 23.0 %copy-start.2 = (f32[32,896]{1,0:T(8,128)S(1)}, f32[32,896]{1,0:T(8,128)}, u32[]{:S(2)}) copy-start(f32[32,896]{1,0:T(8,128)} %second_ref.1) | copy-start | bytes 344068
  157.0 6.1 %collective-permute-start.1 = (bf16[16,32,896]{2,1,0:T(8,128)(2,1)S(1)}, bf16[16,32,896]{2,1,0:T(8,128)(2,1)S(1)}, u32[]{:S(2)}, u32[]{:S(2)}) collective-permute-start(bf16[16,32,896]{2,1,0:T(8,128)(2,1)S(1)} %all_to_all.11.mine_ref), channel_id=1, source_target_pairs={{0,16},{16,0},{1,17},{17,1},{2,18},{18,2},{3,19},{19,3},{4,20},{20... | collective-permute-start | bytes 2752520 | tf_op jit(solution)/shard_map/ppermute | solution.py:157

commit v7 on v2

v7 whole, which is shorter than its diff:
```python
import numpy as np
import jax
import jax.numpy as jnp
from jax import lax
from jax.experimental import pallas as pl
from jax.experimental.pallas import tpu as pltpu
from jax.sharding import Mesh, PartitionSpec as P

decay_first = 0.9
decay_second = 0.999
epsilon = 1e-08

SWAP = [(0, 1), (1, 0)]
VMEM_LIMIT = 40 * 1024 * 1024
LAST = (((1,), (1,)), ((), ()))
IN_VMEM = pl.BlockSpec(memory_space=pltpu.VMEM)
IN_HBM = pl.BlockSpec(memory_space=pltpu.HBM)
IN_SMEM = pl.BlockSpec(memory_space=pltpu.SMEM)


def params(limit=VMEM_LIMIT):
    return pltpu.CompilerParams(vmem_limit_bytes=limit)


def cost(flops, moved):
    return pl.CostEstimate(flops=flops, bytes_accessed=moved, transcendentals=0)


def project_rows(picked, act_ref, out_ref, out_hbm, sems):
    part = out_ref.shape[0] // 2
    copies = []
    for i in range(2):
        rows = pl.ds(i * part, part)
        out_ref[rows, :] = lax.dot_general(
            picked[i * part : (i + 1) * part], act_ref[...], LAST, preferred_element_type=jnp.float32
        )
        copies.append(pltpu.make_async_copy(out_ref.at[rows, :], out_hbm.at[rows, :], sems.at[i]))
        copies[i].start()
    return copies


def project_own(core_ref, holds_ref, basis_hbm, act_hbm, out_hbm, picked_ref, basis_ref, act_ref, turned_ref, own_ref, block_ref, sems):
    features, rank = basis_ref.shape
    tokens = act_ref.shape[0]
    half = rank // 2
    rows = features // 2
    load_basis = pltpu.make_async_copy(basis_hbm, basis_ref, sems.at[0])
    load_act = pltpu.make_async_copy(act_hbm, act_ref, sems.at[1])
    load_basis.start()
    load_act.start()
    load_basis.wait()
    mine = basis_ref[pl.ds(pl.multiple_of(core_ref[0] * rows, rows), rows), :].astype(jnp.float32)
    mine = jnp.where(holds_ref[0] == 1, mine, 0.0)
    block_ref[:rows, :] = mine[:, :half]
    block_ref[rows:, :] = mine[:, half:]
    save_block = pltpu.make_async_copy(block_ref, out_hbm.at[:, pl.ds(2 * tokens, half)], sems.at[2])
    save_block.start()
    turned_ref[...] = basis_ref[...].T.reshape(turned_ref.shape)
    picked = turned_ref[:, pl.ds(core_ref[0], 1)].reshape(half, features)
    picked_ref[...] = picked
    load_act.wait()
    copies = project_rows(picked, act_ref, own_ref, out_hbm.at[:, pl.ds(0, tokens)], sems.at[pl.ds(3, 2)])
    for copy in [save_block] + copies:
        copy.wait()


def project_other(picked_ref, act_ref, _, out_hbm, other_ref, sems):
    tokens = act_ref.shape[0]
    copies = project_rows(picked_ref[...], act_ref, other_ref, out_hbm.at[:, pl.ds(tokens, tokens)], sems)
    for copy in copies:
        copy.wait()


def grad_terms(summed_ref, own_ref, other_hbm, out_ref, other_ref, total_ref, sems):
    tokens = own_ref.shape[0]
    part = tokens // 2
    loads = []
    for i in range(2):
        rows = pl.ds(i * part, part)
        loads.append(pltpu.make_async_copy(other_hbm.at[rows, :], other_ref.at[rows, :], sems.at[i]))
        loads[i].start()
    total_ref[...] = jnp.dot(summed_ref[:, :tokens], own_ref[...], preferred_element_type=jnp.float32)
    for load in loads:
        load.wait()
    part = out_ref.shape[0] // 2
    for i in range(2):
        rows = pl.ds(i * part, part)
        more = jnp.dot(summed_ref[rows, tokens : 2 * tokens], other_ref[...], preferred_element_type=jnp.float32)
        out_ref[rows, :] = (total_ref[rows, :] + more).astype(jnp.bfloat16)


def adam(terms_ref, first_ref, second_ref, moment_ref, square_ref, copies_ref):
    gradient = terms_ref[0].astype(jnp.float32)
    for i in range(1, terms_ref.shape[0]):
        gradient += terms_ref[i].astype(jnp.float32)
    moment_next = decay_first * first_ref[...] + (1.0 - decay_first) * gradient
    square_next = decay_second * second_ref[...] + (1.0 - decay_second) * gradient * gradient
    moment_ref[...] = moment_next
    square_ref[...] = square_next
    direction = (moment_next / (jnp.sqrt(square_next) + epsilon)).astype(jnp.bfloat16)
    for i in range(copies_ref.shape[0]):
        copies_ref[i] = direction


def expand(core_ref, summed_ref, mine_ref, other_ref, out_ref, all_ref):
    rows, columns = out_ref.shape
    half = summed_ref.shape[0]
    start = summed_ref.shape[1] - half
    core = core_ref[0]
    all_ref[:, pl.ds(core, 1)] = mine_ref[...][:, None]
    all_ref[:, pl.ds(1 - core, 1)] = other_ref[...][:, None]
    direction = all_ref[...].reshape(2 * half, columns)
    total = jnp.dot(summed_ref[:rows, start:], direction[:half], preferred_element_type=jnp.float32)
    total += jnp.dot(summed_ref[rows:, start:], direction[half:], preferred_element_type=jnp.float32)
    out_ref[...] = total.astype(jnp.bfloat16)


def body(activations, cotangent, basis, first_moment, second_moment):
    chips = lax.axis_size("chip")
    features, rank = basis.shape
    tokens = activations.shape[0]
    half = rank // 2
    own_rows, columns = first_moment.shape
    core = lax.axis_index("core").astype(jnp.int32).reshape(1)
    holds = (lax.axis_index("chip") == lax.axis_index("fsdp")).astype(jnp.int32).reshape(1)
    f32, bf16 = jnp.float32, jnp.bfloat16

    other_act = lax.ppermute(activations, "core", SWAP)
    other_cot = lax.ppermute(cotangent, "core", SWAP)
    width = 2 * tokens + half
    partial, picked = pl.pallas_call(
        project_own,
        out_shape=(pltpu.HBM((half, width), f32), pltpu.VMEM((half, features), bf16)),
        in_specs=[IN_SMEM, IN_SMEM, IN_HBM, IN_HBM],
        out_specs=(IN_HBM, IN_VMEM),
        scratch_shapes=[
            pltpu.VMEM((features, rank), bf16),
            pltpu.VMEM((tokens, features), bf16),
            pltpu.VMEM((chips, 2, own_rows, features), bf16),
            pltpu.VMEM((half, tokens), f32),
            pltpu.VMEM((half, half), f32),
            pltpu.SemaphoreType.DMA((5,)),
        ],
        compiler_params=params(60 * 1024 * 1024),
        cost_estimate=cost(2 * rank * tokens * features, 5 << 20),
    )(core, holds, basis, activations)
    partial = pl.pallas_call(
        project_other,
        out_shape=pltpu.HBM((half, width), f32),
        in_specs=[IN_VMEM, IN_VMEM, IN_HBM],
        out_specs=IN_HBM,
        scratch_shapes=[pltpu.VMEM((half, tokens), f32), pltpu.SemaphoreType.DMA((2,))],
        input_output_aliases={2: 0},
        compiler_params=params(),
        cost_estimate=cost(rank * tokens * features, 3 << 20),
    )(picked, other_act, partial)
    summed = lax.psum(partial, "fsdp").astype(bf16)

    terms = pl.pallas_call(
        grad_terms,
        out_shape=jax.ShapeDtypeStruct((half, columns), bf16),
        in_specs=[IN_VMEM, IN_VMEM, IN_HBM],
        out_specs=IN_VMEM,
        scratch_shapes=[
            pltpu.VMEM((tokens, columns), bf16),
            pltpu.VMEM((half, columns), f32),
            pltpu.SemaphoreType.DMA((2,)),
        ],
        compiler_params=params(),
        cost_estimate=cost(2 * rank * tokens * columns, 5 << 20),
    )(summed, cotangent, other_cot)
    terms = lax.all_to_all(terms.reshape(chips, own_rows, columns), "chip", 0, 0, tiled=True)

    moment_next, square_next, copies = pl.pallas_call(
        adam,
        out_shape=(
            jax.ShapeDtypeStruct((own_rows, columns), f32),
            jax.ShapeDtypeStruct((own_rows, columns), f32),
            jax.ShapeDtypeStruct((chips, own_rows, columns), bf16),
        ),
        in_specs=[IN_VMEM] * 3,
        out_specs=(IN_VMEM,) * 3,
        compiler_params=params(),
        cost_estimate=cost(1 << 20, 2 << 20),
    )(terms, first_moment, second_moment)
    mine = lax.all_to_all(copies, "chip", 0, 0, tiled=True)
    other = lax.ppermute(mine, "core", SWAP)
    expanded = pl.pallas_call(
        expand,
        out_shape=jax.ShapeDtypeStruct((features // 2, columns), bf16),
        in_specs=[IN_SMEM, IN_VMEM, IN_VMEM, IN_VMEM],
        out_specs=IN_VMEM,
        scratch_shapes=[pltpu.VMEM((chips, 2, own_rows, columns), bf16)],
        compiler_params=params(),
        cost_estimate=cost(features * rank * columns, 4 << 20),
    )(core, summed, mine, other)
    return (moment_next, square_next, expanded)


def solution(mesh):
    devices = np.asarray(mesh.devices)
    inner = Mesh(devices.reshape(devices.shape[0] // 2, 2, devices.shape[1]), ("chip", "core", "fsdp"))
    split = P(("chip", "core"), "fsdp")
    in_specs = (split, split, P("fsdp", None), split, split)
    return jax.shard_map(body, mesh=inner, in_specs=in_specs, out_specs=(split, split, split), check_vma=False)
```

time: 164 us -> 162 us (0.988)
  Pallas kernels: 12.9 us -> 10.7 us
  transfers between devices with their start and end apart: 3 -> 3, of which waited for: 1 -> 1; matrix products, arithmetic and copies ran while one was open for 0% -> 0% of each run, Pallas kernels for 4% -> 3%
where the time goes in v7:
time: 162 us; the launch traced here: 161 us
  blocking collectives  129 us (80%)
  starting transfers between devices  19 us (12%)
  Pallas kernels  10.7 us (7%)
  waiting for transfers between devices  2.08 us (1%)
    psum x1, blocking collectives, body(): summed = lax.psum(partial, 'fsdp').astype(bf16)  96.7 us
    all_to_all x1, blocking collectives, body(): lax.all_to_all(terms.reshape(chips, own_rows, columns), 'chip', 0, 0, til...  18.2 us
    all_to_all x1, blocking collectives, body(): mine = lax.all_to_all(copies, 'chip', 0, 0, tiled=True)  13.8 us
    ppermute x1, starting transfers between devices, body(): other_act = lax.ppermute(activations, 'core', SWAP)  8.79 us
    ppermute x1, starting transfers between devices, body(): other = lax.ppermute(mine, 'core', SWAP)  8.33 us
    pallas_call x1, Pallas kernels, body(): pl.pallas_call(project_own, out_shape=(pltpu.HBM((half, width), f32), plt...  3.43 us
  transfers between devices with their start and end apart: 3, of which 1 were waited for; matrix products, arithmetic and copies ran while one was open for 0% of the time, Pallas kernels for 3%

profile of v7, /device:TPU:1, one launch (start us, length us, event | category | flops | bytes accessed | tf_op | source)
XLA Modules:
  0.0 161.3 jit_solution(18172437674317538380)
XLA Ops:
  0.6 8.8 %collective-permute-start = (bf16[768,512]{1,0:T(8,128)(2,1)}, bf16[768,512]{1,0:T(8,128)(2,1)S(1)}, u32[]{:S(2)}, u32[]{:S(2)}) collective-permute-start(bf16[768,512]{1,0:T(8,128)(2,1)} %act_hbm.1), channel_id=1, source_target_pairs={{0,16},{16,0},{1,17},{17,1},{2,18},{18,2},{3,19},{19,3},{4,20},{20... | collective-permute-start | bytes 2359304 | tf_op jit(solution)/shard_map/ppermute | solution.py:128
  9.4 1.9 %collective-permute-start.1 = (bf16[768,896]{1,0:T(8,128)(2,1)}, bf16[768,896]{1,0:T(8,128)(2,1)}, u32[]{:S(2)}, u32[]{:S(2)}) collective-permute-start(bf16[768,896]{1,0:T(8,128)(2,1)} %own_ref.1), channel_id=1, source_target_pairs={{0,16},{16,0},{1,17},{17,1},{2,18},{18,2},{3,19},{19,3},{4,20},{20... | collective-permute-start | bytes 4128776 | tf_op jit(solution)/shard_map/ppermute | solution.py:129
  11.4 3.4 %shard_map.76 = (f32[512,2048]{1,0:T(8,128)}, bf16[512,512]{1,0:T(8,128)(2,1)S(1)}) custom-call(s32[1]{0:T(128)} %bitcast.core_ref, s32[1]{0:T(128)} %bitcast.1.holds_ref, bf16[512,1024]{1,0:T(8,128)(2,1)} %basis_hbm.1, bf16[768,512]{1,0:T(8,128)(2,1)} %act_hbm.1), custom_call_target="tpu_custom_call" | custom-call | flops 805306368 | bytes 5242880 | tf_op jit(solution)/shard_map/pallas_call | solution.py:131
  14.8 0.0 collective-permute-done.act_ref
  14.8 1.7 %shard_map.77 = f32[512,2048]{1,0:T(8,128)} custom-call(bf16[512,512]{1,0:T(8,128)(2,1)S(1)} %get-tuple-element.8.picked_ref, bf16[768,512]{1,0:T(8,128)(2,1)S(1)} %collective-permute-done.act_ref, f32[512,2048]{1,0:T(8,128)} %get-tuple-element.9._), custom_call_target="tpu_custom_call", output_to_operand_aliasing={{}: (2, {})} | custom-call | flops 402653184 | bytes 3145728 | tf_op jit(solution)/shard_map/pallas_call | solution.py:147
  16.5 0.0 copy-start
  16.5 96.7 %all-reduce.1.summed_ref = bf16[512,2048]{1,0:T(8,128)(2,1)S(1)} all-reduce(f32[512,2048]{1,0:T(8,128)} %shard_map.77), channel_id=1, replica_groups=mesh['chip'=16,'core'=2,'fsdp'=16] {'fsdp'}, use_global_device_ids=true, to_apply=%region_0.0 | all-reduce | flops 1048576 | bytes 6291456 | tf_op jit(solution)/shard_map/psum | solution.py:157
  113.2 0.0 copy-start.1
  113.3 0.0 copy-start.2
  113.3 0.0 collective-permute-done.1.other_hbm
  113.3 0.0 copy-done
  113.3 3.1 %shard_map.78 = bf16[512,896]{1,0:T(8,128)(2,1)S(1)} custom-call(bf16[512,2048]{1,0:T(8,128)(2,1)S(1)} %all-reduce.1.summed_ref, bf16[768,896]{1,0:T(8,128)(2,1)S(1)} %copy-done, bf16[768,896]{1,0:T(8,128)(2,1)} %collective-permute-done.1.other_hbm), custom_call_target="tpu_custom_call" | custom-call | flops 1409286144 | bytes 5242880 | tf_op jit(solution)/shard_map/pallas_call | solution.py:159
  116.4 18.2 %all_to_all.10.terms_ref = bf16[16,32,896]{2,1,0:T(8,128)(2,1)S(1)} all-to-all(bf16[16,32,896]{2,1,0:T(8,128)(2,1)S(1)} %bitcast.3), channel_id=1, replica_groups=mesh['chip'=16,'core'=2,'fsdp'=16] {'chip'}, dimensions={0} | all-to-all | bytes 1835008 | tf_op jit(solution)/shard_map/all_to_all | solution.py:172
  134.5 0.0 copy-done.1
  134.5 0.0 copy-done.2
  134.5 0.9 shard_map.79
  135.4 13.8 %all_to_all.11.mine_ref = bf16[16,32,896]{2,1,0:T(8,128)(2,1)S(1)} all-to-all(bf16[16,32,896]{2,1,0:T(8,128)(2,1)S(1)} %get-tuple-element.12), channel_id=1, replica_groups=mesh['chip'=16,'core'=2,'fsdp'=16] {'chip'}, dimensions={0} | all-to-all | bytes 1835008 | tf_op jit(solution)/shard_map/all_to_all | solution.py:186
  149.2 8.3 %collective-permute-start.2 = (bf16[16,32,896]{2,1,0:T(8,128)(2,1)S(1)}, bf16[16,32,896]{2,1,0:T(8,128)(2,1)S(1)}, u32[]{:S(2)}, u32[]{:S(2)}) collective-permute-start(bf16[16,32,896]{2,1,0:T(8,128)(2,1)S(1)} %all_to_all.11.mine_ref), channel_id=1, source_target_pairs={{0,16},{16,0},{1,17},{17,1},{2,18},{18,2},{3,19},{19,3},{4,20},{20... | collective-permute-start | bytes 2752520 | tf_op jit(solution)/shard_map/ppermute | solution.py:187
  157.6 2.1 %collective-permute-done.2.other_ref = bf16[16,32,896]{2,1,0:T(8,128)(2,1)S(1)} collective-permute-done((bf16[16,32,896]{2,1,0:T(8,128)(2,1)S(1)}, bf16[16,32,896]{2,1,0:T(8,128)(2,1)S(1)}, u32[]{:S(2)}, u32[]{:S(2)}) %collective-permute-start.2) | collective-permute-done | bytes 917536 | tf_op jit(solution)/shard_map/ppermute | solution.py:187
  159.7 1.6 %shard_map.80 = bf16[256,896]{1,0:T(8,128)(2,1)} custom-call(s32[1]{0:T(128)} %bitcast.core_ref, bf16[512,2048]{1,0:T(8,128)(2,1)S(1)} %all-reduce.1.summed_ref, bf16[16,32,896]{2,1,0:T(8,128)(2,1)S(1)} %all_to_all.11.mine_ref, bf16[16,32,896]{2,1,0:T(8,128)(2,1)S(1)} %collective-permute-done.2.other_ref), custom_call_target="tpu_custom_call" | custom-call | flops 469762048 | bytes 4194304 | tf_op jit(solution)/shard_map/pallas_call | solution.py:188
Async XLA Ops:
  0.6 14.2 %collective-permute-start = (bf16[768,512]{1,0:T(8,128)(2,1)}, bf16[768,512]{1,0:T(8,128)(2,1)S(1)}, u32[]{:S(2)}, u32[]{:S(2)}) collective-permute-start(bf16[768,512]{1,0:T(8,128)(2,1)} %act_hbm.1), channel_id=1, source_target_pairs={{0,16},{16,0},{1,17},{17,1},{2,18},{18,2},{3,19},{19,3},{4,20},{20... | collective-permute-start | bytes 2359304 | tf_op jit(solution)/shard_map/ppermute | solution.py:128
  9.4 103.8 %collective-permute-start.1 = (bf16[768,896]{1,0:T(8,128)(2,1)}, bf16[768,896]{1,0:T(8,128)(2,1)}, u32[]{:S(2)}, u32[]{:S(2)}) collective-permute-start(bf16[768,896]{1,0:T(8,128)(2,1)} %own_ref.1), channel_id=1, source_target_pairs={{0,16},{16,0},{1,17},{17,1},{2,18},{18,2},{3,19},{19,3},{4,20},{20... | collective-permute-start | bytes 4128776 | tf_op jit(solution)/shard_map/ppermute | solution.py:129
  16.5 96.8 %copy-start = (bf16[768,896]{1,0:T(8,128)(2,1)S(1)}, bf16[768,896]{1,0:T(8,128)(2,1)}, u32[]{:S(2)}) copy-start(bf16[768,896]{1,0:T(8,128)(2,1)} %own_ref.1) | copy-start | bytes 4128772
  113.2 21.3 %copy-start.1 = (f32[32,896]{1,0:T(8,128)S(1)}, f32[32,896]{1,0:T(8,128)}, u32[]{:S(2)}) copy-start(f32[32,896]{1,0:T(8,128)} %first_ref.1) | copy-start | bytes 344068
  113.3 21.3 %copy-start.2 = (f32[32,896]{1,0:T(8,128)S(1)}, f32[32,896]{1,0:T(8,128)}, u32[]{:S(2)}) copy-start(f32[32,896]{1,0:T(8,128)} %second_ref.1) | copy-start | bytes 344068
  149.2 10.4 %collective-permute-start.2 = (bf16[16,32,896]{2,1,0:T(8,128)(2,1)S(1)}, bf16[16,32,896]{2,1,0:T(8,128)(2,1)S(1)}, u32[]{:S(2)}, u32[]{:S(2)}) collective-permute-start(bf16[16,32,896]{2,1,0:T(8,128)(2,1)S(1)} %all_to_all.11.mine_ref), channel_id=1, source_target_pairs={{0,16},{16,0},{1,17},{17,1},{2,18},{18,2},{3,19},{19,3},{4,20},{20... | collective-permute-start | bytes 2752520 | tf_op jit(solution)/shard_map/ppermute | solution.py:187

commit v8 on v7

--- a/solution.py
+++ b/solution.py
@@ -71,22 +71,18 @@
         copy.wait()
 
 
-def grad_terms(summed_ref, own_ref, other_hbm, out_ref, other_ref, total_ref, sems):
+def own_terms(summed_ref, own_ref, other_hbm, out_ref, other_ref, sem):
     tokens = own_ref.shape[0]
-    part = tokens // 2
-    loads = []
-    for i in range(2):
-        rows = pl.ds(i * part, part)
-        loads.append(pltpu.make_async_copy(other_hbm.at[rows, :], other_ref.at[rows, :], sems.at[i]))
-        loads[i].start()
-    total_ref[...] = jnp.dot(summed_ref[:, :tokens], own_ref[...], preferred_element_type=jnp.float32)
-    for load in loads:
-        load.wait()
-    part = out_ref.shape[0] // 2
-    for i in range(2):
-        rows = pl.ds(i * part, part)
-        more = jnp.dot(summed_ref[rows, tokens : 2 * tokens], other_ref[...], preferred_element_type=jnp.float32)
-        out_ref[rows, :] = (total_ref[rows, :] + more).astype(jnp.bfloat16)
+    load = pltpu.make_async_copy(other_hbm, other_ref, sem)
+    load.start()
+    out_ref[...] = jnp.dot(summed_ref[:, :tokens], own_ref[...], preferred_element_type=jnp.float32)
+    load.wait()
+
+
+def all_terms(own_ref, summed_ref, other_ref, out_ref):
+    tokens = other_ref.shape[0]
+    more = jnp.dot(summed_ref[:, tokens : 2 * tokens], other_ref[...], preferred_element_type=jnp.float32)
+    out_ref[...] = (own_ref[...] + more).astype(jnp.bfloat16)
 
 
 def adam(terms_ref, first_ref, second_ref, moment_ref, square_ref, copies_ref):
@@ -102,17 +98,28 @@
         copies_ref[i] = direction
 
 
-def expand(core_ref, summed_ref, mine_ref, other_ref, out_ref, all_ref):
-    rows, columns = out_ref.shape
-    half = summed_ref.shape[0]
+def expand_own(core_ref, summed_ref, mine_ref, out_ref, rest_ref):
+    rows, half = rest_ref.shape
+    own_rows = mine_ref.shape[1]
     start = summed_ref.shape[1] - half
-    core = core_ref[0]
-    all_ref[:, pl.ds(core, 1)] = mine_ref[...][:, None]
-    all_ref[:, pl.ds(1 - core, 1)] = other_ref[...][:, None]
-    direction = all_ref[...].reshape(2 * half, columns)
-    total = jnp.dot(summed_ref[:rows, start:], direction[:half], preferred_element_type=jnp.float32)
-    total += jnp.dot(summed_ref[rows:, start:], direction[half:], preferred_element_type=jnp.float32)
-    out_ref[...] = total.astype(jnp.bfloat16)
+    left, right = summed_ref[:rows, start:], summed_ref[rows:, start:]
+
+    def columns_of(side):
+        at = lax.broadcasted_iota(jnp.int32, (half // 2, half), 0)
+        wanted = at // own_rows * (2 * own_rows) + side * own_rows + at % own_rows
+        pick = (lax.broadcasted_iota(jnp.int32, (half // 2, half), 1) == wanted).astype(jnp.bfloat16)
+        picked = [lax.dot_general(part, pick, LAST, preferred_element_type=jnp.float32) for part in (left, right)]
+        return jnp.concatenate(picked, 1).astype(jnp.bfloat16)
+
+    direction = mine_ref[...].reshape(half, mine_ref.shape[2])
+    out_ref[...] = jnp.dot(columns_of(core_ref[0]), direction, preferred_element_type=jnp.float32)
+    rest_ref[...] = columns_of(1 - core_ref[0])
+
+
+def expand(own_ref, rest_ref, other_ref, out_ref):
+    direction = other_ref[...].reshape(rest_ref.shape[1], other_ref.shape[2])
+    more = jnp.dot(rest_ref[...], direction, preferred_element_type=jnp.float32)
+    out_ref[...] = (own_ref[...] + more).astype(jnp.bfloat16)
 
 
 def body(activations, cotangent, basis, first_moment, second_moment):
@@ -156,19 +163,23 @@
     )(picked, other_act, partial)
     summed = lax.psum(partial, "fsdp").astype(bf16)
 
+    own, other = pl.pallas_call(
+        own_terms,
+        out_shape=(pltpu.VMEM((half, columns), f32), pltpu.VMEM((tokens, columns), bf16)),
+        in_specs=[IN_VMEM, IN_VMEM, IN_HBM],
+        out_specs=(IN_VMEM, IN_VMEM),
+        scratch_shapes=[pltpu.SemaphoreType.DMA],
+        compiler_params=params(),
+        cost_estimate=cost(rank * tokens * columns, 4 << 20),
+    )(summed, cotangent, other_cot)
     terms = pl.pallas_call(
-        grad_terms,
+        all_terms,
         out_shape=jax.ShapeDtypeStruct((half, columns), bf16),
-        in_specs=[IN_VMEM, IN_VMEM, IN_HBM],
+        in_specs=[IN_VMEM] * 3,
         out_specs=IN_VMEM,
-        scratch_shapes=[
-            pltpu.VMEM((tokens, columns), bf16),
-            pltpu.VMEM((half, columns), f32),
-            pltpu.SemaphoreType.DMA((2,)),
-        ],
-        compiler_params=params(),
-        cost_estimate=cost(2 * rank * tokens * columns, 5 << 20),
-    )(summed, cotangent, other_cot)
+        compiler_params=params(),
+        cost_estimate=cost(rank * tokens * columns, 4 << 20),
+    )(own, summed, other)
     terms = lax.all_to_all(terms.reshape(chips, own_rows, columns), "chip", 0, 0, tiled=True)
 
     moment_next, square_next, copies = pl.pallas_call(
@@ -185,15 +196,23 @@
     )(terms, first_moment, second_moment)
     mine = lax.all_to_all(copies, "chip", 0, 0, tiled=True)
     other = lax.ppermute(mine, "core", SWAP)
+    rows = features // 2
+    own, rest = pl.pallas_call(
+        expand_own,
+        out_shape=(pltpu.VMEM((rows, columns), f32), pltpu.VMEM((rows, half), bf16)),
+        in_specs=[IN_SMEM, IN_VMEM, IN_VMEM],
+        out_specs=(IN_VMEM, IN_VMEM),
+        compiler_params=params(),
+        cost_estimate=cost(rows * rank * columns, 3 << 20),
+    )(core, summed, mine)
     expanded = pl.pallas_call(
         expand,
-        out_shape=jax.ShapeDtypeStruct((features // 2, columns), bf16),
-        in_specs=[IN_SMEM, IN_VMEM, IN_VMEM, IN_VMEM],
+        out_shape=jax.ShapeDtypeStruct((rows, columns), bf16),
+        in_specs=[IN_VMEM] * 3,
         out_specs=IN_VMEM,
-        scratch_shapes=[pltpu.VMEM((chips, 2, own_rows, columns), bf16)],
-        compiler_params=params(),
-        cost_estimate=cost(features * rank * columns, 4 << 20),
-    )(core, summed, mine, other)
+        compiler_params=params(),
+        cost_estimate=cost(rows * rank * columns, 3 << 20),
+    )(own, rest, other)
     return (moment_next, square_next, expanded)
 
 

time: 162 us -> 161 us (level)
    pallas_call x2 -> x4, Pallas kernels: 4.68 us -> 4.4 us  [the longest x1 1.36 us: body(): pl.pallas_call(own_terms, out_shape=(pltpu.VMEM((half, columns), f32), pl...]
  transfers between devices with their start and end apart: 3 -> 3, of which waited for: 1 -> 1; matrix products, arithmetic and copies ran while one was open for 0% -> 0% of each run, Pallas kernels for 3% -> 4%
where the time goes in v8:
time: 161 us; the launch traced here: 160 us
  blocking collectives  129 us (80%)
  starting transfers between devices  19 us (12%)
  Pallas kernels  10.5 us (7%)
    psum x1, blocking collectives, body(): summed = lax.psum(partial, 'fsdp').astype(bf16)  96.7 us
    all_to_all x1, blocking collectives, body(): lax.all_to_all(terms.reshape(chips, own_rows, columns), 'chip', 0, 0, til...  18.3 us
    all_to_all x1, blocking collectives, body(): mine = lax.all_to_all(copies, 'chip', 0, 0, tiled=True)  13.8 us
    ppermute x1, starting transfers between devices, body(): other_act = lax.ppermute(activations, 'core', SWAP)  8.79 us
    ppermute x1, starting transfers between devices, body(): other = lax.ppermute(mine, 'core', SWAP)  8.33 us
    pallas_call x1, Pallas kernels, body(): pl.pallas_call(project_own, out_shape=(pltpu.HBM((half, width), f32), plt...  3.47 us
  transfers between devices with their start and end apart: 3, of which 1 were waited for; matrix products, arithmetic and copies ran while one was open for 0% of the time, Pallas kernels for 4%

profile of v8, /device:TPU:1, one launch (start us, length us, event | category | flops | bytes accessed | tf_op | source)
XLA Modules:
  0.0 160.4 jit_solution(14190740416624005118)
XLA Ops:
  0.6 8.8 %collective-permute-start = (bf16[768,512]{1,0:T(8,128)(2,1)}, bf16[768,512]{1,0:T(8,128)(2,1)S(1)}, u32[]{:S(2)}, u32[]{:S(2)}) collective-permute-start(bf16[768,512]{1,0:T(8,128)(2,1)} %act_hbm.1), channel_id=1, source_target_pairs={{0,16},{16,0},{1,17},{17,1},{2,18},{18,2},{3,19},{19,3},{4,20},{20... | collective-permute-start | bytes 2359304 | tf_op jit(solution)/shard_map/ppermute | solution.py:135
  9.4 1.9 %collective-permute-start.1 = (bf16[768,896]{1,0:T(8,128)(2,1)}, bf16[768,896]{1,0:T(8,128)(2,1)}, u32[]{:S(2)}, u32[]{:S(2)}) collective-permute-start(bf16[768,896]{1,0:T(8,128)(2,1)} %own_ref.1), channel_id=1, source_target_pairs={{0,16},{16,0},{1,17},{17,1},{2,18},{18,2},{3,19},{19,3},{4,20},{20... | collective-permute-start | bytes 4128776 | tf_op jit(solution)/shard_map/ppermute | solution.py:136
  11.4 3.5 %shard_map.76 = (f32[512,2048]{1,0:T(8,128)}, bf16[512,512]{1,0:T(8,128)(2,1)S(1)}) custom-call(s32[1]{0:T(128)} %bitcast.core_ref, s32[1]{0:T(128)} %bitcast.1.holds_ref, bf16[512,1024]{1,0:T(8,128)(2,1)} %basis_hbm.1, bf16[768,512]{1,0:T(8,128)(2,1)} %act_hbm.1), custom_call_target="tpu_custom_call" | custom-call | flops 805306368 | bytes 5242880 | tf_op jit(solution)/shard_map/pallas_call | solution.py:138
  14.8 0.0 collective-permute-done.act_ref
  14.9 1.7 %shard_map.77 = f32[512,2048]{1,0:T(8,128)} custom-call(bf16[512,512]{1,0:T(8,128)(2,1)S(1)} %get-tuple-element.12.picked_ref, bf16[768,512]{1,0:T(8,128)(2,1)S(1)} %collective-permute-done.act_ref, f32[512,2048]{1,0:T(8,128)} %get-tuple-element.13._), custom_call_target="tpu_custom_call", output_to_operand_aliasing={{}: (2, {})} | custom-call | flops 402653184 | bytes 3145728 | tf_op jit(solution)/shard_map/pallas_call | solution.py:154
  16.6 0.0 copy-start
  16.6 96.7 %all-reduce.1.summed_ref = bf16[512,2048]{1,0:T(8,128)(2,1)S(1)} all-reduce(f32[512,2048]{1,0:T(8,128)} %shard_map.77), channel_id=1, replica_groups=mesh['chip'=16,'core'=2,'fsdp'=16] {'fsdp'}, use_global_device_ids=true, to_apply=%region_0.0 | all-reduce | flops 1048576 | bytes 6291456 | tf_op jit(solution)/shard_map/psum | solution.py:164
  113.3 0.0 collective-permute-done.1.other_hbm
  113.3 0.0 copy-done
  113.3 1.4 shard_map.78
  114.7 1.0 shard_map.79
  115.7 0.0 copy-start.1
  115.7 0.0 copy-start.2
  115.7 18.3 %all_to_all.10.terms_ref = bf16[16,32,896]{2,1,0:T(8,128)(2,1)S(1)} all-to-all(bf16[16,32,896]{2,1,0:T(8,128)(2,1)S(1)} %bitcast.3), channel_id=1, replica_groups=mesh['chip'=16,'core'=2,'fsdp'=16] {'chip'}, dimensions={0} | all-to-all | bytes 1835008 | tf_op jit(solution)/shard_map/all_to_all | solution.py:183
  134.0 0.0 copy-done.1
  134.0 0.0 copy-done.2
  134.0 0.9 shard_map.80
  134.9 13.8 %all_to_all.11.mine_ref = bf16[16,32,896]{2,1,0:T(8,128)(2,1)S(1)} all-to-all(bf16[16,32,896]{2,1,0:T(8,128)(2,1)S(1)} %get-tuple-element.18), channel_id=1, replica_groups=mesh['chip'=16,'core'=2,'fsdp'=16] {'chip'}, dimensions={0} | all-to-all | bytes 1835008 | tf_op jit(solution)/shard_map/all_to_all | solution.py:197
  148.7 8.3 %collective-permute-start.2 = (bf16[16,32,896]{2,1,0:T(8,128)(2,1)S(1)}, bf16[16,32,896]{2,1,0:T(8,128)(2,1)S(1)}, u32[]{:S(2)}, u32[]{:S(2)}) collective-permute-start(bf16[16,32,896]{2,1,0:T(8,128)(2,1)S(1)} %all_to_all.11.mine_ref), channel_id=1, source_target_pairs={{0,16},{16,0},{1,17},{17,1},{2,18},{18,2},{3,19},{19,3},{4,20},{20... | collective-permute-start | bytes 2752520 | tf_op jit(solution)/shard_map/ppermute | solution.py:198
  157.1 0.8 shard_map.81
  157.9 1.2 collective-permute-done.2.other_ref
  159.2 1.2 shard_map.82
Async XLA Ops:
  0.6 14.2 %collective-permute-start = (bf16[768,512]{1,0:T(8,128)(2,1)}, bf16[768,512]{1,0:T(8,128)(2,1)S(1)}, u32[]{:S(2)}, u32[]{:S(2)}) collective-permute-start(bf16[768,512]{1,0:T(8,128)(2,1)} %act_hbm.1), channel_id=1, source_target_pairs={{0,16},{16,0},{1,17},{17,1},{2,18},{18,2},{3,19},{19,3},{4,20},{20... | collective-permute-start | bytes 2359304 | tf_op jit(solution)/shard_map/ppermute | solution.py:135
  9.4 103.9 %collective-permute-start.1 = (bf16[768,896]{1,0:T(8,128)(2,1)}, bf16[768,896]{1,0:T(8,128)(2,1)}, u32[]{:S(2)}, u32[]{:S(2)}) collective-permute-start(bf16[768,896]{1,0:T(8,128)(2,1)} %own_ref.1), channel_id=1, source_target_pairs={{0,16},{16,0},{1,17},{17,1},{2,18},{18,2},{3,19},{19,3},{4,20},{20... | collective-permute-start | bytes 4128776 | tf_op jit(solution)/shard_map/ppermute | solution.py:136
  16.6 96.7 %copy-start = (bf16[768,896]{1,0:T(8,128)(2,1)S(1)}, bf16[768,896]{1,0:T(8,128)(2,1)}, u32[]{:S(2)}) copy-start(bf16[768,896]{1,0:T(8,128)(2,1)} %own_ref.1) | copy-start | bytes 4128772
  115.7 18.3 %copy-start.1 = (f32[32,896]{1,0:T(8,128)S(1)}, f32[32,896]{1,0:T(8,128)}, u32[]{:S(2)}) copy-start(f32[32,896]{1,0:T(8,128)} %first_ref.1) | copy-start | bytes 344068
  115.7 18.3 %copy-start.2 = (f32[32,896]{1,0:T(8,128)S(1)}, f32[32,896]{1,0:T(8,128)}, u32[]{:S(2)}) copy-start(f32[32,896]{1,0:T(8,128)} %second_ref.1) | copy-start | bytes 344068
  148.7 10.4 %collective-permute-start.2 = (bf16[16,32,896]{2,1,0:T(8,128)(2,1)S(1)}, bf16[16,32,896]{2,1,0:T(8,128)(2,1)S(1)}, u32[]{:S(2)}, u32[]{:S(2)}) collective-permute-start(bf16[16,32,896]{2,1,0:T(8,128)(2,1)S(1)} %all_to_all.11.mine_ref), channel_id=1, source_target_pairs={{0,16},{16,0},{1,17},{17,1},{2,18},{18,2},{3,19},{19,3},{4,20},{20... | collective-permute-start | bytes 2752520 | tf_op jit(solution)/shard_map/ppermute | solution.py:198

commit v9 on v8

--- a/solution.py
+++ b/solution.py
@@ -12,6 +12,8 @@
 
 SWAP = [(0, 1), (1, 0)]
 VMEM_LIMIT = 40 * 1024 * 1024
+GRAD_LIMIT = 40 * 1024 * 1024
+LANES = 128
 LAST = (((1,), (1,)), ((), ()))
 IN_VMEM = pl.BlockSpec(memory_space=pltpu.VMEM)
 IN_HBM = pl.BlockSpec(memory_space=pltpu.HBM)
@@ -24,6 +26,17 @@
 
 def cost(flops, moved):
     return pl.CostEstimate(flops=flops, bytes_accessed=moved, transcendentals=0)
+
+
+def give_pieces(core_ref, chip_ref, basis_hbm, out_hbm, sems):
+    count, rows, _ = out_hbm.shape
+    start = pl.multiple_of(core_ref[0] * (basis_hbm.shape[0] // 2) + chip_ref[0] * rows, rows)
+    copies = []
+    for i in range(count):
+        copies.append(pltpu.make_async_copy(basis_hbm.at[pl.ds(start, rows), :], out_hbm.at[i], sems.at[i]))
+        copies[i].start()
+    for copy in copies:
+        copy.wait()
 
 
 def project_rows(picked, act_ref, out_ref, out_hbm, sems):
@@ -39,28 +52,21 @@
     return copies
 
 
-def project_own(core_ref, holds_ref, basis_hbm, act_hbm, out_hbm, picked_ref, basis_ref, act_ref, turned_ref, own_ref, block_ref, sems):
+def project_own(core_ref, basis_hbm, act_hbm, out_hbm, picked_ref, basis_ref, act_ref, turned_ref, own_ref, sems):
     features, rank = basis_ref.shape
     tokens = act_ref.shape[0]
     half = rank // 2
-    rows = features // 2
     load_basis = pltpu.make_async_copy(basis_hbm, basis_ref, sems.at[0])
     load_act = pltpu.make_async_copy(act_hbm, act_ref, sems.at[1])
     load_basis.start()
     load_act.start()
     load_basis.wait()
-    mine = basis_ref[pl.ds(pl.multiple_of(core_ref[0] * rows, rows), rows), :].astype(jnp.float32)
-    mine = jnp.where(holds_ref[0] == 1, mine, 0.0)
-    block_ref[:rows, :] = mine[:, :half]
-    block_ref[rows:, :] = mine[:, half:]
-    save_block = pltpu.make_async_copy(block_ref, out_hbm.at[:, pl.ds(2 * tokens, half)], sems.at[2])
-    save_block.start()
     turned_ref[...] = basis_ref[...].T.reshape(turned_ref.shape)
     picked = turned_ref[:, pl.ds(core_ref[0], 1)].reshape(half, features)
     picked_ref[...] = picked
     load_act.wait()
-    copies = project_rows(picked, act_ref, own_ref, out_hbm.at[:, pl.ds(0, tokens)], sems.at[pl.ds(3, 2)])
-    for copy in [save_block] + copies:
+    copies = project_rows(picked, act_ref, own_ref, out_hbm.at[:, pl.ds(0, tokens)], sems.at[pl.ds(2, 2)])
+    for copy in copies:
         copy.wait()
 
 
@@ -71,24 +77,36 @@
         copy.wait()
 
 
-def own_terms(summed_ref, own_ref, other_hbm, out_ref, other_ref, sem):
+def grad_terms(summed_ref, own_ref, other_hbm, pieces_ref, out_ref, other_ref, total_ref, sem):
     tokens = own_ref.shape[0]
+    chips, rows, rank = pieces_ref.shape
     load = pltpu.make_async_copy(other_hbm, other_ref, sem)
     load.start()
-    out_ref[...] = jnp.dot(summed_ref[:, :tokens], own_ref[...], preferred_element_type=jnp.float32)
+    own_rows = total_ref.shape[0] // chips
+    total_ref[...] = jnp.dot(summed_ref[:, :tokens], own_ref[...], preferred_element_type=jnp.float32)
+    at = own_rows * (total_ref.shape[1] // LANES)
+    for i in range(0, rank, LANES):
+        out_ref[:, at : at + rows, :] = pieces_ref[:, :, i : i + LANES]
+        at += rows
     load.wait()
-
-
-def all_terms(own_ref, summed_ref, other_ref, out_ref):
-    tokens = other_ref.shape[0]
-    more = jnp.dot(summed_ref[:, tokens : 2 * tokens], other_ref[...], preferred_element_type=jnp.float32)
-    out_ref[...] = (own_ref[...] + more).astype(jnp.bfloat16)
+    half = chips // 2
+    for j in range(0, chips, half):
+        these = slice(j * own_rows, (j + half) * own_rows)
+        more = jnp.dot(summed_ref[these, tokens:], other_ref[...], preferred_element_type=jnp.float32)
+        total = (total_ref[these, :] + more).astype(jnp.bfloat16)
+        at = 0
+        for i in range(0, total.shape[1], LANES):
+            out_ref[j : j + half, at : at + own_rows, :] = total[:, i : i + LANES].reshape(half, own_rows, LANES)
+            at += own_rows
 
 
 def adam(terms_ref, first_ref, second_ref, moment_ref, square_ref, copies_ref):
-    gradient = terms_ref[0].astype(jnp.float32)
+    own_rows, columns = first_ref.shape
+    size = own_rows * (columns // LANES)
+    total = terms_ref[0, :size, :].astype(jnp.float32)
     for i in range(1, terms_ref.shape[0]):
-        gradient += terms_ref[i].astype(jnp.float32)
+        total += terms_ref[i, :size, :].astype(jnp.float32)
+    gradient = jnp.concatenate([total[i : i + own_rows] for i in range(0, size, own_rows)], 1)
     moment_next = decay_first * first_ref[...] + (1.0 - decay_first) * gradient
     square_next = decay_second * second_ref[...] + (1.0 - decay_second) * gradient * gradient
     moment_ref[...] = moment_next
@@ -98,20 +116,24 @@
         copies_ref[i] = direction
 
 
-def expand_own(core_ref, summed_ref, mine_ref, out_ref, rest_ref):
+def expand_own(core_ref, terms_ref, mine_ref, out_ref, rest_ref, block_ref):
     rows, half = rest_ref.shape
-    own_rows = mine_ref.shape[1]
-    start = summed_ref.shape[1] - half
-    left, right = summed_ref[:rows, start:], summed_ref[rows:, start:]
+    chips, own_rows, columns = mine_ref.shape
+    piece = rows // chips
+    at = own_rows * (columns // LANES)
+    for i in range(0, 2 * half, LANES):
+        block_ref[:, i : i + LANES] = terms_ref[:, at : at + piece, :].reshape(rows, LANES)
+        at += piece
 
     def columns_of(side):
         at = lax.broadcasted_iota(jnp.int32, (half // 2, half), 0)
         wanted = at // own_rows * (2 * own_rows) + side * own_rows + at % own_rows
         pick = (lax.broadcasted_iota(jnp.int32, (half // 2, half), 1) == wanted).astype(jnp.bfloat16)
-        picked = [lax.dot_general(part, pick, LAST, preferred_element_type=jnp.float32) for part in (left, right)]
+        parts = (block_ref[:, :half], block_ref[:, half:])
+        picked = [lax.dot_general(part, pick, LAST, preferred_element_type=jnp.float32) for part in parts]
         return jnp.concatenate(picked, 1).astype(jnp.bfloat16)
 
-    direction = mine_ref[...].reshape(half, mine_ref.shape[2])
+    direction = mine_ref[...].reshape(half, columns)
     out_ref[...] = jnp.dot(columns_of(core_ref[0]), direction, preferred_element_type=jnp.float32)
     rest_ref[...] = columns_of(1 - core_ref[0])
 
@@ -129,28 +151,39 @@
     half = rank // 2
     own_rows, columns = first_moment.shape
     core = lax.axis_index("core").astype(jnp.int32).reshape(1)
-    holds = (lax.axis_index("chip") == lax.axis_index("fsdp")).astype(jnp.int32).reshape(1)
+    chip = lax.axis_index("chip").astype(jnp.int32).reshape(1)
     f32, bf16 = jnp.float32, jnp.bfloat16
+
+    piece = features // (2 * chips)
+    pieces = pl.pallas_call(
+        give_pieces,
+        out_shape=pltpu.HBM((lax.axis_size("fsdp"), piece, rank), bf16),
+        in_specs=[IN_SMEM, IN_SMEM, IN_HBM],
+        out_specs=IN_HBM,
+        scratch_shapes=[pltpu.SemaphoreType.DMA((lax.axis_size("fsdp"),))],
+        compiler_params=params(60 * 1024 * 1024),
+        cost_estimate=cost(0, 1 << 20),
+    )(core, chip, basis)
+    pieces = lax.all_to_all(pieces, "fsdp", 0, 0, tiled=True)
 
     other_act = lax.ppermute(activations, "core", SWAP)
     other_cot = lax.ppermute(cotangent, "core", SWAP)
-    width = 2 * tokens + half
+    width = 2 * tokens
     partial, picked = pl.pallas_call(
         project_own,
         out_shape=(pltpu.HBM((half, width), f32), pltpu.VMEM((half, features), bf16)),
-        in_specs=[IN_SMEM, IN_SMEM, IN_HBM, IN_HBM],
+        in_specs=[IN_SMEM, IN_HBM, IN_HBM],
         out_specs=(IN_HBM, IN_VMEM),
         scratch_shapes=[
             pltpu.VMEM((features, rank), bf16),
             pltpu.VMEM((tokens, features), bf16),
             pltpu.VMEM((chips, 2, own_rows, features), bf16),
             pltpu.VMEM((half, tokens), f32),
-            pltpu.VMEM((half, half), f32),
-            pltpu.SemaphoreType.DMA((5,)),
+            pltpu.SemaphoreType.DMA((4,)),
         ],
         compiler_params=params(60 * 1024 * 1024),
         cost_estimate=cost(2 * rank * tokens * features, 5 << 20),
-    )(core, holds, basis, activations)
+    )(core, basis, activations)
     partial = pl.pallas_call(
         project_other,
         out_shape=pltpu.HBM((half, width), f32),
@@ -163,24 +196,20 @@
     )(picked, other_act, partial)
     summed = lax.psum(partial, "fsdp").astype(bf16)
 
-    own, other = pl.pallas_call(
-        own_terms,
-        out_shape=(pltpu.VMEM((half, columns), f32), pltpu.VMEM((tokens, columns), bf16)),
-        in_specs=[IN_VMEM, IN_VMEM, IN_HBM],
-        out_specs=(IN_VMEM, IN_VMEM),
-        scratch_shapes=[pltpu.SemaphoreType.DMA],
-        compiler_params=params(),
-        cost_estimate=cost(rank * tokens * columns, 4 << 20),
-    )(summed, cotangent, other_cot)
     terms = pl.pallas_call(
-        all_terms,
-        out_shape=jax.ShapeDtypeStruct((half, columns), bf16),
-        in_specs=[IN_VMEM] * 3,
+        grad_terms,
+        out_shape=jax.ShapeDtypeStruct((chips, (own_rows * columns + piece * rank) // LANES, LANES), bf16),
+        in_specs=[IN_VMEM, IN_VMEM, IN_HBM, IN_VMEM],
         out_specs=IN_VMEM,
-        compiler_params=params(),
-        cost_estimate=cost(rank * tokens * columns, 4 << 20),
-    )(own, summed, other)
-    terms = lax.all_to_all(terms.reshape(chips, own_rows, columns), "chip", 0, 0, tiled=True)
+        scratch_shapes=[
+            pltpu.VMEM((tokens, columns), bf16),
+            pltpu.VMEM((half, columns), f32),
+            pltpu.SemaphoreType.DMA,
+        ],
+        compiler_params=params(GRAD_LIMIT),
+        cost_estimate=cost(2 * rank * tokens * columns, 5 << 20),
+    )(summed, cotangent, other_cot, pieces)
+    terms = lax.all_to_all(terms, "chip", 0, 0, tiled=True)
 
     moment_next, square_next, copies = pl.pallas_call(
         adam,
@@ -202,9 +231,10 @@
         out_shape=(pltpu.VMEM((rows, columns), f32), pltpu.VMEM((rows, half), bf16)),
         in_specs=[IN_SMEM, IN_VMEM, IN_VMEM],
         out_specs=(IN_VMEM, IN_VMEM),
+        scratch_shapes=[pltpu.VMEM((rows, rank), bf16)],
         compiler_params=params(),
         cost_estimate=cost(rows * rank * columns, 3 << 20),
-    )(core, summed, mine)
+    )(core, terms, mine)
     expanded = pl.pallas_call(
         expand,
         out_shape=jax.ShapeDtypeStruct((rows, columns), bf16),

time: 161 us -> 183 us (1.14)
  Pallas kernels: 10.5 us -> 27.6 us
  starting transfers between devices: 19 us -> 32.4 us
  blocking collectives: 129 us -> 120 us
    pallas_call x2, Pallas kernels: 2.35 us -> 19.5 us  [the longest x1 17.1 us: body(): pl.pallas_call(give_pieces, out_shape=pltpu.HBM((lax.axis_size('fsdp'), p...]
    psum x1, blocking collectives: 96.7 us -> 85.6 us  [body(): summed = lax.psum(partial, 'fsdp').astype(bf16)]
    all_to_all x0 -> x1, starting transfers between devices: none -> 9.55 us  [body(): pieces = lax.all_to_all(pieces, 'fsdp', 0, 0, tiled=True)]
    ppermute x1, starting transfers between devices: 8.33 us -> 11.7 us  [body(): other = lax.ppermute(mine, 'core', SWAP)]
    all_to_all x1, blocking collectives: 18.3 us -> 21 us  [body(): terms = lax.all_to_all(terms, 'chip', 0, 0, tiled=True)]
  transfers between devices with their start and end apart: 3 -> 4, of which waited for: 1 -> 1; matrix products, arithmetic and copies ran while one was open for 0% -> 0% of each run, Pallas kernels for 4% -> 13%
where the time goes in v9:
time: 183 us; the launch traced here: 182 us
  blocking collectives  120 us (66%)
  starting transfers between devices  32.4 us (18%)
  Pallas kernels  27.6 us (15%)
    psum x1, blocking collectives, body(): summed = lax.psum(partial, 'fsdp').astype(bf16)  85.6 us
    all_to_all x1, blocking collectives, body(): terms = lax.all_to_all(terms, 'chip', 0, 0, tiled=True)  21 us
    pallas_call x1, Pallas kernels, body(): pl.pallas_call(give_pieces, out_shape=pltpu.HBM((lax.axis_size('fsdp'), p...  17.1 us
    all_to_all x1, blocking collectives, body(): mine = lax.all_to_all(copies, 'chip', 0, 0, tiled=True)  13.7 us
    ppermute x1, starting transfers between devices, body(): other = lax.ppermute(mine, 'core', SWAP)  11.7 us
    all_to_all x1, starting transfers between devices, body(): pieces = lax.all_to_all(pieces, 'fsdp', 0, 0, tiled=True)  9.55 us
    ppermute x1, starting transfers between devices, body(): other_act = lax.ppermute(activations, 'core', SWAP)  8.92 us
  transfers between devices with their start and end apart: 4, of which 1 were waited for; matrix products, arithmetic and copies ran while one was open for 0% of the time, Pallas kernels for 13%

profile of v9, /device:TPU:1, one launch (start us, length us, event | category | flops | bytes accessed | tf_op | source)
XLA Modules:
  0.0 182.2 jit_solution(7653230662959351237)
XLA Ops:
  0.6 0.0 copy-start
  0.6 8.9 %collective-permute-start = (bf16[768,512]{1,0:T(8,128)(2,1)}, bf16[768,512]{1,0:T(8,128)(2,1)S(1)}, u32[]{:S(2)}, u32[]{:S(2)}) collective-permute-start(bf16[768,512]{1,0:T(8,128)(2,1)} %act_hbm.1), channel_id=1, source_target_pairs={{0,16},{16,0},{1,17},{17,1},{2,18},{18,2},{3,19},{19,3},{4,20},{20... | collective-permute-start | bytes 2359304 | tf_op jit(solution)/shard_map/ppermute | solution.py:169
  9.6 17.1 %shard_map.78 = bf16[16,16,1024]{2,1,0:T(8,128)(2,1)} custom-call(s32[1]{0:T(128)} %bitcast.core_ref, s32[1]{0:T(128)} %bitcast.1.chip_ref, bf16[512,1024]{1,0:T(8,128)(2,1)} %basis_hbm.3), custom_call_target="tpu_custom_call" | custom-call | bytes 1048576 | tf_op jit(solution)/shard_map/pallas_call | solution.py:158
  26.7 9.6 %all-to-all-start = ((bf16[16,16,1024]{2,1,0:T(8,128)(2,1)}), bf16[16,16,1024]{2,1,0:T(8,128)(2,1)S(1)}, u32[]{:S(2)}, u32[]{:S(2)}) async-start(bf16[16,16,1024]{2,1,0:T(8,128)(2,1)} %shard_map.78), calls=%async_computation | async-start | bytes 1048576 | tf_op jit(solution)/shard_map/all_to_all | solution.py:167
  36.3 0.0 copy-done
  36.3 2.2 %collective-permute-start.1 = (bf16[768,896]{1,0:T(8,128)(2,1)S(1)}, bf16[768,896]{1,0:T(8,128)(2,1)}, u32[]{:S(2)}, u32[]{:S(2)}) collective-permute-start(bf16[768,896]{1,0:T(8,128)(2,1)S(1)} %copy-done), channel_id=1, source_target_pairs={{0,16},{16,0},{1,17},{17,1},{2,18},{18,2},{3,19},{19,3},{4,20},{20... | collective-permute-start | bytes 4128776 | tf_op jit(solution)/shard_map/ppermute | solution.py:170
  38.5 3.4 %shard_map.76 = (f32[512,1536]{1,0:T(8,128)}, bf16[512,512]{1,0:T(8,128)(2,1)S(1)}) custom-call(s32[1]{0:T(128)} %bitcast.core_ref, bf16[512,1024]{1,0:T(8,128)(2,1)} %basis_hbm.3, bf16[768,512]{1,0:T(8,128)(2,1)} %act_hbm.1), custom_call_target="tpu_custom_call" | custom-call | flops 805306368 | bytes 5242880 | tf_op jit(solution)/shard_map/pallas_call | solution.py:172
  41.9 0.0 collective-permute-done.act_ref
  41.9 1.7 shard_map.77
  43.6 85.6 %all-reduce.1.summed_ref = bf16[512,1536]{1,0:T(8,128)(2,1)S(1)} all-reduce(f32[512,1536]{1,0:T(8,128)} %shard_map.77), channel_id=1, replica_groups=mesh['chip'=16,'core'=2,'fsdp'=16] {'fsdp'}, use_global_device_ids=true, to_apply=%region_0.0 | all-reduce | flops 786432 | bytes 4718592 | tf_op jit(solution)/shard_map/psum | solution.py:197
  129.2 0.0 collective-permute-done.1.other_hbm
  129.2 0.0 all-to-all-done.pieces_ref
  129.2 2.4 %shard_map.79 = bf16[16,352,128]{2,1,0:T(8,128)(2,1)S(1)} custom-call(bf16[512,1536]{1,0:T(8,128)(2,1)S(1)} %all-reduce.1.summed_ref, bf16[768,896]{1,0:T(8,128)(2,1)S(1)} %copy-done, bf16[768,896]{1,0:T(8,128)(2,1)} %collective-permute-done.1.other_hbm, bf16[16,16,1024]{2,1,0:T(8,128)(2,1)S(1)} %all-to-all-done.pieces_ref), custom_call_target="tpu_custom_call" | custom-call | flops 1409286144 | bytes 5242880 | tf_op jit(solution)/shard_map/pallas_call | solution.py:199
  131.6 0.0 copy-start.1
  131.6 0.0 copy-start.2
  131.6 21.0 %all_to_all.15.terms_ref = bf16[16,352,128]{2,1,0:T(8,128)(2,1)S(1)} all-to-all(bf16[16,352,128]{2,1,0:T(8,128)(2,1)S(1)} %shard_map.79), channel_id=1, replica_groups=mesh['chip'=16,'core'=2,'fsdp'=16] {'chip'}, dimensions={0} | all-to-all | bytes 2883584 | tf_op jit(solution)/shard_map/all_to_all | solution.py:212
  152.6 0.0 copy-done.1
  152.6 0.0 copy-done.2
  152.6 0.9 shard_map.80
  153.5 13.7 %all_to_all.16.mine_ref = bf16[16,32,896]{2,1,0:T(8,128)(2,1)S(1)} all-to-all(bf16[16,32,896]{2,1,0:T(8,128)(2,1)S(1)} %get-tuple-element.14), channel_id=1, replica_groups=mesh['chip'=16,'core'=2,'fsdp'=16] {'chip'}, dimensions={0} | all-to-all | bytes 1835008 | tf_op jit(solution)/shard_map/all_to_all | solution.py:226
  167.2 11.7 %collective-permute-start.2 = (bf16[16,32,896]{2,1,0:T(8,128)(2,1)S(1)}, bf16[16,32,896]{2,1,0:T(8,128)(2,1)S(1)}, u32[]{:S(2)}, u32[]{:S(2)}) collective-permute-start(bf16[16,32,896]{2,1,0:T(8,128)(2,1)S(1)} %all_to_all.16.mine_ref), channel_id=1, source_target_pairs={{0,16},{16,0},{1,17},{17,1},{2,18},{18,2},{3,19},{19,3},{4,20},{20... | collective-permute-start | bytes 2752520 | tf_op jit(solution)/shard_map/ppermute | solution.py:227
  178.9 0.9 shard_map.81
  179.8 1.2 collective-permute-done.2.other_ref
  181.0 1.2 shard_map.82
Async XLA Ops:
  0.6 35.6 %copy-start = (bf16[768,896]{1,0:T(8,128)(2,1)S(1)}, bf16[768,896]{1,0:T(8,128)(2,1)}, u32[]{:S(2)}) copy-start(bf16[768,896]{1,0:T(8,128)(2,1)} %own_ref.1) | copy-start | bytes 4128772
  0.6 41.2 %collective-permute-start = (bf16[768,512]{1,0:T(8,128)(2,1)}, bf16[768,512]{1,0:T(8,128)(2,1)S(1)}, u32[]{:S(2)}, u32[]{:S(2)}) collective-permute-start(bf16[768,512]{1,0:T(8,128)(2,1)} %act_hbm.1), channel_id=1, source_target_pairs={{0,16},{16,0},{1,17},{17,1},{2,18},{18,2},{3,19},{19,3},{4,20},{20... | collective-permute-start | bytes 2359304 | tf_op jit(solution)/shard_map/ppermute | solution.py:169
  26.7 102.5 %all-to-all-start = ((bf16[16,16,1024]{2,1,0:T(8,128)(2,1)}), bf16[16,16,1024]{2,1,0:T(8,128)(2,1)S(1)}, u32[]{:S(2)}, u32[]{:S(2)}) async-start(bf16[16,16,1024]{2,1,0:T(8,128)(2,1)} %shard_map.78), calls=%async_computation | async-start | bytes 1048576 | tf_op jit(solution)/shard_map/all_to_all | solution.py:167
  36.3 92.9 %collective-permute-start.1 = (bf16[768,896]{1,0:T(8,128)(2,1)S(1)}, bf16[768,896]{1,0:T(8,128)(2,1)}, u32[]{:S(2)}, u32[]{:S(2)}) collective-permute-start(bf16[768,896]{1,0:T(8,128)(2,1)S(1)} %copy-done), channel_id=1, source_target_pairs={{0,16},{16,0},{1,17},{17,1},{2,18},{18,2},{3,19},{19,3},{4,20},{20... | collective-permute-start | bytes 4128776 | tf_op jit(solution)/shard_map/ppermute | solution.py:170
  131.6 21.0 %copy-start.1 = (f32[32,896]{1,0:T(8,128)S(1)}, f32[32,896]{1,0:T(8,128)}, u32[]{:S(2)}) copy-start(f32[32,896]{1,0:T(8,128)} %first_ref.1) | copy-start | bytes 344068
  131.6 21.0 %copy-start.2 = (f32[32,896]{1,0:T(8,128)S(1)}, f32[32,896]{1,0:T(8,128)}, u32[]{:S(2)}) copy-start(f32[32,896]{1,0:T(8,128)} %second_ref.1) | copy-start | bytes 344068
  167.2 13.8 %collective-permute-start.2 = (bf16[16,32,896]{2,1,0:T(8,128)(2,1)S(1)}, bf16[16,32,896]{2,1,0:T(8,128)(2,1)S(1)}, u32[]{:S(2)}, u32[]{:S(2)}) collective-permute-start(bf16[16,32,896]{2,1,0:T(8,128)(2,1)S(1)} %all_to_all.16.mine_ref), channel_id=1, source_target_pairs={{0,16},{16,0},{1,17},{17,1},{2,18},{18,2},{3,19},{19,3},{4,20},{20... | collective-permute-start | bytes 2752520 | tf_op jit(solution)/shard_map/ppermute | solution.py:227

commit v10 on v8

--- a/solution.py
+++ b/solution.py
@@ -12,6 +12,7 @@
 
 SWAP = [(0, 1), (1, 0)]
 VMEM_LIMIT = 40 * 1024 * 1024
+OWN_LIMIT = 60 * 1024 * 1024
 LAST = (((1,), (1,)), ((), ()))
 IN_VMEM = pl.BlockSpec(memory_space=pltpu.VMEM)
 IN_HBM = pl.BlockSpec(memory_space=pltpu.HBM)
@@ -26,22 +27,8 @@
     return pl.CostEstimate(flops=flops, bytes_accessed=moved, transcendentals=0)
 
 
-def project_rows(picked, act_ref, out_ref, out_hbm, sems):
-    part = out_ref.shape[0] // 2
-    copies = []
-    for i in range(2):
-        rows = pl.ds(i * part, part)
-        out_ref[rows, :] = lax.dot_general(
-            picked[i * part : (i + 1) * part], act_ref[...], LAST, preferred_element_type=jnp.float32
-        )
-        copies.append(pltpu.make_async_copy(out_ref.at[rows, :], out_hbm.at[rows, :], sems.at[i]))
-        copies[i].start()
-    return copies
-
-
-def project_own(core_ref, holds_ref, basis_hbm, act_hbm, out_hbm, picked_ref, basis_ref, act_ref, turned_ref, own_ref, block_ref, sems):
+def project_own(core_ref, holds_ref, basis_hbm, act_hbm, own_ref, block_ref, picked_ref, basis_ref, act_ref, turned_ref, sems):
     features, rank = basis_ref.shape
-    tokens = act_ref.shape[0]
     half = rank // 2
     rows = features // 2
     load_basis = pltpu.make_async_copy(basis_hbm, basis_ref, sems.at[0])
@@ -53,20 +40,30 @@
     mine = jnp.where(holds_ref[0] == 1, mine, 0.0)
     block_ref[:rows, :] = mine[:, :half]
     block_ref[rows:, :] = mine[:, half:]
-    save_block = pltpu.make_async_copy(block_ref, out_hbm.at[:, pl.ds(2 * tokens, half)], sems.at[2])
-    save_block.start()
     turned_ref[...] = basis_ref[...].T.reshape(turned_ref.shape)
     picked = turned_ref[:, pl.ds(core_ref[0], 1)].reshape(half, features)
     picked_ref[...] = picked
     load_act.wait()
-    copies = project_rows(picked, act_ref, own_ref, out_hbm.at[:, pl.ds(0, tokens)], sems.at[pl.ds(3, 2)])
-    for copy in [save_block] + copies:
-        copy.wait()
-
-
-def project_other(picked_ref, act_ref, _, out_hbm, other_ref, sems):
+    own_ref[...] = lax.dot_general(picked, act_ref[...], LAST, preferred_element_type=jnp.float32)
+
+
+def project_other(picked_ref, act_ref, own_ref, block_ref, out_hbm, other_ref, sems):
     tokens = act_ref.shape[0]
-    copies = project_rows(picked_ref[...], act_ref, other_ref, out_hbm.at[:, pl.ds(tokens, tokens)], sems)
+    half = block_ref.shape[0]
+    copies = [
+        pltpu.make_async_copy(own_ref, out_hbm.at[:, pl.ds(0, tokens)], sems.at[0]),
+        pltpu.make_async_copy(block_ref, out_hbm.at[:, pl.ds(2 * tokens, half)], sems.at[1]),
+    ]
+    for copy in copies:
+        copy.start()
+    part = half // 2
+    for i in range(2):
+        rows = pl.ds(i * part, part)
+        other_ref[rows, :] = lax.dot_general(picked_ref[rows, :], act_ref[...], LAST, preferred_element_type=jnp.float32)
+        copies.append(
+            pltpu.make_async_copy(other_ref.at[rows, :], out_hbm.at[rows, pl.ds(tokens, tokens)], sems.at[2 + i])
+        )
+        copies[-1].start()
     for copy in copies:
         copy.wait()
 
@@ -98,7 +95,13 @@
         copies_ref[i] = direction
 
 
-def expand_own(core_ref, summed_ref, mine_ref, out_ref, rest_ref):
+def expand_own(core_ref, summed_ref, mine_ref, moment_ref, square_ref, out_ref, rest_ref, moment_hbm, square_hbm, sems):
+    saves = [
+        pltpu.make_async_copy(moment_ref, moment_hbm, sems.at[0]),
+        pltpu.make_async_copy(square_ref, square_hbm, sems.at[1]),
+    ]
+    for save in saves:
+        save.start()
     rows, half = rest_ref.shape
     own_rows = mine_ref.shape[1]
     start = summed_ref.shape[1] - half
@@ -114,6 +117,8 @@
     direction = mine_ref[...].reshape(half, mine_ref.shape[2])
     out_ref[...] = jnp.dot(columns_of(core_ref[0]), direction, preferred_element_type=jnp.float32)
     rest_ref[...] = columns_of(1 - core_ref[0])
+    for save in saves:
+        save.wait()
 
 
 def expand(own_ref, rest_ref, other_ref, out_ref):
@@ -135,32 +140,33 @@
     other_act = lax.ppermute(activations, "core", SWAP)
     other_cot = lax.ppermute(cotangent, "core", SWAP)
     width = 2 * tokens + half
-    partial, picked = pl.pallas_call(
+    own, block, picked = pl.pallas_call(
         project_own,
-        out_shape=(pltpu.HBM((half, width), f32), pltpu.VMEM((half, features), bf16)),
+        out_shape=(
+            pltpu.VMEM((half, tokens), f32),
+            pltpu.VMEM((half, half), f32),
+            pltpu.VMEM((half, features), bf16),
+        ),
         in_specs=[IN_SMEM, IN_SMEM, IN_HBM, IN_HBM],
-        out_specs=(IN_HBM, IN_VMEM),
+        out_specs=(IN_VMEM,) * 3,
         scratch_shapes=[
             pltpu.VMEM((features, rank), bf16),
             pltpu.VMEM((tokens, features), bf16),
             pltpu.VMEM((chips, 2, own_rows, features), bf16),
-            pltpu.VMEM((half, tokens), f32),
-            pltpu.VMEM((half, half), f32),
-            pltpu.SemaphoreType.DMA((5,)),
+            pltpu.SemaphoreType.DMA((2,)),
         ],
-        compiler_params=params(60 * 1024 * 1024),
+        compiler_params=params(OWN_LIMIT),
         cost_estimate=cost(2 * rank * tokens * features, 5 << 20),
     )(core, holds, basis, activations)
     partial = pl.pallas_call(
         project_other,
         out_shape=pltpu.HBM((half, width), f32),
-        in_specs=[IN_VMEM, IN_VMEM, IN_HBM],
+        in_specs=[IN_VMEM] * 4,
         out_specs=IN_HBM,
-        scratch_shapes=[pltpu.VMEM((half, tokens), f32), pltpu.SemaphoreType.DMA((2,))],
-        input_output_aliases={2: 0},
+        scratch_shapes=[pltpu.VMEM((half, tokens), f32), pltpu.SemaphoreType.DMA((4,))],
         compiler_params=params(),
         cost_estimate=cost(rank * tokens * features, 3 << 20),
-    )(picked, other_act, partial)
+    )(picked, other_act, own, block)
     summed = lax.psum(partial, "fsdp").astype(bf16)
 
     own, other = pl.pallas_call(
@@ -185,8 +191,8 @@
     moment_next, square_next, copies = pl.pallas_call(
         adam,
         out_shape=(
-            jax.ShapeDtypeStruct((own_rows, columns), f32),
-            jax.ShapeDtypeStruct((own_rows, columns), f32),
+            pltpu.VMEM((own_rows, columns), f32),
+            pltpu.VMEM((own_rows, columns), f32),
             jax.ShapeDtypeStruct((chips, own_rows, columns), bf16),
         ),
         in_specs=[IN_VMEM] * 3,
@@ -197,14 +203,20 @@
     mine = lax.all_to_all(copies, "chip", 0, 0, tiled=True)
     other = lax.ppermute(mine, "core", SWAP)
     rows = features // 2
-    own, rest = pl.pallas_call(
+    own, rest, moment_next, square_next = pl.pallas_call(
         expand_own,
-        out_shape=(pltpu.VMEM((rows, columns), f32), pltpu.VMEM((rows, half), bf16)),
-        in_specs=[IN_SMEM, IN_VMEM, IN_VMEM],
-        out_specs=(IN_VMEM, IN_VMEM),
+        out_shape=(
+            pltpu.VMEM((rows, columns), f32),
+            pltpu.VMEM((rows, half), bf16),
+            pltpu.HBM((own_rows, columns), f32),
+            pltpu.HBM((own_rows, columns), f32),
+        ),
+        in_specs=[IN_SMEM] + [IN_VMEM] * 4,
+        out_specs=(IN_VMEM, IN_VMEM, IN_HBM, IN_HBM),
+        scratch_shapes=[pltpu.SemaphoreType.DMA((2,))],
         compiler_params=params(),
         cost_estimate=cost(rows * rank * columns, 3 << 20),
-    )(core, summed, mine)
+    )(core, summed, mine, moment_next, square_next)
     expanded = pl.pallas_call(
         expand,
         out_shape=jax.ShapeDtypeStruct((rows, columns), bf16),

time: 161 us -> 159 us (0.988)
    pallas_call x2, Pallas kernels: 4.35 us -> 2.56 us  [the longest x1 2.36 us: body(): pl.pallas_call(project_own, out_shape=(pltpu.VMEM((half, tokens), f32), p...]
  transfers between devices with their start and end apart: 3 -> 3, of which waited for: 1 -> 1; matrix products, arithmetic and copies ran while one was open for 0% -> 0% of each run, Pallas kernels for 4% -> 3%
where the time goes in v10:
time: 159 us
  blocking collectives  129 us (81%)
  starting transfers between devices  19.1 us (12%)
  Pallas kernels  9.07 us (6%)
    psum x1, blocking collectives, body(): summed = lax.psum(partial, 'fsdp').astype(bf16)  96.7 us
    all_to_all x1, blocking collectives, body(): lax.all_to_all(terms.reshape(chips, own_rows, columns), 'chip', 0, 0, til...  18.3 us
    all_to_all x1, blocking collectives, body(): mine = lax.all_to_all(copies, 'chip', 0, 0, tiled=True)  13.9 us
    ppermute x1, starting transfers between devices, body(): other_act = lax.ppermute(activations, 'core', SWAP)  8.79 us
    ppermute x1, starting transfers between devices, body(): other = lax.ppermute(mine, 'core', SWAP)  8.34 us
  transfers between devices with their start and end apart: 3, of which 1 were waited for; matrix products, arithmetic and copies ran while one was open for 0% of the time, Pallas kernels for 3%

profile of v10, /device:TPU:1, one launch (start us, length us, event | category | flops | bytes accessed | tf_op | source)
XLA Modules:
  0.0 158.9 jit_solution(2835567496940105479)
XLA Ops:
  0.6 8.8 %collective-permute-start = (bf16[768,512]{1,0:T(8,128)(2,1)}, bf16[768,512]{1,0:T(8,128)(2,1)S(1)}, u32[]{:S(2)}, u32[]{:S(2)}) collective-permute-start(bf16[768,512]{1,0:T(8,128)(2,1)} %act_hbm.1), channel_id=1, source_target_pairs={{0,16},{16,0},{1,17},{17,1},{2,18},{18,2},{3,19},{19,3},{4,20},{20... | collective-permute-start | bytes 2359304 | tf_op jit(solution)/shard_map/ppermute | solution.py:140
  9.4 1.9 %collective-permute-start.1 = (bf16[768,896]{1,0:T(8,128)(2,1)}, bf16[768,896]{1,0:T(8,128)(2,1)}, u32[]{:S(2)}, u32[]{:S(2)}) collective-permute-start(bf16[768,896]{1,0:T(8,128)(2,1)} %own_ref.1), channel_id=1, source_target_pairs={{0,16},{16,0},{1,17},{17,1},{2,18},{18,2},{3,19},{19,3},{4,20},{20... | collective-permute-start | bytes 4128776 | tf_op jit(solution)/shard_map/ppermute | solution.py:141
  11.4 2.4 %shard_map.76 = (f32[512,768]{1,0:T(8,128)S(1)}, f32[512,512]{1,0:T(8,128)S(1)}, bf16[512,512]{1,0:T(8,128)(2,1)S(1)}) custom-call(s32[1]{0:T(128)} %bitcast.core_ref, s32[1]{0:T(128)} %bitcast.1.holds_ref, bf16[512,1024]{1,0:T(8,128)(2,1)} %basis_hbm.1, bf16[768,512]{1,0:T(8,128)(2,1)} %act_hbm.1), custom_call_target="tpu_custom_call" | custom-call | flops 805306368 | bytes 5242880 | tf_op jit(solution)/shard_map/pallas_call | solution.py:143
  13.7 0.0 collective-permute-done.act_ref
  13.7 2.1 %shard_map.77 = f32[512,2048]{1,0:T(8,128)} custom-call(bf16[512,512]{1,0:T(8,128)(2,1)S(1)} %get-tuple-element.15.picked_ref, bf16[768,512]{1,0:T(8,128)(2,1)S(1)} %collective-permute-done.act_ref, f32[512,768]{1,0:T(8,128)S(1)} %get-tuple-element.16.own_ref, f32[512,512]{1,0:T(8,128)S(1)} %get-tuple-element.17.block_ref), custom_call_target="tpu_custom_call" | custom-call | flops 402653184 | bytes 3145728 | tf_op jit(solution)/shard_map/pallas_call | solution.py:161
  15.8 0.0 copy-start
  15.8 96.7 %all-reduce.1.summed_ref = bf16[512,2048]{1,0:T(8,128)(2,1)S(1)} all-reduce(f32[512,2048]{1,0:T(8,128)} %shard_map.77), channel_id=1, replica_groups=mesh['chip'=16,'core'=2,'fsdp'=16] {'fsdp'}, use_global_device_ids=true, to_apply=%region_0.0 | all-reduce | flops 1048576 | bytes 6291456 | tf_op jit(solution)/shard_map/psum | solution.py:170
  112.5 0.0 collective-permute-done.1.other_hbm
  112.5 0.0 copy-done
  112.6 1.4 shard_map.78
  113.9 1.0 shard_map.79
  114.9 0.0 copy-start.1
  114.9 0.0 copy-start.2
  114.9 18.3 %all_to_all.10.terms_ref = bf16[16,32,896]{2,1,0:T(8,128)(2,1)S(1)} all-to-all(bf16[16,32,896]{2,1,0:T(8,128)(2,1)S(1)} %bitcast.3), channel_id=1, replica_groups=mesh['chip'=16,'core'=2,'fsdp'=16] {'chip'}, dimensions={0} | all-to-all | bytes 1835008 | tf_op jit(solution)/shard_map/all_to_all | solution.py:189
  133.2 0.0 copy-done.1
  133.2 0.0 copy-done.2
  133.2 0.2 shard_map.80
  133.4 13.9 %all_to_all.11.mine_ref = bf16[16,32,896]{2,1,0:T(8,128)(2,1)S(1)} all-to-all(bf16[16,32,896]{2,1,0:T(8,128)(2,1)S(1)} %get-tuple-element.20), channel_id=1, replica_groups=mesh['chip'=16,'core'=2,'fsdp'=16] {'chip'}, dimensions={0} | all-to-all | bytes 1835008 | tf_op jit(solution)/shard_map/all_to_all | solution.py:203
  147.3 8.3 %collective-permute-start.2 = (bf16[16,32,896]{2,1,0:T(8,128)(2,1)S(1)}, bf16[16,32,896]{2,1,0:T(8,128)(2,1)S(1)}, u32[]{:S(2)}, u32[]{:S(2)}) collective-permute-start(bf16[16,32,896]{2,1,0:T(8,128)(2,1)S(1)} %all_to_all.11.mine_ref), channel_id=1, source_target_pairs={{0,16},{16,0},{1,17},{17,1},{2,18},{18,2},{3,19},{19,3},{4,20},{20... | collective-permute-start | bytes 2752520 | tf_op jit(solution)/shard_map/ppermute | solution.py:204
  155.7 0.9 shard_map.81
  156.5 1.2 collective-permute-done.2.other_ref
  157.7 1.2 shard_map.82
Async XLA Ops:
  0.6 13.1 %collective-permute-start = (bf16[768,512]{1,0:T(8,128)(2,1)}, bf16[768,512]{1,0:T(8,128)(2,1)S(1)}, u32[]{:S(2)}, u32[]{:S(2)}) collective-permute-start(bf16[768,512]{1,0:T(8,128)(2,1)} %act_hbm.1), channel_id=1, source_target_pairs={{0,16},{16,0},{1,17},{17,1},{2,18},{18,2},{3,19},{19,3},{4,20},{20... | collective-permute-start | bytes 2359304 | tf_op jit(solution)/shard_map/ppermute | solution.py:140
  9.4 103.1 %collective-permute-start.1 = (bf16[768,896]{1,0:T(8,128)(2,1)}, bf16[768,896]{1,0:T(8,128)(2,1)}, u32[]{:S(2)}, u32[]{:S(2)}) collective-permute-start(bf16[768,896]{1,0:T(8,128)(2,1)} %own_ref.1), channel_id=1, source_target_pairs={{0,16},{16,0},{1,17},{17,1},{2,18},{18,2},{3,19},{19,3},{4,20},{20... | collective-permute-start | bytes 4128776 | tf_op jit(solution)/shard_map/ppermute | solution.py:141
  15.8 96.7 %copy-start = (bf16[768,896]{1,0:T(8,128)(2,1)S(1)}, bf16[768,896]{1,0:T(8,128)(2,1)}, u32[]{:S(2)}) copy-start(bf16[768,896]{1,0:T(8,128)(2,1)} %own_ref.1) | copy-start | bytes 4128772
  114.9 18.3 %copy-start.1 = (f32[32,896]{1,0:T(8,128)S(1)}, f32[32,896]{1,0:T(8,128)}, u32[]{:S(2)}) copy-start(f32[32,896]{1,0:T(8,128)} %first_ref.1) | copy-start | bytes 344068
  114.9 18.3 %copy-start.2 = (f32[32,896]{1,0:T(8,128)S(1)}, f32[32,896]{1,0:T(8,128)}, u32[]{:S(2)}) copy-start(f32[32,896]{1,0:T(8,128)} %second_ref.1) | copy-start | bytes 344068
  147.3 10.4 %collective-permute-start.2 = (bf16[16,32,896]{2,1,0:T(8,128)(2,1)S(1)}, bf16[16,32,896]{2,1,0:T(8,128)(2,1)S(1)}, u32[]{:S(2)}, u32[]{:S(2)}) collective-permute-start(bf16[16,32,896]{2,1,0:T(8,128)(2,1)S(1)} %all_to_all.11.mine_ref), channel_id=1, source_target_pairs={{0,16},{16,0},{1,17},{17,1},{2,18},{18,2},{3,19},{19,3},{4,20},{20... | collective-permute-start | bytes 2752520 | tf_op jit(solution)/shard_map/ppermute | solution.py:204

commit v11 on v10

--- a/solution.py
+++ b/solution.py
@@ -27,41 +27,50 @@
     return pl.CostEstimate(flops=flops, bytes_accessed=moved, transcendentals=0)
 
 
-def project_own(core_ref, holds_ref, basis_hbm, act_hbm, own_ref, block_ref, picked_ref, basis_ref, act_ref, turned_ref, sems):
-    features, rank = basis_ref.shape
-    half = rank // 2
+def project_own(core_ref, holds_ref, basis_hbm, act_hbm, out_hbm, own_ref, picked_ref, basis_ref, act_ref, turned_ref, block_ref, sems):
+    tokens, features = act_ref.shape
+    parts, _, wide = basis_ref.shape
     rows = features // 2
-    load_basis = pltpu.make_async_copy(basis_hbm, basis_ref, sems.at[0])
-    load_act = pltpu.make_async_copy(act_hbm, act_ref, sems.at[1])
-    load_basis.start()
+    groups = turned_ref.shape[0] // parts
+    size = picked_ref.shape[0] // parts
+    first = pl.multiple_of(core_ref[0] * rows, rows)
+    loads = [pltpu.make_async_copy(basis_hbm.at[:, pl.ds(i * wide, wide)], basis_ref.at[i], sems.at[i]) for i in range(parts)]
+    load_act = pltpu.make_async_copy(act_hbm, act_ref, sems.at[parts])
+    loads[0].start()
     load_act.start()
-    load_basis.wait()
-    mine = basis_ref[pl.ds(pl.multiple_of(core_ref[0] * rows, rows), rows), :].astype(jnp.float32)
-    mine = jnp.where(holds_ref[0] == 1, mine, 0.0)
-    block_ref[:rows, :] = mine[:, :half]
-    block_ref[rows:, :] = mine[:, half:]
-    turned_ref[...] = basis_ref[...].T.reshape(turned_ref.shape)
-    picked = turned_ref[:, pl.ds(core_ref[0], 1)].reshape(half, features)
-    picked_ref[...] = picked
-    load_act.wait()
-    own_ref[...] = lax.dot_general(picked, act_ref[...], LAST, preferred_element_type=jnp.float32)
-
-
-def project_other(picked_ref, act_ref, own_ref, block_ref, out_hbm, other_ref, sems):
-    tokens = act_ref.shape[0]
-    half = block_ref.shape[0]
-    copies = [
-        pltpu.make_async_copy(own_ref, out_hbm.at[:, pl.ds(0, tokens)], sems.at[0]),
-        pltpu.make_async_copy(block_ref, out_hbm.at[:, pl.ds(2 * tokens, half)], sems.at[1]),
-    ]
-    for copy in copies:
-        copy.start()
+    for load in loads[1:]:
+        load.start()
+    saves = []
+    for i in range(parts):
+        loads[i].wait()
+        mine = basis_ref[i, pl.ds(first, rows), :].astype(jnp.float32)
+        here = pl.ds(i * rows, rows)
+        block_ref[here, :] = jnp.where(holds_ref[0] == 1, mine, 0.0)
+        saves.append(
+            pltpu.make_async_copy(block_ref.at[here, :], out_hbm.at[here, pl.ds(2 * tokens, wide)], sems.at[parts + 1 + i])
+        )
+        saves[i].start()
+        these = pl.ds(i * groups, groups)
+        turned_ref[these] = basis_ref[i].T.reshape(groups, *turned_ref.shape[1:])
+        picked = turned_ref[these, pl.ds(core_ref[0], 1)].reshape(size, features)
+        picked_ref[pl.ds(i * size, size), :] = picked
+        if i == 0:
+            load_act.wait()
+        own_ref[pl.ds(i * size, size), :] = lax.dot_general(picked, act_ref[...], LAST, preferred_element_type=jnp.float32)
+    for save in saves:
+        save.wait()
+
+
+def project_other(picked_ref, act_ref, own_ref, _, out_hbm, other_ref, sems):
+    half, tokens = own_ref.shape
+    copies = [pltpu.make_async_copy(own_ref, out_hbm.at[:, pl.ds(0, tokens)], sems.at[0])]
+    copies[0].start()
     part = half // 2
     for i in range(2):
         rows = pl.ds(i * part, part)
         other_ref[rows, :] = lax.dot_general(picked_ref[rows, :], act_ref[...], LAST, preferred_element_type=jnp.float32)
         copies.append(
-            pltpu.make_async_copy(other_ref.at[rows, :], out_hbm.at[rows, pl.ds(tokens, tokens)], sems.at[2 + i])
+            pltpu.make_async_copy(other_ref.at[rows, :], out_hbm.at[rows, pl.ds(tokens, tokens)], sems.at[1 + i])
         )
         copies[-1].start()
     for copy in copies:
@@ -121,10 +130,18 @@
         save.wait()
 
 
-def expand(own_ref, rest_ref, other_ref, out_ref):
+def expand(own_ref, rest_ref, other_ref, out_hbm, out_ref, sems):
     direction = other_ref[...].reshape(rest_ref.shape[1], other_ref.shape[2])
-    more = jnp.dot(rest_ref[...], direction, preferred_element_type=jnp.float32)
-    out_ref[...] = (own_ref[...] + more).astype(jnp.bfloat16)
+    part = out_ref.shape[0] // 2
+    saves = []
+    for i in range(2):
+        rows = pl.ds(i * part, part)
+        more = jnp.dot(rest_ref[rows, :], direction, preferred_element_type=jnp.float32)
+        out_ref[rows, :] = (own_ref[rows, :] + more).astype(jnp.bfloat16)
+        saves.append(pltpu.make_async_copy(out_ref.at[rows, :], out_hbm.at[rows, :], sems.at[i]))
+        saves[i].start()
+    for save in saves:
+        save.wait()
 
 
 def body(activations, cotangent, basis, first_moment, second_moment):
@@ -140,20 +157,21 @@
     other_act = lax.ppermute(activations, "core", SWAP)
     other_cot = lax.ppermute(cotangent, "core", SWAP)
     width = 2 * tokens + half
-    own, block, picked = pl.pallas_call(
+    partial, own, picked = pl.pallas_call(
         project_own,
         out_shape=(
+            pltpu.HBM((half, width), f32),
             pltpu.VMEM((half, tokens), f32),
-            pltpu.VMEM((half, half), f32),
             pltpu.VMEM((half, features), bf16),
         ),
         in_specs=[IN_SMEM, IN_SMEM, IN_HBM, IN_HBM],
-        out_specs=(IN_VMEM,) * 3,
+        out_specs=(IN_HBM, IN_VMEM, IN_VMEM),
         scratch_shapes=[
-            pltpu.VMEM((features, rank), bf16),
+            pltpu.VMEM((2, features, half), bf16),
             pltpu.VMEM((tokens, features), bf16),
             pltpu.VMEM((chips, 2, own_rows, features), bf16),
-            pltpu.SemaphoreType.DMA((2,)),
+            pltpu.VMEM((features, half), f32),
+            pltpu.SemaphoreType.DMA((5,)),
         ],
         compiler_params=params(OWN_LIMIT),
         cost_estimate=cost(2 * rank * tokens * features, 5 << 20),
@@ -161,12 +179,13 @@
     partial = pl.pallas_call(
         project_other,
         out_shape=pltpu.HBM((half, width), f32),
-        in_specs=[IN_VMEM] * 4,
+        in_specs=[IN_VMEM] * 3 + [IN_HBM],
         out_specs=IN_HBM,
-        scratch_shapes=[pltpu.VMEM((half, tokens), f32), pltpu.SemaphoreType.DMA((4,))],
+        scratch_shapes=[pltpu.VMEM((half, tokens), f32), pltpu.SemaphoreType.DMA((3,))],
+        input_output_aliases={3: 0},
         compiler_params=params(),
         cost_estimate=cost(rank * tokens * features, 3 << 20),
-    )(picked, other_act, own, block)
+    )(picked, other_act, own, partial)
     summed = lax.psum(partial, "fsdp").astype(bf16)
 
     own, other = pl.pallas_call(
@@ -219,9 +238,10 @@
     )(core, summed, mine, moment_next, square_next)
     expanded = pl.pallas_call(
         expand,
-        out_shape=jax.ShapeDtypeStruct((rows, columns), bf16),
+        out_shape=pltpu.HBM((rows, columns), bf16),
         in_specs=[IN_VMEM] * 3,
-        out_specs=IN_VMEM,
+        out_specs=IN_HBM,
+        scratch_shapes=[pltpu.VMEM((rows, columns), bf16), pltpu.SemaphoreType.DMA((2,))],
         compiler_params=params(),
         cost_estimate=cost(rows * rank * columns, 3 << 20),
     )(own, rest, other)

time: 159 us -> 160 us (level)
  transfers between devices with their start and end apart: 3 -> 3, of which waited for: 1 -> 1; matrix products, arithmetic and copies ran while one was open for 0% -> 0% of each run, Pallas kernels for 3% -> 4%
where the time goes in v11:
time: 160 us; the launch traced here: 159 us
  blocking collectives  129 us (81%)
  starting transfers between devices  19 us (12%)
  Pallas kernels  9.56 us (6%)
    psum x1, blocking collectives, body(): summed = lax.psum(partial, 'fsdp').astype(bf16)  96.7 us
    all_to_all x1, blocking collectives, body(): lax.all_to_all(terms.reshape(chips, own_rows, columns), 'chip', 0, 0, til...  18.3 us
    all_to_all x1, blocking collectives, body(): mine = lax.all_to_all(copies, 'chip', 0, 0, tiled=True)  13.9 us
    ppermute x1, starting transfers between devices, body(): other_act = lax.ppermute(activations, 'core', SWAP)  8.79 us
    ppermute x1, starting transfers between devices, body(): other = lax.ppermute(mine, 'core', SWAP)  8.33 us
    pallas_call x1, Pallas kernels, body(): pl.pallas_call(project_own, out_shape=(pltpu.HBM((half, width), f32), plt...  3.23 us
  transfers between devices with their start and end apart: 3, of which 1 were waited for; matrix products, arithmetic and copies ran while one was open for 0% of the time, Pallas kernels for 4%

profile of v11, /device:TPU:1, one launch (start us, length us, event | category | flops | bytes accessed | tf_op | source)
XLA Modules:
  0.0 159.5 jit_solution(15480759149844905444)
XLA Ops:
  0.6 8.8 %collective-permute-start = (bf16[768,512]{1,0:T(8,128)(2,1)}, bf16[768,512]{1,0:T(8,128)(2,1)S(1)}, u32[]{:S(2)}, u32[]{:S(2)}) collective-permute-start(bf16[768,512]{1,0:T(8,128)(2,1)} %act_hbm.1), channel_id=1, source_target_pairs={{0,16},{16,0},{1,17},{17,1},{2,18},{18,2},{3,19},{19,3},{4,20},{20... | collective-permute-start | bytes 2359304 | tf_op jit(solution)/shard_map/ppermute | solution.py:157
  9.4 1.9 %collective-permute-start.1 = (bf16[768,896]{1,0:T(8,128)(2,1)}, bf16[768,896]{1,0:T(8,128)(2,1)}, u32[]{:S(2)}, u32[]{:S(2)}) collective-permute-start(bf16[768,896]{1,0:T(8,128)(2,1)} %own_ref.1), channel_id=1, source_target_pairs={{0,16},{16,0},{1,17},{17,1},{2,18},{18,2},{3,19},{19,3},{4,20},{20... | collective-permute-start | bytes 4128776 | tf_op jit(solution)/shard_map/ppermute | solution.py:158
  11.4 3.2 %shard_map.76 = (f32[512,2048]{1,0:T(8,128)}, f32[512,768]{1,0:T(8,128)S(1)}, bf16[512,512]{1,0:T(8,128)(2,1)S(1)}) custom-call(s32[1]{0:T(128)} %bitcast.core_ref, s32[1]{0:T(128)} %bitcast.1.holds_ref, bf16[512,1024]{1,0:T(8,128)(2,1)} %basis_hbm.1, bf16[768,512]{1,0:T(8,128)(2,1)} %act_hbm.1), custom_call_target="tpu_custom_call" | custom-call | flops 805306368 | bytes 5242880 | tf_op jit(solution)/shard_map/pallas_call | solution.py:160
  14.6 0.0 collective-permute-done.act_ref
  14.6 1.8 %shard_map.77 = f32[512,2048]{1,0:T(8,128)} custom-call(bf16[512,512]{1,0:T(8,128)(2,1)S(1)} %get-tuple-element.15.picked_ref, bf16[768,512]{1,0:T(8,128)(2,1)S(1)} %collective-permute-done.act_ref, f32[512,768]{1,0:T(8,128)S(1)} %get-tuple-element.16.own_ref, f32[512,2048]{1,0:T(8,128)} %get-tuple-element.17._), custom_call_target="tpu_custom_call", output_to_operand_aliasing={{}: (3, {})} | custom-call | flops 402653184 | bytes 3145728 | tf_op jit(solution)/shard_map/pallas_call | solution.py:179
  16.4 0.0 copy-start
  16.4 96.7 %all-reduce.1.summed_ref = bf16[512,2048]{1,0:T(8,128)(2,1)S(1)} all-reduce(f32[512,2048]{1,0:T(8,128)} %shard_map.77), channel_id=1, replica_groups=mesh['chip'=16,'core'=2,'fsdp'=16] {'fsdp'}, use_global_device_ids=true, to_apply=%region_0.0 | all-reduce | flops 1048576 | bytes 6291456 | tf_op jit(solution)/shard_map/psum | solution.py:189
  113.1 0.0 collective-permute-done.1.other_hbm
  113.1 0.0 copy-done
  113.1 1.4 shard_map.78
  114.5 1.0 shard_map.79
  115.5 0.0 copy-start.1
  115.5 0.0 copy-start.2
  115.5 18.3 %all_to_all.10.terms_ref = bf16[16,32,896]{2,1,0:T(8,128)(2,1)S(1)} all-to-all(bf16[16,32,896]{2,1,0:T(8,128)(2,1)S(1)} %bitcast.3), channel_id=1, replica_groups=mesh['chip'=16,'core'=2,'fsdp'=16] {'chip'}, dimensions={0} | all-to-all | bytes 1835008 | tf_op jit(solution)/shard_map/all_to_all | solution.py:208
  133.8 0.0 copy-done.1
  133.8 0.0 copy-done.2
  133.8 0.2 shard_map.80
  134.0 13.9 %all_to_all.11.mine_ref = bf16[16,32,896]{2,1,0:T(8,128)(2,1)S(1)} all-to-all(bf16[16,32,896]{2,1,0:T(8,128)(2,1)S(1)} %get-tuple-element.20), channel_id=1, replica_groups=mesh['chip'=16,'core'=2,'fsdp'=16] {'chip'}, dimensions={0} | all-to-all | bytes 1835008 | tf_op jit(solution)/shard_map/all_to_all | solution.py:222
  147.9 8.3 %collective-permute-start.2 = (bf16[16,32,896]{2,1,0:T(8,128)(2,1)S(1)}, bf16[16,32,896]{2,1,0:T(8,128)(2,1)S(1)}, u32[]{:S(2)}, u32[]{:S(2)}) collective-permute-start(bf16[16,32,896]{2,1,0:T(8,128)(2,1)S(1)} %all_to_all.11.mine_ref), channel_id=1, source_target_pairs={{0,16},{16,0},{1,17},{17,1},{2,18},{18,2},{3,19},{19,3},{4,20},{20... | collective-permute-start | bytes 2752520 | tf_op jit(solution)/shard_map/ppermute | solution.py:223
  156.2 0.9 shard_map.81
  157.1 1.2 collective-permute-done.2.other_ref
  158.3 1.2 shard_map.82
Async XLA Ops:
  0.6 14.0 %collective-permute-start = (bf16[768,512]{1,0:T(8,128)(2,1)}, bf16[768,512]{1,0:T(8,128)(2,1)S(1)}, u32[]{:S(2)}, u32[]{:S(2)}) collective-permute-start(bf16[768,512]{1,0:T(8,128)(2,1)} %act_hbm.1), channel_id=1, source_target_pairs={{0,16},{16,0},{1,17},{17,1},{2,18},{18,2},{3,19},{19,3},{4,20},{20... | collective-permute-start | bytes 2359304 | tf_op jit(solution)/shard_map/ppermute | solution.py:157
  9.4 103.7 %collective-permute-start.1 = (bf16[768,896]{1,0:T(8,128)(2,1)}, bf16[768,896]{1,0:T(8,128)(2,1)}, u32[]{:S(2)}, u32[]{:S(2)}) collective-permute-start(bf16[768,896]{1,0:T(8,128)(2,1)} %own_ref.1), channel_id=1, source_target_pairs={{0,16},{16,0},{1,17},{17,1},{2,18},{18,2},{3,19},{19,3},{4,20},{20... | collective-permute-start | bytes 4128776 | tf_op jit(solution)/shard_map/ppermute | solution.py:158
  16.4 96.7 %copy-start = (bf16[768,896]{1,0:T(8,128)(2,1)S(1)}, bf16[768,896]{1,0:T(8,128)(2,1)}, u32[]{:S(2)}) copy-start(bf16[768,896]{1,0:T(8,128)(2,1)} %own_ref.1) | copy-start | bytes 4128772
  115.5 18.3 %copy-start.1 = (f32[32,896]{1,0:T(8,128)S(1)}, f32[32,896]{1,0:T(8,128)}, u32[]{:S(2)}) copy-start(f32[32,896]{1,0:T(8,128)} %first_ref.1) | copy-start | bytes 344068
  115.5 18.3 %copy-start.2 = (f32[32,896]{1,0:T(8,128)S(1)}, f32[32,896]{1,0:T(8,128)}, u32[]{:S(2)}) copy-start(f32[32,896]{1,0:T(8,128)} %second_ref.1) | copy-start | bytes 344068
  147.9 10.4 %collective-permute-start.2 = (bf16[16,32,896]{2,1,0:T(8,128)(2,1)S(1)}, bf16[16,32,896]{2,1,0:T(8,128)(2,1)S(1)}, u32[]{:S(2)}, u32[]{:S(2)}) collective-permute-start(bf16[16,32,896]{2,1,0:T(8,128)(2,1)S(1)} %all_to_all.11.mine_ref), channel_id=1, source_target_pairs={{0,16},{16,0},{1,17},{17,1},{2,18},{18,2},{3,19},{19,3},{4,20},{20... | collective-permute-start | bytes 2752520 | tf_op jit(solution)/shard_map/ppermute | solution.py:223

commit v12 on v11

--- a/solution.py
+++ b/solution.py
@@ -28,37 +28,26 @@
 
 
 def project_own(core_ref, holds_ref, basis_hbm, act_hbm, out_hbm, own_ref, picked_ref, basis_ref, act_ref, turned_ref, block_ref, sems):
-    tokens, features = act_ref.shape
-    parts, _, wide = basis_ref.shape
+    features, rank = basis_ref.shape
+    half = rank // 2
     rows = features // 2
-    groups = turned_ref.shape[0] // parts
-    size = picked_ref.shape[0] // parts
-    first = pl.multiple_of(core_ref[0] * rows, rows)
-    loads = [pltpu.make_async_copy(basis_hbm.at[:, pl.ds(i * wide, wide)], basis_ref.at[i], sems.at[i]) for i in range(parts)]
-    load_act = pltpu.make_async_copy(act_hbm, act_ref, sems.at[parts])
-    loads[0].start()
+    load_basis = pltpu.make_async_copy(basis_hbm, basis_ref, sems.at[0])
+    load_act = pltpu.make_async_copy(act_hbm, act_ref, sems.at[1])
+    load_basis.start()
     load_act.start()
-    for load in loads[1:]:
-        load.start()
-    saves = []
-    for i in range(parts):
-        loads[i].wait()
-        mine = basis_ref[i, pl.ds(first, rows), :].astype(jnp.float32)
-        here = pl.ds(i * rows, rows)
-        block_ref[here, :] = jnp.where(holds_ref[0] == 1, mine, 0.0)
-        saves.append(
-            pltpu.make_async_copy(block_ref.at[here, :], out_hbm.at[here, pl.ds(2 * tokens, wide)], sems.at[parts + 1 + i])
-        )
-        saves[i].start()
-        these = pl.ds(i * groups, groups)
-        turned_ref[these] = basis_ref[i].T.reshape(groups, *turned_ref.shape[1:])
-        picked = turned_ref[these, pl.ds(core_ref[0], 1)].reshape(size, features)
-        picked_ref[pl.ds(i * size, size), :] = picked
-        if i == 0:
-            load_act.wait()
-        own_ref[pl.ds(i * size, size), :] = lax.dot_general(picked, act_ref[...], LAST, preferred_element_type=jnp.float32)
-    for save in saves:
-        save.wait()
+    load_basis.wait()
+    mine = basis_ref[pl.ds(pl.multiple_of(core_ref[0] * rows, rows), rows), :].astype(jnp.float32)
+    mine = jnp.where(holds_ref[0] == 1, mine, 0.0)
+    block_ref[:rows, :] = mine[:, :half]
+    block_ref[rows:, :] = mine[:, half:]
+    save = pltpu.make_async_copy(block_ref, out_hbm.at[:, pl.ds(2 * act_ref.shape[0], half)], sems.at[2])
+    save.start()
+    turned_ref[...] = basis_ref[...].T.reshape(turned_ref.shape)
+    picked = turned_ref[:, pl.ds(core_ref[0], 1)].reshape(half, features)
+    picked_ref[...] = picked
+    load_act.wait()
+    own_ref[...] = lax.dot_general(picked, act_ref[...], LAST, preferred_element_type=jnp.float32)
+    save.wait()
 
 
 def project_other(picked_ref, act_ref, own_ref, _, out_hbm, other_ref, sems):
@@ -167,11 +156,11 @@
         in_specs=[IN_SMEM, IN_SMEM, IN_HBM, IN_HBM],
         out_specs=(IN_HBM, IN_VMEM, IN_VMEM),
         scratch_shapes=[
-            pltpu.VMEM((2, features, half), bf16),
+            pltpu.VMEM((features, rank), bf16),
             pltpu.VMEM((tokens, features), bf16),
             pltpu.VMEM((chips, 2, own_rows, features), bf16),
-            pltpu.VMEM((features, half), f32),
-            pltpu.SemaphoreType.DMA((5,)),
+            pltpu.VMEM((half, half), f32),
+            pltpu.SemaphoreType.DMA((3,)),
         ],
         compiler_params=params(OWN_LIMIT),
         cost_estimate=cost(2 * rank * tokens * features, 5 << 20),

time: 160 us -> 159 us (level)
  transfers between devices with their start and end apart: 3 -> 3, of which waited for: 1 -> 1; matrix products, arithmetic and copies ran while one was open for 0% -> 0% of each run, Pallas kernels for 4% -> 3%
where the time goes in v12:
time: 159 us
  blocking collectives  129 us (81%)
  starting transfers between devices  19 us (12%)
  Pallas kernels  9.09 us (6%)
    psum x1, blocking collectives, body(): summed = lax.psum(partial, 'fsdp').astype(bf16)  96.7 us
    all_to_all x1, blocking collectives, body(): lax.all_to_all(terms.reshape(chips, own_rows, columns), 'chip', 0, 0, til...  18.3 us
    all_to_all x1, blocking collectives, body(): mine = lax.all_to_all(copies, 'chip', 0, 0, tiled=True)  13.9 us
    ppermute x1, starting transfers between devices, body(): other_act = lax.ppermute(activations, 'core', SWAP)  8.79 us
    ppermute x1, starting transfers between devices, body(): other = lax.ppermute(mine, 'core', SWAP)  8.33 us
  transfers between devices with their start and end apart: 3, of which 1 were waited for; matrix products, arithmetic and copies ran while one was open for 0% of the time, Pallas kernels for 3%

profile of v12, /device:TPU:1, one launch (start us, length us, event | category | flops | bytes accessed | tf_op | source)
XLA Modules:
  0.0 159.0 jit_solution(14776120806668962585)
XLA Ops:
  0.6 8.8 %collective-permute-start = (bf16[768,512]{1,0:T(8,128)(2,1)}, bf16[768,512]{1,0:T(8,128)(2,1)S(1)}, u32[]{:S(2)}, u32[]{:S(2)}) collective-permute-start(bf16[768,512]{1,0:T(8,128)(2,1)} %act_hbm.1), channel_id=1, source_target_pairs={{0,16},{16,0},{1,17},{17,1},{2,18},{18,2},{3,19},{19,3},{4,20},{20... | collective-permute-start | bytes 2359304 | tf_op jit(solution)/shard_map/ppermute | solution.py:146
  9.4 1.9 %collective-permute-start.1 = (bf16[768,896]{1,0:T(8,128)(2,1)}, bf16[768,896]{1,0:T(8,128)(2,1)}, u32[]{:S(2)}, u32[]{:S(2)}) collective-permute-start(bf16[768,896]{1,0:T(8,128)(2,1)} %own_ref.1), channel_id=1, source_target_pairs={{0,16},{16,0},{1,17},{17,1},{2,18},{18,2},{3,19},{19,3},{4,20},{20... | collective-permute-start | bytes 4128776 | tf_op jit(solution)/shard_map/ppermute | solution.py:147
  11.4 2.7 %shard_map.76 = (f32[512,2048]{1,0:T(8,128)}, f32[512,768]{1,0:T(8,128)S(1)}, bf16[512,512]{1,0:T(8,128)(2,1)S(1)}) custom-call(s32[1]{0:T(128)} %bitcast.core_ref, s32[1]{0:T(128)} %bitcast.1.holds_ref, bf16[512,1024]{1,0:T(8,128)(2,1)} %basis_hbm.1, bf16[768,512]{1,0:T(8,128)(2,1)} %act_hbm.1), custom_call_target="tpu_custom_call" | custom-call | flops 805306368 | bytes 5242880 | tf_op jit(solution)/shard_map/pallas_call | solution.py:149
  14.1 0.0 collective-permute-done.act_ref
  14.1 1.8 %shard_map.77 = f32[512,2048]{1,0:T(8,128)} custom-call(bf16[512,512]{1,0:T(8,128)(2,1)S(1)} %get-tuple-element.15.picked_ref, bf16[768,512]{1,0:T(8,128)(2,1)S(1)} %collective-permute-done.act_ref, f32[512,768]{1,0:T(8,128)S(1)} %get-tuple-element.16.own_ref, f32[512,2048]{1,0:T(8,128)} %get-tuple-element.17._), custom_call_target="tpu_custom_call", output_to_operand_aliasing={{}: (3, {})} | custom-call | flops 402653184 | bytes 3145728 | tf_op jit(solution)/shard_map/pallas_call | solution.py:168
  15.9 0.0 copy-start
  15.9 96.7 %all-reduce.1.summed_ref = bf16[512,2048]{1,0:T(8,128)(2,1)S(1)} all-reduce(f32[512,2048]{1,0:T(8,128)} %shard_map.77), channel_id=1, replica_groups=mesh['chip'=16,'core'=2,'fsdp'=16] {'fsdp'}, use_global_device_ids=true, to_apply=%region_0.0 | all-reduce | flops 1048576 | bytes 6291456 | tf_op jit(solution)/shard_map/psum | solution.py:178
  112.6 0.0 collective-permute-done.1.other_hbm
  112.6 0.0 copy-done
  112.6 1.4 shard_map.78
  114.0 1.0 shard_map.79
  115.0 0.0 copy-start.1
  115.0 0.0 copy-start.2
  115.0 18.3 %all_to_all.10.terms_ref = bf16[16,32,896]{2,1,0:T(8,128)(2,1)S(1)} all-to-all(bf16[16,32,896]{2,1,0:T(8,128)(2,1)S(1)} %bitcast.3), channel_id=1, replica_groups=mesh['chip'=16,'core'=2,'fsdp'=16] {'chip'}, dimensions={0} | all-to-all | bytes 1835008 | tf_op jit(solution)/shard_map/all_to_all | solution.py:197
  133.3 0.0 copy-done.1
  133.3 0.0 copy-done.2
  133.3 0.2 shard_map.80
  133.5 13.9 %all_to_all.11.mine_ref = bf16[16,32,896]{2,1,0:T(8,128)(2,1)S(1)} all-to-all(bf16[16,32,896]{2,1,0:T(8,128)(2,1)S(1)} %get-tuple-element.20), channel_id=1, replica_groups=mesh['chip'=16,'core'=2,'fsdp'=16] {'chip'}, dimensions={0} | all-to-all | bytes 1835008 | tf_op jit(solution)/shard_map/all_to_all | solution.py:211
  147.4 8.3 %collective-permute-start.2 = (bf16[16,32,896]{2,1,0:T(8,128)(2,1)S(1)}, bf16[16,32,896]{2,1,0:T(8,128)(2,1)S(1)}, u32[]{:S(2)}, u32[]{:S(2)}) collective-permute-start(bf16[16,32,896]{2,1,0:T(8,128)(2,1)S(1)} %all_to_all.11.mine_ref), channel_id=1, source_target_pairs={{0,16},{16,0},{1,17},{17,1},{2,18},{18,2},{3,19},{19,3},{4,20},{20... | collective-permute-start | bytes 2752520 | tf_op jit(solution)/shard_map/ppermute | solution.py:212
  155.7 0.9 shard_map.81
  156.6 1.2 collective-permute-done.2.other_ref
  157.8 1.2 shard_map.82
Async XLA Ops:
  0.6 13.5 %collective-permute-start = (bf16[768,512]{1,0:T(8,128)(2,1)}, bf16[768,512]{1,0:T(8,128)(2,1)S(1)}, u32[]{:S(2)}, u32[]{:S(2)}) collective-permute-start(bf16[768,512]{1,0:T(8,128)(2,1)} %act_hbm.1), channel_id=1, source_target_pairs={{0,16},{16,0},{1,17},{17,1},{2,18},{18,2},{3,19},{19,3},{4,20},{20... | collective-permute-start | bytes 2359304 | tf_op jit(solution)/shard_map/ppermute | solution.py:146
  9.4 103.2 %collective-permute-start.1 = (bf16[768,896]{1,0:T(8,128)(2,1)}, bf16[768,896]{1,0:T(8,128)(2,1)}, u32[]{:S(2)}, u32[]{:S(2)}) collective-permute-start(bf16[768,896]{1,0:T(8,128)(2,1)} %own_ref.1), channel_id=1, source_target_pairs={{0,16},{16,0},{1,17},{17,1},{2,18},{18,2},{3,19},{19,3},{4,20},{20... | collective-permute-start | bytes 4128776 | tf_op jit(solution)/shard_map/ppermute | solution.py:147
  15.9 96.7 %copy-start = (bf16[768,896]{1,0:T(8,128)(2,1)S(1)}, bf16[768,896]{1,0:T(8,128)(2,1)}, u32[]{:S(2)}) copy-start(bf16[768,896]{1,0:T(8,128)(2,1)} %own_ref.1) | copy-start | bytes 4128772
  115.0 18.3 %copy-start.1 = (f32[32,896]{1,0:T(8,128)S(1)}, f32[32,896]{1,0:T(8,128)}, u32[]{:S(2)}) copy-start(f32[32,896]{1,0:T(8,128)} %first_ref.1) | copy-start | bytes 344068
  115.0 18.3 %copy-start.2 = (f32[32,896]{1,0:T(8,128)S(1)}, f32[32,896]{1,0:T(8,128)}, u32[]{:S(2)}) copy-start(f32[32,896]{1,0:T(8,128)} %second_ref.1) | copy-start | bytes 344068
  147.4 10.4 %collective-permute-start.2 = (bf16[16,32,896]{2,1,0:T(8,128)(2,1)S(1)}, bf16[16,32,896]{2,1,0:T(8,128)(2,1)S(1)}, u32[]{:S(2)}, u32[]{:S(2)}) collective-permute-start(bf16[16,32,896]{2,1,0:T(8,128)(2,1)S(1)} %all_to_all.11.mine_ref), channel_id=1, source_target_pairs={{0,16},{16,0},{1,17},{17,1},{2,18},{18,2},{3,19},{19,3},{4,20},{20... | collective-permute-start | bytes 2752520 | tf_op jit(solution)/shard_map/ppermute | solution.py:212
